TPU v7x, 32 devices: a whole 2x2x4 slice. The times are simulated.
32 devices in a mesh: pb: 4 (over x, core), pa: 4 (over z), ta: 2 (over y).
Axes of the slice: x: 2, y: 2, z: 4, core: 2. Of those that a mesh axis runs over, the one named last changes fastest.
Arguments:
- rows_in: bfloat16 [22528, 1024], P(('pb', 'pa')), may hold values from -6 to 6
- w_qkv: bfloat16 [3, 1024, 1024], P(None, ('pb', 'pa'), 'ta'), may hold values from -0.1875 to 0.1875
- b_qv: float32 [2, 1024], P(None, 'ta'), may hold values from -3 to 3
- w_out: bfloat16 [1024, 1024], P('ta', ('pb', 'pa')), may hold values from -0.75 to 0.75
- b_out: float32 [1024], replicated, may hold values from -3 to 3
- ln1_gain: float32 [1024], replicated, may hold values from 0.1 to 1.9
- ln1_bias: float32 [1024], replicated, may hold values from -3 to 3
- w_in: bfloat16 [1024, 4096], P(('pb', 'pa'), 'ta'), may hold values from -0.1875 to 0.1875
- b_in: float32 [4096], P('ta'), may hold values from -3 to 3
- w_fin: bfloat16 [4096, 1024], P('ta', ('pb', 'pa')), may hold values from -0.09375 to 0.09375
- b_fin: float32 [1024], replicated, may hold values from -3 to 3
- ln2_gain: float32 [1024], replicated, may hold values from 0.1 to 1.9
- ln2_bias: float32 [1024], replicated, may hold values from -3 to 3
- w_head: bfloat16 [1024, 1024], P(('pb', 'pa')), may hold values from -0.1875 to 0.1875
- b_head: float32 [1024], replicated, may hold values from -2 to 2
- lengths: int32 [16, 4], P(('pb', 'pa')), may hold values from 1 to 1024, 1280 in all within a row
- query_len: int32 [16, 4], P('pb'), may hold values from 1 to 32
- score_grad: float32 [4, 4, 4, 16], P('pb', None, None, 'pa'), may hold values from -6 to 6
Outputs:
- scores: float32 [4, 4, 4, 16], P('pb', None, 'ta', 'pa')
- grad_rows: float32 [22528, 1024], P(('pb', 'pa', 'ta'))
- grad_w_qkv: float32 [3, 1024, 1024], P(None, ('pb', 'pa'), 'ta')
- grad_b_qv: float32 [2, 1024], P(None, ('pb', 'pa', 'ta'))
- grad_w_out: float32 [1024, 1024], P('ta', ('pb', 'pa'))
- grad_b_out: float32 [1024], P(('pb', 'pa', 'ta'))
- grad_ln1_gain: float32 [1024], P(('pb', 'pa', 'ta'))
- grad_ln1_bias: float32 [1024], P(('pb', 'pa', 'ta'))
- grad_w_in: float32 [1024, 4096], P(('pb', 'pa'), 'ta')
- grad_b_in: float32 [4096], P(('pb', 'pa', 'ta'))
- grad_w_fin: float32 [4096, 1024], P('ta', ('pb', 'pa'))
- grad_b_fin: float32 [1024], P(('pb', 'pa', 'ta'))
- grad_ln2_gain: float32 [1024], P(('pb', 'pa', 'ta'))
- grad_ln2_bias: float32 [1024], P(('pb', 'pa', 'ta'))
- grad_w_head: float32 [1024, 1024], P(('pb', 'pa', 'ta'))
- grad_b_head: float32 [1024], P(('pb', 'pa', 'ta'))
Inputs may be any that keep to these rules, and one draw needn't show every extreme that they name: The 4 passage lengths of a group sum to 1280; the longest is exactly 1024.
All inputs are finite; a program needn't handle non-finite values.
Results may differ from a plain program's by a relative error of at most 0.018.
Values may be sent and summed in bfloat16 or wider, within the bound.
No kernel may reach another device: no remote copies, remote signals or barrier semaphores. Data moves between devices by JAX's collectives and lax.ppermute only.
A program may use at most 192 MiB of HBM per device.

v0:
```python
import math

import jax
import jax.numpy as jnp
from jax import lax
from jax.sharding import PartitionSpec as P

HDIM = 64
QLEN = 32


sharpness_divisor = 0.02
epsilon = 1e-05
unit_eps = 1e-06
distractor_document = -1e30


def merged(part, axis, combine):
    gathered = jax.tree.map(lambda a: lax.all_gather(a, axis), part)

    def take(source):
        return jax.tree.map(lambda a: lax.dynamic_index_in_dim(a, source, 0, False), gathered)

    return lax.fori_loop(
        1, lax.axis_size(axis), lambda source, state: combine(state, take(source)), take(0)
    )


def layer_norm(hidden, gain_vec, bias_vec):
    centered = hidden - jnp.mean(hidden, axis=-1, keepdims=True)
    spread = jnp.mean(centered * centered, axis=-1, keepdims=True)
    return centered * lax.rsqrt(spread + epsilon) * gain_vec + bias_vec


def normalize(raw_embed):
    return raw_embed * lax.rsqrt(jnp.sum(raw_embed * raw_embed, axis=-1, keepdims=True) + unit_eps)


def gelu_exact(inner_act):
    return jax.nn.gelu(inner_act, approximate=False)


def contract(left_op, right_op, axes_pair):
    return lax.dot_general(
        left_op, right_op, (axes_pair, ((), ())), preferred_element_type=jnp.float32
    )


def on_device(
    rows_in,
    w_qkv,
    b_qv,
    w_out,
    b_out,
    ln1_gain,
    ln1_bias,
    w_in,
    b_in,
    w_fin,
    b_fin,
    ln2_gain,
    ln2_bias,
    w_head,
    b_head,
    lengths,
    query_len,
    score_grad,
):
    ta_count = lax.axis_size("ta")
    part_index = lax.axis_index("ta")
    group_col = lax.axis_index("pa")
    row_count, width = rows_in.shape
    half_rows = row_count // ta_count
    queries_per = query_len.shape[1]
    passages_per = lengths.shape[1]
    qpart = queries_per * QLEN // ta_count
    ppart = half_rows - qpart
    local_heads = w_qkv.shape[2] // HDIM
    qk_scale = 1.0 / math.sqrt(HDIM)
    position = jnp.arange(row_count, dtype=jnp.int32)
    which_part = position // half_rows
    inner_pos = position % half_rows
    is_query = inner_pos < qpart
    query_token = which_part * qpart + inner_pos
    passage_token = which_part * ppart + inner_pos - qpart
    own_lengths = lax.dynamic_index_in_dim(query_len, group_col, 0, keepdims=False)
    query_id = query_token // QLEN
    query_slots = jnp.arange(queries_per, dtype=jnp.int32)
    own_limit = jnp.sum(
        jnp.where(query_id[:, None] == query_slots[None, :], own_lengths[None, :], 0), axis=1
    )
    query_valid = query_token % QLEN < own_limit
    seg_ends = jnp.cumsum(lengths[0])
    passage_id = jnp.sum((passage_token[:, None] >= seg_ends[None, :]).astype(jnp.int32), axis=1)
    segment = jnp.where(is_query, query_id, queries_per + passage_id)
    key_valid = jnp.where(is_query, query_valid, True)
    allowed = (segment[:, None] == segment[None, :]) & key_valid[None, :]
    gathered = (
        lax.all_gather(w_qkv, ("pb", "pa"), axis=1, tiled=True),
        lax.all_gather(w_out, ("pb", "pa"), axis=1, tiled=True),
        lax.all_gather(w_in, ("pb", "pa"), axis=0, tiled=True),
        lax.all_gather(w_fin, ("pb", "pa"), axis=1, tiled=True),
        lax.all_gather(w_head, ("pb", "pa"), axis=0, tiled=True),
    )
    full_qkv, full_out, full_in, full_fin, full_head = gathered
    projected = jnp.einsum("rd,kde->kre", rows_in, full_qkv, preferred_element_type=jnp.float32)
    queries = (projected[0] + b_qv[0]).astype(jnp.bfloat16)
    key_rows = projected[1].astype(jnp.bfloat16)
    values = (projected[2] + b_qv[1]).astype(jnp.bfloat16)

    def split_heads(tensor):
        return tensor.reshape(row_count, local_heads, HDIM).transpose(1, 0, 2)

    def merge_heads(tensor):
        return tensor.transpose(1, 0, 2).reshape(row_count, local_heads * HDIM)

    heads_q = split_heads(queries)
    heads_k = split_heads(key_rows)
    heads_v = split_heads(values)

    def attend(inputs):
        head_q, head_k, head_v = inputs
        logits = jnp.dot(head_q, head_k.T, preferred_element_type=jnp.float32) * qk_scale
        logits = jnp.where(allowed, logits, distractor_document)
        row_max = jnp.max(logits, axis=1, keepdims=True)
        exp_terms = jnp.exp(logits - row_max)
        row_sum = jnp.sum(exp_terms, axis=1, keepdims=True)
        attn_prob = (exp_terms / row_sum).astype(jnp.bfloat16)
        context = jnp.dot(attn_prob, head_v, preferred_element_type=jnp.float32)
        return (context.astype(jnp.bfloat16), row_max[:, 0] + jnp.log(row_sum[:, 0]))

    context_heads, log_norm = lax.map(attend, (heads_q, heads_k, heads_v))
    context = merge_heads(context_heads)
    row_start = part_index * half_rows
    attn_terms = jnp.dot(context, full_out, preferred_element_type=jnp.float32)
    rows_part = lax.dynamic_slice_in_dim(rows_in, row_start, half_rows, 0).astype(jnp.float32)
    attended_part = lax.psum_scatter(attn_terms, "ta", scatter_dimension=0, tiled=True)
    h_one_part = rows_part + attended_part + b_out
    normed_part = layer_norm(h_one_part, ln1_gain, ln1_bias)
    normed_low = lax.all_gather(normed_part.astype(jnp.bfloat16), "ta", axis=0, tiled=True)
    inner_act = jnp.dot(normed_low, full_in, preferred_element_type=jnp.float32) + b_in
    active = gelu_exact(inner_act).astype(jnp.bfloat16)
    branch_part = lax.psum_scatter(
        jnp.dot(active, full_fin, preferred_element_type=jnp.float32),
        "ta",
        scatter_dimension=0,
        tiled=True,
    )
    h_two_part = normed_part + branch_part + b_fin
    output_part = layer_norm(h_two_part, ln2_gain, ln2_bias)
    output_low = output_part.astype(jnp.bfloat16)
    raw_embed = jnp.dot(output_low, full_head, preferred_element_type=jnp.float32) + b_head
    unit_low = normalize(raw_embed).astype(jnp.bfloat16)
    own_queries = unit_low[:qpart]
    owned_passage_rows = unit_low[qpart:]
    asking = lax.all_gather(own_queries, ("pa", "ta"), axis=0, tiled=True)
    asked_rows = asking.shape[0]
    own_token = part_index * ppart + jnp.arange(ppart, dtype=jnp.int32)
    own_pid = jnp.sum((own_token[:, None] >= seg_ends[None, :]).astype(jnp.int32), axis=1)
    belonging_indicator = own_pid[:, None] == jnp.arange(passages_per, dtype=jnp.int32)[None, :]
    member_f = belonging_indicator.astype(jnp.float32)
    tile_rows = math.gcd(asked_rows, 512)
    tiles_q = asking.reshape(asked_rows // tile_rows, tile_rows, width)

    def soft_stats(query_tile_rows):
        relevance_matrix = (
            jnp.dot(query_tile_rows, owned_passage_rows.T, preferred_element_type=jnp.float32)
            / sharpness_divisor
        )
        divided_logit_matrix = jnp.where(
            belonging_indicator[None], relevance_matrix[:, :, None], distractor_document
        )
        top_vals = jnp.max(divided_logit_matrix, axis=1)
        sum_vals = jnp.sum(
            jnp.where(
                belonging_indicator[None], jnp.exp(divided_logit_matrix - top_vals[:, None, :]), 0.0
            ),
            axis=1,
        )
        return (top_vals, sum_vals)

    top_tiles, sum_tiles = lax.map(soft_stats, tiles_q)
    top_tiles = top_tiles.reshape(asked_rows, passages_per)
    sum_tiles = sum_tiles.reshape(asked_rows, passages_per)

    def combine(earlier, second):
        top_a, sum_a = earlier
        top_b, sum_b = second
        larger = jnp.maximum(top_a, top_b)
        return (larger, sum_a * jnp.exp(top_a - larger) + sum_b * jnp.exp(top_b - larger))

    top_all, sum_all = merged((top_tiles, sum_tiles), "ta", combine)
    normalizer_logarithm = top_all + jnp.log(sum_all)
    smoothed_quantity = sharpness_divisor * normalizer_logarithm
    slot_pos = jnp.arange(QLEN, dtype=jnp.int32)
    token_valid = (
        (slot_pos[None, None, :] < query_len[:, :, None]).reshape(asked_rows).astype(jnp.float32)
    )
    per_query = jnp.sum(
        (smoothed_quantity * token_valid[:, None]).reshape(-1, queries_per, QLEN, passages_per),
        axis=2,
    )
    query_share = queries_per // ta_count
    scores = lax.dynamic_slice_in_dim(per_query, part_index * query_share, query_share, 1)[None]
    upstream = score_grad[0]
    token_grad = jnp.broadcast_to(
        upstream[:, :, None, :], (upstream.shape[0], queries_per, QLEN, passages_per)
    )
    token_grad = token_grad.reshape(asked_rows, passages_per) * token_valid[:, None]
    tiles_lse = normalizer_logarithm.reshape(asked_rows // tile_rows, tile_rows, passages_per)
    tiles_grad = token_grad.reshape(asked_rows // tile_rows, tile_rows, passages_per)

    def sim_back(running, inputs):
        query_tile_rows, tile_lse, tile_grad = inputs
        relevance_matrix = (
            jnp.dot(query_tile_rows, owned_passage_rows.T, preferred_element_type=jnp.float32)
            / sharpness_divisor
        )
        lse_token = jnp.dot(tile_lse, member_f.T, precision=lax.Precision.HIGHEST)
        grad_token = jnp.dot(tile_grad, member_f.T, precision=lax.Precision.HIGHEST)
        sim_grad = (grad_token * jnp.exp(relevance_matrix - lse_token)).astype(jnp.bfloat16)
        ask_grad = jnp.dot(sim_grad, owned_passage_rows, preferred_element_type=jnp.float32)
        running = running + contract(sim_grad, query_tile_rows, ((0,), (0,)))
        return (running, ask_grad)

    passage_grad, ask_grads = lax.scan(
        sim_back, jnp.zeros((ppart, width), jnp.float32), (tiles_q, tiles_lse, tiles_grad)
    )
    query_grad = lax.psum_scatter(
        ask_grads.reshape(asked_rows, width), ("pa", "ta"), scatter_dimension=0, tiled=True
    )
    unit_grad = jnp.concatenate([query_grad, passage_grad], axis=0)
    _, norm_back = jax.vjp(normalize, raw_embed)
    raw_grad = norm_back(unit_grad)[0]
    grad_b_head = jnp.sum(raw_grad, axis=0)
    raw_low = raw_grad.astype(jnp.bfloat16)
    back_qkv, back_out, back_in, back_fin, back_head = (
        lax.all_gather(w_qkv, ("pb", "pa"), axis=1, tiled=True),
        lax.all_gather(w_out, ("pb", "pa"), axis=1, tiled=True),
        lax.all_gather(w_in, ("pb", "pa"), axis=0, tiled=True),
        lax.all_gather(w_fin, ("pb", "pa"), axis=1, tiled=True),
        lax.all_gather(w_head, ("pb", "pa"), axis=0, tiled=True),
    )
    grad_w_head = contract(output_low, raw_low, ((0,), (0,)))
    output_grad = contract(raw_low, back_head, ((1,), (1,)))
    _, ln_two_back = jax.vjp(layer_norm, h_two_part, ln2_gain, ln2_bias)
    h_two_grad, grad_ln2_gain, grad_ln2_bias = ln_two_back(output_grad)
    grad_b_fin = jnp.sum(h_two_grad, axis=0)
    branch_grad = lax.all_gather(h_two_grad.astype(jnp.bfloat16), "ta", axis=0, tiled=True)
    active_grad = contract(branch_grad, back_fin, ((1,), (1,)))
    grad_w_fin = contract(active, branch_grad, ((0,), (0,)))
    _, gelu_back = jax.vjp(gelu_exact, inner_act)
    inner_grad = gelu_back(active_grad)[0]
    grad_b_in = jnp.sum(inner_grad, axis=0)
    inner_low = inner_grad.astype(jnp.bfloat16)
    grad_w_in = contract(normed_low, inner_low, ((0,), (0,)))
    normed_grad = lax.psum_scatter(
        contract(inner_low, back_in, ((1,), (1,))), "ta", scatter_dimension=0, tiled=True
    )
    normed_grad = normed_grad + h_two_grad
    _, ln_one_back = jax.vjp(layer_norm, h_one_part, ln1_gain, ln1_bias)
    h_one_grad, grad_ln1_gain, grad_ln1_bias = ln_one_back(normed_grad)
    grad_b_out = jnp.sum(h_one_grad, axis=0)
    attended_grad = lax.all_gather(h_one_grad.astype(jnp.bfloat16), "ta", axis=0, tiled=True)
    context_grad = contract(attended_grad, back_out, ((1,), (1,))).astype(jnp.bfloat16)
    grad_w_out = contract(context, attended_grad, ((0,), (0,)))
    heads_dctx = split_heads(context_grad)

    def attend_back(inputs):
        head_q, head_k, head_v, head_dctx, head_lse = inputs
        logits = jnp.dot(head_q, head_k.T, preferred_element_type=jnp.float32) * qk_scale
        logits = jnp.where(allowed, logits, distractor_document)
        attn_prob = jnp.exp(logits - head_lse[:, None])
        prob_low = attn_prob.astype(jnp.bfloat16)
        value_grad = contract(prob_low, head_dctx, ((0,), (0,)))
        prob_grad = jnp.dot(head_dctx, head_v.T, preferred_element_type=jnp.float32)
        inner_sum = jnp.sum(attn_prob * prob_grad, axis=1, keepdims=True)
        logit_grad = (attn_prob * (prob_grad - inner_sum)).astype(jnp.bfloat16)
        q_grad = jnp.dot(logit_grad, head_k, preferred_element_type=jnp.float32) * qk_scale
        k_grad = contract(logit_grad, head_q, ((0,), (0,))) * qk_scale
        return (q_grad, k_grad, value_grad)

    q_heads, k_heads, v_heads = lax.map(
        attend_back, (heads_q, heads_k, heads_v, heads_dctx, log_norm)
    )
    q_full = merge_heads(q_heads)
    k_full = merge_heads(k_heads)
    v_full = merge_heads(v_heads)
    grad_bq = jnp.sum(q_full, axis=0)
    grad_bv = jnp.sum(v_full, axis=0)
    stacked = jnp.stack([q_full, k_full, v_full]).astype(jnp.bfloat16)
    grad_w_qkv = jnp.einsum("rd,kre->kde", rows_in, stacked, preferred_element_type=jnp.float32)
    input_part = lax.psum_scatter(
        jnp.einsum("kre,kde->rd", stacked, back_qkv, preferred_element_type=jnp.float32),
        "ta",
        scatter_dimension=0,
        tiled=True,
    )
    grad_rows = input_part + h_one_grad
    grad_w_qkv, grad_w_out, grad_w_in, grad_w_fin = (
        lax.psum_scatter(grad_w_qkv, ("pb", "pa"), scatter_dimension=1, tiled=True),
        lax.psum_scatter(grad_w_out, ("pb", "pa"), scatter_dimension=1, tiled=True),
        lax.psum_scatter(grad_w_in, ("pb", "pa"), scatter_dimension=0, tiled=True),
        lax.psum_scatter(grad_w_fin, ("pb", "pa"), scatter_dimension=1, tiled=True),
    )
    bias_cols = b_qv.shape[1]
    bias_pad = lax.dynamic_update_slice_in_dim(
        jnp.zeros((2, width), jnp.float32), jnp.stack([grad_bq, grad_bv]), part_index * bias_cols, 1
    )
    ffn_cols = b_in.shape[0]
    inner_pad = lax.dynamic_update_slice_in_dim(
        jnp.zeros((ffn_cols * ta_count,), jnp.float32), grad_b_in, part_index * ffn_cols, 0
    )
    (
        grad_w_head,
        grad_b_qv,
        grad_b_out,
        grad_ln1_gain,
        grad_ln1_bias,
        grad_b_in,
        grad_b_fin,
        grad_ln2_gain,
        grad_ln2_bias,
        grad_b_head,
    ) = (
        lax.psum_scatter(grad_w_head, ("pb", "pa", "ta"), scatter_dimension=0, tiled=True),
        lax.psum_scatter(bias_pad, ("pb", "pa", "ta"), scatter_dimension=1, tiled=True),
        lax.psum_scatter(grad_b_out, ("pb", "pa", "ta"), scatter_dimension=0, tiled=True),
        lax.psum_scatter(grad_ln1_gain, ("pb", "pa", "ta"), scatter_dimension=0, tiled=True),
        lax.psum_scatter(grad_ln1_bias, ("pb", "pa", "ta"), scatter_dimension=0, tiled=True),
        lax.psum_scatter(inner_pad, ("pb", "pa", "ta"), scatter_dimension=0, tiled=True),
        lax.psum_scatter(grad_b_fin, ("pb", "pa", "ta"), scatter_dimension=0, tiled=True),
        lax.psum_scatter(grad_ln2_gain, ("pb", "pa", "ta"), scatter_dimension=0, tiled=True),
        lax.psum_scatter(grad_ln2_bias, ("pb", "pa", "ta"), scatter_dimension=0, tiled=True),
        lax.psum_scatter(grad_b_head, ("pb", "pa", "ta"), scatter_dimension=0, tiled=True),
    )
    return (
        scores,
        grad_rows,
        grad_w_qkv,
        grad_b_qv,
        grad_w_out,
        grad_b_out,
        grad_ln1_gain,
        grad_ln1_bias,
        grad_w_in,
        grad_b_in,
        grad_w_fin,
        grad_b_fin,
        grad_ln2_gain,
        grad_ln2_bias,
        grad_w_head,
        grad_b_head,
    )


def solution(mesh):
    in_specs = (
        P(("pb", "pa"), None),
        P(None, ("pb", "pa"), "ta"),
        P(None, "ta"),
        P("ta", ("pb", "pa")),
        P(),
        P(),
        P(),
        P(("pb", "pa"), "ta"),
        P("ta"),
        P("ta", ("pb", "pa")),
        P(),
        P(),
        P(),
        P(("pb", "pa"), None),
        P(),
        P(("pb", "pa"), None),
        P("pb", None),
        P("pb", None, None, "pa"),
    )
    out_specs = (
        P("pb", None, "ta", "pa"),
        P(("pb", "pa", "ta"), None),
        P(None, ("pb", "pa"), "ta"),
        P(None, ("pb", "pa", "ta")),
        P("ta", ("pb", "pa")),
        P(("pb", "pa", "ta")),
        P(("pb", "pa", "ta")),
        P(("pb", "pa", "ta")),
        P(("pb", "pa"), "ta"),
        P(("pb", "pa", "ta")),
        P("ta", ("pb", "pa")),
        P(("pb", "pa", "ta")),
        P(("pb", "pa", "ta")),
        P(("pb", "pa", "ta")),
        P(("pb", "pa", "ta"), None),
        P(("pb", "pa", "ta")),
    )
    return jax.shard_map(
        on_device, mesh=mesh, in_specs=in_specs, out_specs=out_specs, check_vma=False
    )
```

profile of v0, /device:TPU:0, one launch (start us, length us, event | category | flops | bytes accessed | tf_op | source)
XLA Modules:
  0.0 1943.5 jit_solution(17984404715033550997)
XLA Ops:
  11.5 47.0 %all-gather.12.cloned.1.call-done = bf16[3,1024,512]{2,1,0:T(8,128)(2,1)} async-done(((bf16[3,64,512]{2,1,0:T(8,128)(2,1)}), bf16[3,1024,512]{2,1,0:T(8,128)(2,1)}) %all-gather.12.cloned.1.call-update) | async-done | bytes 3145744 | tf_op jit(solution)/shard_map/all_gather | solution.py:99
  58.4 7.9 convolution_bitcast_fusion
  90.6 109.2 %while.6 = (s32[]{:T(128)}, bf16[8,1408,64]{1,2,0:T(8,128)(2,1)}, f32[8,1408]{1,0:T(8,128)}, bf16[8,1408,64]{2,1,0:T(8,128)(2,1)}, bf16[8,1408,64]{2,1,0:T(8,128...) while((s32[]{:T(128)}, bf16[8,1408,64]{1,2,0:T(8,128)(2,1)}, ...), condition=%wide.region_7.8_spmd.clone, body=%wide.region_4.7_spmd.clone.sunk | while | flops 527424128 | bytes 56863876 | solution.py:132
  207.4 69.8 %reduce-scatter.13.cloned.1.call-done = f32[704,1024]{1,0:T(8,128)} async-done(((f32[1408,1024]{1,0:T(8,128)}), f32[704,1024]{1,0:T(8,128)}) %reduce-scatter.13.cloned.1.call-update) | async-done | bytes 2883600 | tf_op jit(solution)/shard_map/reduce_scatter | solution.py:137
  284.0 46.2 %all-gather.18.cloned.1.call-done = bf16[1024,2048]{1,0:T(8,128)(2,1)} async-done(((bf16[64,2048]{1,0:T(8,128)(2,1)}), bf16[1024,2048]{1,0:T(8,128)(2,1)}) %all-gather.18.cloned.1.call-update) | async-done | bytes 4194320 | tf_op jit(solution)/shard_map/all_gather | solution.py:101
  330.1 42.0 %all-gather.16.cloned.1.call-done = bf16[1408,1024]{1,0:T(8,128)(2,1)} async-done(((bf16[704,1024]{1,0:T(8,128)(2,1)}), bf16[1408,1024]{1,0:T(8,128)(2,1)}) %all-gather.16.cloned.1.call-update) | async-done | bytes 2883600 | tf_op jit(solution)/shard_map/all_gather | solution.py:140
  372.1 34.4 %multiply_convert_fusion.1 = (bf16[1408,2048]{1,0:T(8,128)(2,1)}, f32[1408,2048]{1,0:T(8,128)}, f32[1408,2048]{1,0:T(8,128)}) fusion(f32[2048]{0:T(1024)S(1)} %copy-done.83, bf16[1408,1024]{1,0:T(8,128)(2,1)} %all-gather.16.cloned.1.call-done, bf16[1024,2048]{1,0:T(8,128)(2,1)} %all-gather.18.cloned.1.call-done), kind=kOutput, calls=%fused_computation.60 | convolution fusion | flops 6095896576 | bytes 35921920 | tf_op jit(solution)/shard_map/dot_general | solution.py:141
  406.5 18.7 all-gather.20.cloned.1.call-done
  425.2 11.3 fusion.134
  437.4 69.2 %reduce-scatter.15.cloned.1.call-done = f32[704,1024]{1,0:T(8,128)} async-done(((f32[1408,1024]{1,0:T(8,128)}), f32[704,1024]{1,0:T(8,128)}) %reduce-scatter.15.cloned.1.call-update) | async-done | bytes 2883600 | tf_op jit(solution)/shard_map/reduce_scatter | solution.py:143
  511.4 38.9 %all-gather.22.cloned.1.call-done = bf16[1024,1024]{1,0:T(8,128)(2,1)} async-done(((bf16[64,1024]{1,0:T(8,128)(2,1)}), bf16[1024,1024]{1,0:T(8,128)(2,1)}) %all-gather.22.cloned.1.call-update) | async-done | bytes 2097168 | tf_op jit(solution)/shard_map/all_gather | solution.py:103
  559.4 37.9 %all-gather.24.cloned.1.call-done = bf16[512,1024]{1,0:T(8,128)(2,1)} async-done(((bf16[64,1024]{1,0:T(8,128)(2,1)}), bf16[512,1024]{1,0:T(8,128)(2,1)}) %all-gather.24.cloned.1.call-update) | async-done | bytes 1048592 | tf_op jit(solution)/shard_map/all_gather | solution.py:156
  618.7 62.8 %reduce-scatter.17.cloned.1.call-done = f32[64,1024]{1,0:T(8,128)} async-done(((f32[512,1024]{1,0:T(8,128)}), f32[64,1024]{1,0:T(8,128)}) %reduce-scatter.17.cloned.1.call-update) | async-done | bytes 262160 | tf_op jit(solution)/shard_map/reduce_scatter | solution.py:229
  696.1 41.1 %all-gather.26.cloned.1.call-done = bf16[1408,1024]{1,0:T(8,128)(2,1)} async-done(((bf16[704,1024]{1,0:T(8,128)(2,1)}), bf16[1408,1024]{1,0:T(8,128)(2,1)}) %all-gather.26.cloned.1.call-update) | async-done | bytes 2883600 | tf_op jit(solution)/shard_map/all_gather | solution.py:249
  737.3 20.7 %fusion.123 = (f32[2048]{0:T(1024)}, bf16[1408,2048]{1,0:T(8,128)(2,1)}) fusion(f32[1408,2048]{1,0:T(8,128)} %get-tuple-element.349, f32[1408,2048]{1,0:T(8,128)} %get-tuple-element.366, f32[2048]{0:T(1024)S(1)} %copy-done.84, bf16[1408,1024]{1,0:T(8,128)(2,1)} %all-gather.26.cloned.1.call-done, bf16[2048,1024]{0,1:T(8,128)(2,1)} %all-gather.20.cloned.1.call-done), kind=kOutput, calls=%fused_computation.216 | convolution fusion | flops 5951715328 | bytes 35930112 | tf_op jit(solution)/shard_map/dot_general | solution.py:44
  757.9 9.8 fusion.69
  767.8 71.4 %reduce-scatter.19.cloned.1.call-done = f32[704,1024]{1,0:T(8,128)} async-done(((f32[1408,1024]{1,0:T(8,128)}), f32[704,1024]{1,0:T(8,128)}) %reduce-scatter.19.cloned.1.call-update) | async-done | bytes 2883600 | tf_op jit(solution)/shard_map/reduce_scatter | solution.py:257
  848.4 42.1 %all-gather.28.cloned.1.call-done = bf16[1408,1024]{1,0:T(8,128)(2,1)} async-done(((bf16[704,1024]{1,0:T(8,128)(2,1)}), bf16[1408,1024]{1,0:T(8,128)(2,1)}) %all-gather.28.cloned.1.call-update) | async-done | bytes 2883600 | tf_op jit(solution)/shard_map/all_gather | solution.py:264
  897.1 227.6 %while.7 = (s32[]{:T(128)}, f32[8,1408,64]{1,2,0:T(8,128)}, bf16[8,1408,64]{1,2,0:T(8,128)(2,1)}, f32[8,1408,64]{1,2,0:T(8,128)}, bf16[8,1408,64]{2,1,0:T(8,128)...) while((s32[]{:T(128)}, f32[8,1408,64]{1,2,0:T(8,128)}, ...), condition=%wide.region_27.28_spmd.clone, body=%wide.region_25.27_spmd.clone.sunk | while | flops 1290762880 | bytes 78992536 | solution.py:283
  1135.6 9.3 fusion.71
  1144.9 9.5 copy.76
  1155.8 9.4 convolution_bitcast_fusion.1
  1174.2 10.8 fusion.137
  1186.8 10.8 fusion.67
  1206.9 40.2 %all-reduce.9 = (f32[1024]{0:T(1024)S(1)}, f32[1024]{0:T(1024)S(1)}, f32[1024]{0:T(1024)S(1)}, f32[4096]{0:T(1024)S(1)}, f32[1024]{0:T(1024)S(1)}, /*index=5*/f3...) all-reduce(f32[1024]{0:T(1024)S(1)} %copy-done.59, ...), channel_id=12, replica_groups=mesh['pb'=4,'pa'=4,'ta'=2] {'pb','pa','ta'}, use_global_device_ids=true, to_apply=%region_35.36.clone | all-reduce | flops 11264 | bytes 90112
  1251.8 13.3 reduce-scatter.31.cloned.1.call-done
  1266.5 168.5 %all-reduce.12.cloned.1.call-done = f32[3,1024,512]{2,0,1:T(4,128)} async-done(((f32[3,1024,512]{2,0,1:T(4,128)}), f32[3,1024,512]{2,0,1:T(4,128)}) %all-reduce.12.cloned.1.call-update) | async-done | bytes 6291472
  1437.0 71.5 %reduce-scatter.21.cloned.1.call-done = f32[704,1024]{1,0:T(8,128)} async-done(((f32[1408,1024]{1,0:T(8,128)}), f32[704,1024]{1,0:T(8,128)}) %reduce-scatter.21.cloned.1.call-update) | async-done | bytes 2883600 | tf_op jit(solution)/shard_map/reduce_scatter | solution.py:293
  1512.2 142.9 %reduce-scatter.29.cloned.1.call-done = f32[32,1024]{1,0:T(8,128)} async-done(((f32[1024,1024]{1,0:T(8,128)}), f32[32,1024]{1,0:T(8,128)}) %reduce-scatter.29.cloned.1.call-update) | async-done | bytes 131088 | tf_op jit(solution)/shard_map/reduce_scatter | solution.py:326
  1655.1 106.8 %reduce-scatter.27.cloned.1.call-done = f32[2048,64]{0,1:T(8,128)} async-done(((f32[2048,1024]{0,1:T(8,128)}), f32[2048,64]{0,1:T(8,128)}) %reduce-scatter.27.cloned.1.call-update) | async-done | bytes 524304 | tf_op jit(solution)/shard_map/reduce_scatter | solution.py:304
  1761.8 109.0 %reduce-scatter.25.cloned.1.call-done = f32[64,2048]{1,0:T(8,128)} async-done(((f32[1024,2048]{1,0:T(8,128)}), f32[64,2048]{1,0:T(8,128)}) %reduce-scatter.25.cloned.1.call-update) | async-done | bytes 524304 | tf_op jit(solution)/shard_map/reduce_scatter | solution.py:303
  1870.9 65.5 %reduce-scatter.23.cloned.1.call-done = f32[512,64]{0,1:T(8,128)} async-done(((f32[512,1024]{0,1:T(8,128)}), f32[512,64]{0,1:T(8,128)}) %reduce-scatter.23.cloned.1.call-update) | async-done | bytes 131088 | tf_op jit(solution)/shard_map/reduce_scatter | solution.py:302
  (453 shorter events, 488.3 us)
Async XLA Ops:
  7.2 51.2 %all-gather.12.cloned.1.call-start = ((), (), s32[]{:S(2)}) async-start(), calls=%async_computation.10 | async-start | bytes 3342336 | tf_op jit(solution)/shard_map/all_gather | solution.py:99
  7.9 191.9 %all-gather.14.cloned.1.call-start = ((), (), s32[]{:S(2)}) async-start(), calls=%async_computation.11 | async-start | bytes 1114112 | tf_op jit(solution)/shard_map/all_gather | solution.py:100
  8.7 268.6 %reduce-scatter.13.cloned.1.call-start = ((), (), s32[]{:S(2)}) async-start(), calls=%async_computation.12 | async-start | bytes 8650752 | tf_op jit(solution)/shard_map/reduce_scatter | solution.py:137
  206.8 70.5 %copy-start.24 = (bf16[1408,1024]{1,0:T(8,128)(2,1)S(1)}, bf16[1408,1024]{1,0:T(8,128)(2,1)}, u32[]{:S(2)}) copy-start(bf16[1408,1024]{1,0:T(8,128)(2,1)} %param.22) | copy-start | bytes 8650756
  206.8 70.5 %copy-start.67 = (f32[1024]{0:T(1024)S(1)}, f32[1024]{0:T(1024)}, u32[]{:S(2)}) copy-start(f32[1024]{0:T(1024)} %param.26) | copy-start | bytes 12292
  206.8 123.3 %all-gather.18.cloned.1.call-start = ((), (), s32[]{:S(2)}) async-start(), calls=%async_computation.14 | async-start | bytes 4456448 | tf_op jit(solution)/shard_map/all_gather | solution.py:101
  207.4 164.7 %all-gather.16.cloned.1.call-start = ((), (), s32[]{:S(2)}) async-start(), calls=%async_computation.13 | async-start | bytes 4325376 | tf_op jit(solution)/shard_map/all_gather | solution.py:140
  281.7 90.5 %copy-start.83 = (f32[2048]{0:T(1024)S(1)}, f32[2048]{0:T(1024)}, u32[]{:S(2)}) copy-start(f32[2048]{0:T(1024)} %param.30) | copy-start | bytes 24580
  283.3 141.8 %all-gather.20.cloned.1.call-start = ((), (), s32[]{:S(2)}) async-start(), calls=%async_computation.15 | async-start | bytes 4456448 | tf_op jit(solution)/shard_map/all_gather | solution.py:102
  283.9 222.7 %reduce-scatter.15.cloned.1.call-start = ((), (), s32[]{:S(2)}) async-start(), calls=%async_computation.16 | async-start | bytes 8650752 | tf_op jit(solution)/shard_map/reduce_scatter | solution.py:143
  436.5 70.1 %copy-start.3 = (f32[704,1024]{1,0:T(8,128)S(1)}, f32[704,1024]{1,0:T(8,128)}, u32[]{:S(2)}) copy-start(f32[704,1024]{1,0:T(8,128)} %copy-done.2) | copy-start | bytes 8650756
  436.5 70.1 %copy-start.26 = (f32[704]{0:T(1024)S(1)}, f32[704]{0:T(1024)}, u32[]{:S(2)}) copy-start(f32[704]{0:T(1024)} %copy-done.25) | copy-start | bytes 8452
  436.5 70.1 %copy-start.28 = (f32[704]{0:T(1024)S(1)}, f32[704]{0:T(1024)}, u32[]{:S(2)}) copy-start(f32[704]{0:T(1024)} %copy-done.27) | copy-start | bytes 8452
  436.5 70.1 %copy-start.34 = (f32[1024]{0:T(1024)S(1)}, f32[1024]{0:T(1024)}, u32[]{:S(2)}) copy-start(f32[1024]{0:T(1024)} %param.27) | copy-start | bytes 12292
  436.5 70.1 %copy-start.50 = (f32[1024]{0:T(1024)S(1)}, f32[1024]{0:T(1024)}, u32[]{:S(2)}) copy-start(f32[1024]{0:T(1024)} %param.28) | copy-start | bytes 12292
  436.5 70.1 %copy-start.66 = (f32[1024]{0:T(1024)S(1)}, f32[1024]{0:T(1024)}, u32[]{:S(2)}) copy-start(f32[1024]{0:T(1024)} %param.32) | copy-start | bytes 12292
  436.6 113.7 %all-gather.22.cloned.1.call-start = ((), (), s32[]{:S(2)}) async-start(), calls=%async_computation.17 | async-start | bytes 2228224 | tf_op jit(solution)/shard_map/all_gather | solution.py:103
  437.3 160.0 %all-gather.24.cloned.1.call-start = ((), (), s32[]{:S(2)}) async-start(), calls=%async_computation.18 | async-start | bytes 1179648 | tf_op jit(solution)/shard_map/all_gather | solution.py:156
  558.2 123.3 %reduce-scatter.17.cloned.1.call-start = ((), (), s32[]{:S(2)}) async-start(), calls=%async_computation.19 | async-start | bytes 2359296 | tf_op jit(solution)/shard_map/reduce_scatter | solution.py:229
  615.1 122.2 %all-gather.26.cloned.1.call-start = ((), (), s32[]{:S(2)}) async-start(), calls=%async_computation.20 | async-start | bytes 4325376 | tf_op jit(solution)/shard_map/all_gather | solution.py:249
  696.1 143.1 %reduce-scatter.19.cloned.1.call-start = ((), (), s32[]{:S(2)}) async-start(), calls=%async_computation.21 | async-start | bytes 8650752 | tf_op jit(solution)/shard_map/reduce_scatter | solution.py:257
  767.7 76.1 %copy-start.43 = (f32[704]{0:T(1024)S(1)}, f32[704]{0:T(1024)}, u32[]{:S(2)}) copy-start(f32[704]{0:T(1024)} %copy-done.42) | copy-start | bytes 8452
  767.7 122.8 %all-gather.28.cloned.1.call-start = ((), (), s32[]{:S(2)}) async-start(), calls=%async_computation.22 | async-start | bytes 4325376 | tf_op jit(solution)/shard_map/all_gather | solution.py:264
  848.4 416.8 %reduce-scatter.31.cloned.1.call-start = ((), (), s32[]{:S(2)}) async-start(), calls=%async_computation.28 | async-start | bytes 540672
  1130.8 304.1 %all-reduce.12.cloned.1.call-start = ((), (), s32[]{:S(2)}) async-start(), calls=%async_computation.29 | async-start | bytes 16777216
  1154.4 354.0 %reduce-scatter.21.cloned.1.call-start = ((), (), s32[]{:S(2)}) async-start(), calls=%async_computation.23 | async-start | bytes 8650752 | tf_op jit(solution)/shard_map/reduce_scatter | solution.py:293
  1165.3 489.8 %reduce-scatter.29.cloned.1.call-start = ((), (), s32[]{:S(2)}) async-start(), calls=%async_computation.27 | async-start | bytes 4325376 | tf_op jit(solution)/shard_map/reduce_scatter | solution.py:326
  1172.4 589.4 %reduce-scatter.27.cloned.1.call-start = ((), (), s32[]{:S(2)}) async-start(), calls=%async_computation.26 | async-start | bytes 8912896 | tf_op jit(solution)/shard_map/reduce_scatter | solution.py:304
  1185.0 685.9 %reduce-scatter.25.cloned.1.call-start = ((), (), s32[]{:S(2)}) async-start(), calls=%async_computation.25 | async-start | bytes 8912896 | tf_op jit(solution)/shard_map/reduce_scatter | solution.py:303
  1197.7 738.7 %reduce-scatter.23.cloned.1.call-start = ((), (), s32[]{:S(2)}) async-start(), calls=%async_computation.24 | async-start | bytes 2228224 | tf_op jit(solution)/shard_map/reduce_scatter | solution.py:302
  1203.8 304.6 %copy-start.11 = (f32[704,1024]{1,0:T(8,128)S(1)}, f32[704,1024]{1,0:T(8,128)}, u32[]{:S(2)}) copy-start(f32[704,1024]{1,0:T(8,128)} %copy-done.10) | copy-start | bytes 8650756
  1203.8 304.6 %copy-start.47 = (f32[704]{0:T(1024)S(1)}, f32[704]{0:T(1024)}, u32[]{:S(2)}) copy-start(f32[704]{0:T(1024)} %copy-done.46) | copy-start | bytes 8452
  (90 other events, 1005.3 us)
Sparse Core Ops, SparseCore 0:
  10.2 48.1 all-gather.11
  60.6 36.7 all-gather.13
  206.9 70.2 reduce-scatter.12
  279.6 50.5 all-gather.17
  331.6 40.4 all-gather.15
  374.4 50.7 all-gather.19
  436.7 69.8 reduce-scatter.14
  508.8 41.3 all-gather.21
  558.3 38.9 all-gather.23
  615.2 66.3 reduce-scatter.16
  696.2 40.9 all-gather.25
  767.8 71.3 reduce-scatter.18
  848.5 41.9 all-gather.27
  1130.9 134.1 reduce-scatter.30
  1268.7 166.2 all-reduce.11
  1437.2 71.1 reduce-scatter.20
  1511.2 143.8 reduce-scatter.28
  1659.6 102.2 reduce-scatter.26
  1766.5 104.3 reduce-scatter.24
  1875.0 61.2 reduce-scatter.22
where the time goes:
time: 1950 us; the launch traced here: 1940 us
  waiting for transfers between devices  1270 us (65%)
  matrix products  404 us (21%)
  local copies, waits for them, and re-layouts  103 us (5%)
  other arithmetic  101 us (5%)
  blocking collectives  49.1 us (3%)
    unnamed x22, waiting for transfers between devices  185 us
    reduce_scatter x1, waiting for transfers between devices, on_device(): lax.psum_scatter(grad_w_head, ('pb', 'pa', 'ta'), scatter_dimension=0, ti...  143 us
    dot_general x25, matrix products, contract(): lax.dot_general(left_op, right_op, (axes_pair, ((), ())), preferred_eleme...  138 us
    reduce_scatter x1, waiting for transfers between devices, on_device(): lax.psum_scatter(grad_w_in, ('pb', 'pa'), scatter_dimension=0, tiled=True)  109 us
    reduce_scatter x1, waiting for transfers between devices, on_device(): lax.psum_scatter(grad_w_fin, ('pb', 'pa'), scatter_dimension=1, tiled=True)  107 us
    reduce_scatter x1, waiting for transfers between devices, on_device(): lax.psum_scatter(jnp.einsum('kre,kde->rd', stacked, back_qkv, preferred_e...  71.5 us
    reduce_scatter x1, waiting for transfers between devices, on_device(): lax.psum_scatter(contract(inner_low, back_in, ((1,), (1,))), 'ta', scatte...  71.4 us
    reduce_scatter x1, waiting for transfers between devices, on_device(): lax.psum_scatter(attn_terms, 'ta', scatter_dimension=0, tiled=True)  69.8 us
  transfers between devices with their start and end apart: 20, of which 19 were waited for; matrix products, arithmetic and copies ran while one was open for 13% of the time, Pallas kernels for 0%

commit v1 on v0

v1 whole, which is shorter than its diff:
```python
import functools
import math

import jax
import jax.numpy as jnp
from jax import lax
from jax.experimental import pallas as pl
from jax.experimental.pallas import tpu as pltpu
from jax.sharding import PartitionSpec as P

HDIM = 64
QLEN = 32
LANES = 128
SHARP = 0.02
LN_EPS = 1e-05
UNIT_EPS = 1e-06
BIG = -1e30
BF = jnp.bfloat16
F32 = jnp.float32
MIB = 1024 * 1024


def nn(a, b):
    return lax.dot_general(a, b, (((1,), (0,)), ((), ())), preferred_element_type=F32)


def nt(a, b):
    return lax.dot_general(a, b, (((1,), (1,)), ((), ())), preferred_element_type=F32)


def tn(a, b):
    return lax.dot_general(a, b, (((0,), (0,)), ((), ())), preferred_element_type=F32)


def permute_kernel(segments, block, low_bits, info, x_ref, o_ref):
    tiles = x_ref.shape[1] // LANES
    lane = lax.broadcasted_iota(jnp.int32, (1, LANES), 1)
    low = info[tiles]
    for j in range(tiles):
        source = pl.multiple_of(info[j] * LANES, LANES)
        row = 0
        for i, length in enumerate(segments):
            start = pl.multiple_of(info[tiles + 1 + i], 16)
            part = x_ref[pl.ds(start, length), pl.ds(source, LANES)]
            if low_bits:
                part = part.astype(F32)
                for bit in range(low_bits):
                    step = block << bit
                    up = pltpu.roll(part, step, 1)
                    down = pltpu.roll(part, LANES - step, 1)
                    swapped = jnp.where((lane & step) != 0, up, down)
                    part = jnp.where((low & (1 << bit)) != 0, swapped, part)
                part = part.astype(o_ref.dtype)
            o_ref[pl.ds(row, length), pl.ds(j * LANES, LANES)] = part
            row += length


def permute(x, info, segments, block, low_bits):
    rows = sum(segments)
    return pl.pallas_call(
        functools.partial(permute_kernel, segments, block, low_bits),
        out_shape=jax.ShapeDtypeStruct((rows, x.shape[1]), x.dtype),
        in_specs=[
            pl.BlockSpec(memory_space=pltpu.SMEM),
            pl.BlockSpec(memory_space=pltpu.VMEM),
        ],
        out_specs=pl.BlockSpec(memory_space=pltpu.VMEM),
        compiler_params=pltpu.CompilerParams(vmem_limit_bytes=56 * MIB),
        cost_estimate=pl.CostEstimate(
            flops=rows * x.shape[1], bytes_accessed=4 * rows * x.shape[1], transcendentals=0
        ),
    )(info, x)


def pick(sel, a, b):
    return jnp.where(sel, a.astype(F32), b.astype(F32)).astype(BF)


def split3(v):
    hi = v.astype(BF).astype(F32)
    mid = (v - hi).astype(BF).astype(F32)
    return hi, mid, v - hi - mid


def in_columns(col, v, base):
    hi, mid, lo = split3(v)
    return jnp.where(col == 7, hi, jnp.where(col == 8, mid, jnp.where(col == 9, lo, base)))


def attend_kernel(slots, tile_q, n_deps, q_ref, k_ref, v_ref, aq_ref, ak_ref, *rest):
    o_ref, l_ref, kx_ref, vx_ref = rest[n_deps:]
    lane = lax.broadcasted_iota(jnp.int32, (1, LANES), 1)
    col = lane % HDIM
    sides = (lane < HDIM, lane >= HDIM)
    for h, sel in enumerate(sides):
        kx_ref[h] = pick(sel, k_ref[...], ak_ref[...])
        vx_ref[h] = pick(sel, v_ref[...], jnp.ones_like(v_ref[...]))
    keys = k_ref.shape[0]

    def work(q_at, q_n, k_at, k_n):
        rows = pl.ds(q_at, q_n)
        q, aug = q_ref[rows, :], aq_ref[rows, :]
        outs, logs = [], []
        for h, sel in enumerate(sides):
            s = nt(pick(sel, q, aug), kx_ref[h, pl.ds(k_at, k_n), :])
            top = jnp.max(s, axis=1, keepdims=True)
            p = jnp.exp(s - top).astype(BF)
            o = nn(p, vx_ref[h, pl.ds(k_at, k_n), :])
            outs.append(o / pltpu.roll(o, HDIM, 1))
            logs.append(in_columns(col, -(top + jnp.log(o)), aug.astype(F32)))
        o_ref[rows, :] = jnp.where(sides[0], outs[0], outs[1]).astype(BF)
        l_ref[rows, :] = jnp.where(sides[0], logs[1], logs[0]).astype(BF)

    work(0, slots, 0, slots)
    tokens = q_ref.shape[0] - slots

    def step(i, carry):
        work(pl.multiple_of(slots + i * tile_q, 16), tile_q, slots, keys - slots)
        return carry

    lax.fori_loop(0, tokens // tile_q, step, 0)


def attend(qkv, rows, aug_q, aug_k, slots, tile_q, first, count, kept, deps=()):
    keys, width = qkv.shape[0], qkv.shape[1] // 3
    of = lambda n, m: pl.BlockSpec((n, LANES), lambda j: (0, 3 * (first + j) + m))
    out = pl.BlockSpec((rows, LANES), lambda j: (0, first + j))
    fixed = lambda n: pl.BlockSpec((n, LANES), lambda j: (0, 0))
    deps = tuple(kept) + tuple(deps)
    return pl.pallas_call(
        functools.partial(attend_kernel, slots, tile_q, len(deps)),
        grid=(count,),
        out_shape=(jax.ShapeDtypeStruct((rows, width), BF), jax.ShapeDtypeStruct((rows, width), BF)),
        in_specs=[of(rows, 0), of(keys, 1), of(keys, 2), fixed(rows), fixed(keys)]
        + [pl.BlockSpec(memory_space=pl.ANY)] * len(deps),
        out_specs=(out, out),
        input_output_aliases={5 + i: i for i in range(len(kept))},
        scratch_shapes=[pltpu.VMEM((2, keys, LANES), BF), pltpu.VMEM((2, keys, LANES), BF)],
        compiler_params=pltpu.CompilerParams(vmem_limit_bytes=56 * MIB),
        cost_estimate=pl.CostEstimate(
            flops=16 * rows * keys * count * LANES,
            bytes_accessed=2 * (3 * rows + 2 * keys) * count * LANES,
            transcendentals=2 * rows * keys * count,
        ),
    )(qkv, qkv, qkv, aug_q, aug_k, *deps)


def attend_back_kernel(
    slots, tile_k, scale, n_deps,
    q_ref, k_ref, v_ref, o_ref, do_ref, l_ref, ak_ref, *rest,
):
    (
        dqkv_ref, sum_ref,
        qx_ref, qz_ref, dx_ref, dz_ref, kx_ref, vx_ref, kt_ref, acc_ref,
    ) = rest[n_deps:]
    lane = lax.broadcasted_iota(jnp.int32, (1, LANES), 1)
    col = lane % HDIM
    sides = (lane < HDIM, lane >= HDIM)
    rows, keys = q_ref.shape[0], k_ref.shape[0]
    tokens = rows - slots
    grad = do_ref[...].astype(F32)
    prod = grad * o_ref[...].astype(F32)
    zero = jnp.zeros_like(grad)
    for h, sel in enumerate(sides):
        delta = jnp.sum(jnp.where(sel, prod, 0.0), axis=1, keepdims=True)
        qx_ref[h] = pick(sel, q_ref[...], l_ref[...])
        qz_ref[h] = pick(sel, q_ref[...], zero)
        dx_ref[h] = jnp.where(sel, grad, in_columns(col, -delta, zero)).astype(BF)
        dz_ref[h] = jnp.where(sel, grad, 0.0).astype(BF)
        kx_ref[h] = pick(sel, k_ref[...], ak_ref[...])
        vx_ref[h] = pick(sel, v_ref[...], ak_ref[...])
        kt_ref[h] = jnp.where(sel, k_ref[...].astype(F32), 0.0).T.astype(BF)

    def work(q_at, q_n, k_at, k_n, kt_at):
        dq = None
        dk = jnp.zeros((k_n, LANES), F32)
        dv = jnp.zeros((k_n, LANES), F32)
        for h in range(2):
            at, of = pl.ds(k_at, k_n), pl.ds(q_at, q_n)
            p = jnp.exp(nt(kx_ref[h, at, :], qx_ref[h, of, :]))
            dp = nt(vx_ref[h, at, :], dx_ref[h, of, :])
            ds = (p * dp).astype(BF)
            dv += nn(p.astype(BF), dz_ref[h, of, :])
            dk += nn(ds, qz_ref[h, of, :])
            part = nn(kt_ref[h, :, pl.ds(kt_at, k_n)], ds)
            dq = part if dq is None else dq + part
        return dq, dk, dv

    def keep(at, n, dk, dv):
        dqkv_ref[pl.ds(at, n), pl.ds(LANES, LANES)] = dk.astype(BF)
        dqkv_ref[pl.ds(at, n), pl.ds(2 * LANES, LANES)] = dv.astype(BF)

    dq, dk, dv = work(0, slots, 0, slots, 0)
    dq = dq.T * scale
    dqkv_ref[pl.ds(0, slots), pl.ds(0, LANES)] = dq.astype(BF)
    keep(0, slots, dk, dv)
    acc_ref[...] = jnp.zeros_like(acc_ref)
    sum_v = jnp.sum(dv, axis=0, keepdims=True)
    sum_q = jnp.sum(dq, axis=0, keepdims=True)
    for i in range((keys - slots) // tile_k):
        at = slots + i * tile_k
        dq, dk, dv = work(slots, tokens, at, tile_k, at)
        acc_ref[...] += dq
        keep(at, tile_k, dk, dv)
        sum_v += jnp.sum(dv, axis=0, keepdims=True)
    dq = acc_ref[...].T * scale
    dqkv_ref[pl.ds(slots, tokens), pl.ds(0, LANES)] = dq.astype(BF)
    dqkv_ref[pl.ds(rows, keys - rows), pl.ds(0, LANES)] = jnp.zeros((keys - rows, LANES), BF)
    sum_q += jnp.sum(dq, axis=0, keepdims=True)
    sum_ref[pl.ds(0, 1), :] = sum_q
    sum_ref[pl.ds(1, 1), :] = sum_v
    sum_ref[pl.ds(2, 6), :] = jnp.zeros((6, LANES), F32)


def attend_back(qkv, o, do, logs, aug_k, slots, tile_k, scale, first, count, kept, deps=()):
    rows, width = o.shape
    keys = qkv.shape[0]
    of = lambda n, m: pl.BlockSpec((n, LANES), lambda j: (0, 3 * (first + j) + m))
    col = lambda n: pl.BlockSpec((n, LANES), lambda j: (0, first + j))
    fixed = lambda n: pl.BlockSpec((n, LANES), lambda j: (0, 0))
    wide = lambda n: pltpu.VMEM((2, n, LANES), BF)
    deps = tuple(kept) + tuple(deps)
    return pl.pallas_call(
        functools.partial(attend_back_kernel, slots, tile_k, scale, len(deps)),
        grid=(count,),
        out_shape=(
            jax.ShapeDtypeStruct((keys, 3 * width), BF),
            jax.ShapeDtypeStruct((8, width), F32),
        ),
        in_specs=[of(rows, 0), of(keys, 1), of(keys, 2), col(rows), col(rows), col(rows), fixed(keys)]
        + [pl.BlockSpec(memory_space=pl.ANY)] * len(deps),
        out_specs=(pl.BlockSpec((keys, 3 * LANES), lambda j: (0, first + j)), col(8)),
        input_output_aliases={7 + i: i for i in range(len(kept))},
        scratch_shapes=[
            wide(rows), wide(rows), wide(rows), wide(rows), wide(keys), wide(keys),
            pltpu.VMEM((2, LANES, keys), BF),
            pltpu.VMEM((LANES, rows - slots), F32),
        ],
        compiler_params=pltpu.CompilerParams(vmem_limit_bytes=56 * MIB),
        cost_estimate=pl.CostEstimate(
            flops=40 * rows * keys * count * LANES,
            bytes_accessed=2 * (6 * rows + 4 * keys) * count * LANES,
            transcendentals=2 * rows * keys * count,
        ),
    )(qkv, qkv, qkv, o, do, logs, aug_k, *deps)


def nothing(*refs):
    return None


def tie(x, *deps):
    anywhere = pl.BlockSpec(memory_space=pl.ANY)
    return pl.pallas_call(
        nothing,
        out_shape=jax.ShapeDtypeStruct(x.shape, x.dtype),
        in_specs=[anywhere] * (1 + len(deps)),
        out_specs=anywhere,
        input_output_aliases={0: 0},
        cost_estimate=pl.CostEstimate(flops=0, bytes_accessed=0, transcendentals=0),
    )(x, *deps)


def chunk_of(m):
    return m if m <= 704 else m // 2


def mm_in_kernel(chunk, epilogue, start, finish, n_extra, n_deps, a_ref, h_ref, r_ref, *rest):
    extra, outs = rest[:n_extra], rest[n_extra + n_deps :]
    k = h_ref.shape[0]

    def step(i, carry):
        rows = pl.ds(pl.multiple_of(i * chunk, 16), chunk)
        acc = nn(a_ref[rows, pl.ds(0, k)], h_ref[...]) + nn(a_ref[rows, pl.ds(k, k)], r_ref[...])
        return epilogue(acc, rows, extra, outs, carry)

    last = lax.fori_loop(0, a_ref.shape[0] // chunk, step, start(h_ref.shape[1]))
    finish(last, outs)


def nought(tn):
    return 0


def leave(carry, outs):
    return None


def mm_in(a, h, r, col, width, tn, epilogue, extra, outs, start=nought, finish=leave, deps=()):
    m, k = a.shape[0], h.shape[0] // 2
    tiles = width // tn
    weight = pl.BlockSpec((k, tn), lambda t, j: (t, col // tn + j))
    wide = lambda n: pl.BlockSpec((n, tn), lambda t, j: (0, t * tiles + j))
    return pl.pallas_call(
        functools.partial(mm_in_kernel, chunk_of(m), epilogue, start, finish, len(extra), len(deps)),
        grid=(2, tiles),
        out_shape=tuple(jax.ShapeDtypeStruct((n, 2 * width), dt) for n, dt in outs),
        in_specs=[pl.BlockSpec((m, 2 * k), lambda t, j: (0, 0)), weight, weight]
        + [wide(e.shape[0]) for e in extra]
        + [pl.BlockSpec(memory_space=pl.ANY)] * len(deps),
        out_specs=tuple(wide(n) for n, _ in outs),
        compiler_params=pltpu.CompilerParams(vmem_limit_bytes=56 * MIB),
        cost_estimate=pl.CostEstimate(
            flops=8 * m * k * width,
            bytes_accessed=4 * m * k + 8 * k * width + sum(2 * width * n * 2 for n, _ in outs),
            transcendentals=0,
        ),
    )(a, h, r, *extra, *deps)


def mm_out_kernel(chunk, half_tiles, n_extra, epilogue, a0_ref, a1_ref, h0_ref, h1_ref, r0_ref, r1_ref, *rest):
    extra, o_ref = rest[:n_extra], rest[-1]

    def run(w0_ref, w1_ref):
        def step(i, carry):
            rows = pl.ds(pl.multiple_of(i * chunk, 16), chunk)
            acc = nt(a0_ref[rows, :], w0_ref[...]) + nt(a1_ref[rows, :], w1_ref[...])
            more = [e[rows, :] if e.shape[0] > 8 else e[pl.ds(0, 1), :] for e in extra]
            o_ref[rows, :] = epilogue(acc, *more).astype(o_ref.dtype)
            return carry

        lax.fori_loop(0, a0_ref.shape[0] // chunk, step, 0)

    i = pl.program_id(0)

    @pl.when(i < half_tiles)
    def _():
        run(h0_ref, h1_ref)

    @pl.when(i >= half_tiles)
    def _():
        run(r0_ref, r1_ref)


def mm_out(a, m, h, r, col, width, td, epilogue, extra, dtype, deps=()):
    k = h.shape[0] // 2
    half = k // td
    at = col // width
    lhs = lambda t: pl.BlockSpec((m, width), lambda i: (0, t))
    own = lambda t: pl.BlockSpec((td, width), lambda i: (t * half + jnp.minimum(i, half - 1), at))
    oth = lambda t: pl.BlockSpec((td, width), lambda i: (t * half + jnp.maximum(i - half, 0), at))
    wide = lambda n: pl.BlockSpec((n, td), lambda i: (0, i))
    return pl.pallas_call(
        functools.partial(mm_out_kernel, chunk_of(m), half, len(extra), epilogue),
        grid=(2 * half,),
        out_shape=jax.ShapeDtypeStruct((m, 2 * k), dtype),
        in_specs=[lhs(0), lhs(1), own(0), own(1), oth(0), oth(1)]
        + [wide(e.shape[0]) for e in extra]
        + [pl.BlockSpec(memory_space=pl.ANY)] * len(deps),
        out_specs=wide(m),
        compiler_params=pltpu.CompilerParams(vmem_limit_bytes=56 * MIB),
        cost_estimate=pl.CostEstimate(
            flops=8 * m * k * width,
            bytes_accessed=4 * m * width + 8 * k * width + 8 * m * k,
            transcendentals=0,
        ),
    )(a, a, h, h, r, r, *extra, *deps)


def put_plain(acc, rows, extra, outs, carry):
    outs[0][rows, :] = acc.astype(outs[0].dtype)
    return carry


def put_biased(acc, rows, extra, outs, carry):
    outs[0][rows, :] = (acc + extra[0][pl.ds(0, 1), :]).astype(outs[0].dtype)
    return carry


def put_scaled(acc, rows, extra, outs, carry):
    low = (acc + extra[0][pl.ds(0, 1), :]).astype(BF).astype(F32)
    outs[0][rows, :] = (low * extra[0][pl.ds(1, 1), :]).astype(BF)
    return carry


def put_gelu(acc, rows, extra, outs, carry):
    inner = acc + extra[0][pl.ds(0, 1), :]
    cdf, pdf = normal_parts(inner)
    outs[0][rows, :] = (inner * cdf).astype(BF)
    outs[1][rows, :] = (cdf + inner * pdf).astype(BF)
    return carry


def put_sloped(acc, rows, extra, outs, carry):
    grad = acc * extra[0][rows, :].astype(F32)
    outs[0][rows, :] = grad.astype(BF)
    return carry + jnp.sum(grad, axis=0, keepdims=True)


def row_of_zeros(tn):
    return jnp.zeros((1, tn), F32)


def put_sum(carry, outs):
    outs[1][...] = jnp.broadcast_to(carry, outs[1].shape)


def eight(*rows):
    return jnp.concatenate([jnp.stack(rows), jnp.zeros((8 - len(rows), rows[0].shape[0]), F32)])


def normal_parts(v):
    t = 1.0 / (1.0 + (0.3275911 * math.sqrt(0.5)) * jnp.abs(v))
    bell = jnp.exp(-0.5 * v * v)
    poly = 0.5 * 1.061405429 * t - 0.5 * 1.453152027
    poly = (poly * t + 0.5 * 1.421413741) * t - 0.5 * 0.284496736
    tail = ((poly * t + 0.5 * 0.254829592) * t) * bell
    return jnp.where(v < 0.0, tail, 1.0 - tail), bell * (1.0 / math.sqrt(2.0 * math.pi))


def norm_parts(v):
    centered = v - jnp.mean(v, axis=-1, keepdims=True)
    rstd = lax.rsqrt(jnp.mean(centered * centered, axis=-1, keepdims=True) + LN_EPS)
    return centered * rstd, rstd


def norm_back(c, vhat, rstd, gain):
    gc = c * gain
    back = (
        gc
        - jnp.mean(gc, axis=-1, keepdims=True)
        - vhat * jnp.mean(gc * vhat, axis=-1, keepdims=True)
    ) * rstd
    return back, jnp.sum(c * vhat, axis=0), jnp.sum(c, axis=0)


def make(n_pb, n_pa, n_ta):
    cores = 2
    n_x = n_pb // cores
    blocks = n_pb * n_pa

    def px(v, k):
        return lax.ppermute(v, "pb", [(i, i ^ (cores * k)) for i in range(n_pb)])

    def pc(v):
        return lax.ppermute(v, "pb", [(i, i ^ 1) for i in range(n_pb)])

    def pz(v, k):
        return lax.ppermute(v, "pa", [(i, i ^ k) for i in range(n_pa)])

    def py(v):
        return lax.ppermute(v, "ta", [(i, i ^ 1) for i in range(n_ta)])

    x_bits = n_x.bit_length() - 1
    z_bits = n_pa.bit_length() - 1

    def gather_z_step(have, bit):
        other = pz(have, 1 << bit)
        return jnp.stack([have, other], axis=1).reshape((-1,) + have.shape[1:])

    def gather_z_rest(have):
        for bit in reversed(range(z_bits - 1)):
            have = gather_z_step(have, bit)
        return have.reshape(-1, have.shape[-1])

    def gather_z(shard):
        return gather_z_rest(gather_z_step(shard[None], z_bits - 1))

    def gather_x(a):
        have = a[None]
        for bit in range(x_bits):
            have = jnp.concatenate([have, px(have, 1 << bit)], axis=0)
        return have

    def halves_of(a):
        n = a.shape[0] // 2
        return a[:n], a[n:]

    def gather_xy_one(near, far):
        return gather_x(near), py(far)

    def gather_xy_two(near, far, far_oth):
        n = far.shape[0]
        both = gather_x(jnp.concatenate([far, far_oth], axis=0))
        near_oth = py(near)
        own = jnp.concatenate([near, both[:, :n]], axis=1)
        oth = jnp.concatenate([near_oth, both[:, n:]], axis=1)
        cols = far.shape[1]
        return jnp.concatenate([own.reshape(-1, cols), oth.reshape(-1, cols)], axis=0)

    def add(a, b):
        return (a.astype(F32) + b.astype(F32)).astype(a.dtype)

    def away_part(lhs, rhs):
        return pc(tn(lhs[:, lhs.shape[1] // 2 :], rhs).astype(BF))

    def core_part(lhs, rhs, away):
        return (tn(lhs[:, : lhs.shape[1] // 2], rhs) + away.astype(F32)).astype(BF)

    def cut(parts, x, s, sides):
        size = parts[0].shape[0] // n_x
        half = size // 2
        row = x * size + s * half
        out = []
        for t in sides:
            for r in parts:
                n = r.shape[1] // n_ta
                out.append(r[row : row + half, t * n : (t + 1) * n])
        return jnp.concatenate(out, axis=1) if len(out) > 1 else out[0]

    def p1_send(parts):
        near = [cut(parts, k, 0, (0, 1)) for k in range(n_x)]
        far_own = jnp.concatenate([cut(parts, k, 1, (0,)) for k in range(n_x)], axis=0)
        far_oth = jnp.concatenate([cut(parts, k, 1, (1,)) for k in range(n_x)], axis=0)
        return near, far_own, far_oth

    def p1_go(sent):
        near, far_own, far_oth = sent
        return [px(near[k], k) for k in range(1, n_x)], py(far_oth)

    def p1_end(sent, got):
        near = sent[0][0]
        for g in got[0]:
            near = add(near, g)
        far = add(sent[1], got[1])
        n = near.shape[1] // 2
        half = far.shape[0] // n_x
        return near[:, :n], near[:, n:], [far[k * half : (k + 1) * half] for k in range(n_x)]

    def p2_go(state):
        near_own, near_oth, far = state
        return py(near_oth), [px(far[k], k) for k in range(1, n_x)]

    def p2_end(state, got, w):
        near = add(state[0], got[0])
        far = state[2][0]
        for g in got[1]:
            far = add(far, g)
        return jnp.concatenate([near, far], axis=0).reshape(n_pa, w, -1)

    def z_split(cur):
        cur = cur.reshape((cur.shape[0] // 2, 2) + cur.shape[1:])
        return cur[:, 0], cur[:, 1]

    def reduce_z(cur, first=0):
        for bit in range(first, z_bits):
            keep, give = z_split(cur)
            got = pz(give, 1 << bit)
            cur = add(keep, got) if bit < z_bits - 1 else keep.astype(F32) + got.astype(F32)
        return cur[0]

    def on_device(
        rows_in, w_qkv, b_qv, w_out, b_out, ln1_gain, ln1_bias, w_in, b_in, w_fin, b_fin,
        ln2_gain, ln2_bias, w_head, b_head, lengths, query_len, score_grad,
    ):
        t0 = lax.axis_index("ta")
        z0 = lax.axis_index("pa")
        p0 = lax.axis_index("pb")
        x0, c0 = p0 // cores, p0 % cores
        first_t = t0 == 0
        all_rows, width = rows_in.shape
        half_rows = all_rows // n_ta
        n_q, n_p = query_len.shape[1], lengths.shape[1]
        q_here = n_q // n_ta
        slots = q_here * QLEN
        toks = half_rows - slots
        block = width // blocks
        heads_half = w_qkv.shape[2]
        scale = 1.0 / math.sqrt(HDIM)

        per_tile = LANES // block
        z_tiles = n_pa // per_tile
        low_bits = per_tile.bit_length() - 1
        forward, backward = [], []
        for c in range(cores):
            for x in range(n_x):
                for z in range(z_tiles):
                    forward.append((((x ^ x0) * cores) + (c ^ c0)) * z_tiles + (z ^ (z0 // per_tile)))
        for x in range(n_x):
            for c in range(cores):
                for z in range(z_tiles):
                    backward.append((((c ^ c0) * n_x) + (x ^ x0)) * z_tiles + (z ^ (z0 // per_tile)))
        low = z0 % per_tile
        as_info = lambda v: jnp.stack([jnp.asarray(a, jnp.int32) for a in v])
        row_info = as_info(forward + [low, t0 * half_rows, (1 - t0) * half_rows + slots])
        vec_info = as_info(forward + [low, 0])
        back_info = as_info(backward + [low, 0])

        rows = permute(rows_in, row_info, (half_rows, toks), block, low_bits)
        vecs = jnp.stack(
            [b_out, ln1_gain, ln1_bias, b_fin, ln2_gain, ln2_bias, b_out, b_out]
        )
        vecs = permute(vecs, vec_info, (8,), block, low_bits)
        b_out_r, g1, be1, b_fin_r, g2, be2 = (vecs[i] for i in range(6))
        pairs = heads_half // LANES
        all_pairs = n_ta * pairs
        ff_half = w_in.shape[1]
        head_half = width // n_ta
        qkv_half = 3 * heads_half
        swapped = lambda v: jnp.concatenate([v[..., v.shape[-1] // 2 :], v[..., : v.shape[-1] // 2]], axis=-1)
        in_order = lambda v: jnp.where(first_t, v, swapped(v))

        packed = lambda v: v.reshape(v.shape[0], 3, pairs, LANES).transpose(0, 2, 1, 3)
        shard_q = packed(w_qkv.transpose(1, 0, 2).reshape(block, qkv_half)).reshape(block, -1)
        shard_m = jnp.concatenate([w_in, w_out.T], axis=1)
        head_mine = lax.dynamic_slice_in_dim(w_head, t0 * head_half, head_half, 1)
        shard_e = jnp.concatenate([w_fin.T, head_mine], axis=1)

        zq = gather_z(shard_q)
        near, far = halves_of(zq)
        zm_1 = gather_z_step(tie(shard_m, zq)[None], z_bits - 1)
        near_q, oth_q = gather_xy_one(near, far)
        near_q = tie(near_q, zm_1)
        zm = gather_z_rest(zm_1)
        h_q = tie(gather_xy_two(near_q, far, oth_q), zm)
        r_q = pc(h_q)
        near, far_m = halves_of(zm)
        near_m, oth_m = gather_xy_one(near, far_m)
        ze_1 = gather_z_step(tie(shard_e, zm)[None], z_bits - 1)
        bias_of = lambda b: packed(jnp.concatenate([b[0], jnp.zeros_like(b[0]), b[1]])[None]).reshape(-1)
        qkv_bias = jnp.concatenate([bias_of(b_qv), bias_of(py(b_qv))])
        b_in_r = jnp.concatenate([b_in, py(b_in)])

        row_id = jnp.arange(half_rows + toks, dtype=jnp.int32)
        is_slot = row_id < slots
        token = jnp.where(
            row_id < half_rows, t0 * toks + row_id - slots, (1 - t0) * toks + row_id - half_rows
        )
        ends = jnp.cumsum(lengths[0])
        pid = jnp.sum((token[:, None] >= ends[None, :]).astype(jnp.int32), axis=1)
        q_lens = lax.dynamic_index_in_dim(query_len, z0, 0, keepdims=False)
        q_lens = lax.dynamic_slice_in_dim(q_lens, t0 * q_here, q_here, 0)
        limit = jnp.sum(
            jnp.where(
                (row_id // QLEN)[:, None] == jnp.arange(q_here, dtype=jnp.int32)[None, :],
                q_lens[None, :], 0,
            ),
            axis=1,
        )
        dead = is_slot & (row_id % QLEN >= limit)
        seg = jnp.where(is_slot, n_p + row_id // QLEN, pid)
        lane_c = jnp.arange(LANES, dtype=jnp.int32)[None, :] % HDIM
        same = seg[:, None] == lane_c
        aug_k = jnp.where(
            lane_c < 6, same & ~dead[:, None], jnp.where(lane_c == 6, dead[:, None], (lane_c >= 7) & (lane_c < 10))
        )
        aug_k = aug_k.astype(BF)
        aug_q = jnp.where((lane_c < 7) & ~same[:half_rows], BIG, 0.0).astype(BF)

        col_scale = jnp.tile(jnp.repeat(jnp.array([scale, 1.0, 1.0], F32), LANES), all_pairs)
        (qkv,) = mm_in(
            rows, h_q, r_q, 0, qkv_half, qkv_half // 3, put_scaled, (eight(qkv_bias, col_scale),),
            ((half_rows + toks, BF),),
        )
        oth_m, near_m = tie(oth_m, qkv), tie(near_m, qkv)
        h_m = gather_xy_two(near_m, far_m, oth_m)
        ze_1 = tie(ze_1, qkv)
        ze = gather_z_rest(ze_1)
        kept, n_call = (), all_pairs // 4
        for i in range(4):
            kept = attend(
                qkv, half_rows, aug_q, aug_k, slots, toks // 2, i * n_call, n_call, kept,
                ((oth_m, near_m, ze_1), (), (ze,), ())[i],
            )
            if i == 1:
                ze = tie(ze, kept[0])
                near, far_e = halves_of(ze)
                near_e, oth_e = gather_xy_one(near, far_e)
            if i == 2:
                h_m = tie(h_m, kept[0])
                r_m = pc(h_m)
        ctx, logs = kept
        near_e, oth_e = tie(near_e, kept[0]), tie(oth_e, kept[0])
        h_one = mm_out(
            ctx, half_rows, h_m, r_m, ff_half, heads_half, heads_half // 2,
            lambda acc, res, b: acc + res.astype(F32) + b, (rows[:half_rows], eight(b_out_r)), F32,
            (near_e, oth_e),
        )
        h_e = gather_xy_two(near_e, far_e, oth_e)
        v1, r1 = norm_parts(h_one)
        normed = v1 * g1 + be1
        normed_low = normed.astype(BF)
        active, slope = mm_in(
            normed_low, h_m, r_m, 0, ff_half, ff_half // 4, put_gelu, (eight(b_in_r),),
            ((half_rows, BF), (half_rows, BF)),
        )
        h_e = tie(h_e, active)
        r_e = pc(h_e)
        h_two = mm_out(
            active, half_rows, h_e, r_e, 0, ff_half, heads_half // 2,
            lambda acc, res, b: acc + res + b, (normed, eight(b_fin_r)), F32,
        )
        v2, r2 = norm_parts(h_two)
        output_low = (v2 * g2 + be2).astype(BF)
        (raw,) = mm_in(
            output_low, h_e, r_e, ff_half, head_half, head_half, put_biased,
            (eight(in_order(b_head)),), ((half_rows, F32),),
        )
        inv = lax.rsqrt(jnp.sum(raw * raw, axis=-1, keepdims=True) + UNIT_EPS)
        unit = raw * inv
        unit_low = unit.astype(BF)

        passages = unit_low[slots:]
        mine = gather_z(unit_low[:slots])
        asked = jnp.concatenate([mine, swapped(py(mine))], axis=0)
        n_asked = asked.shape[0]
        z_rel = jnp.arange(n_pa, dtype=jnp.int32) ^ z0
        swap_t = lambda a: jnp.where(first_t, a, a[::-1])
        lens = swap_t(
            jnp.take(query_len, z_rel, axis=0).reshape(n_pa, n_ta, q_here).transpose(1, 0, 2)
        )
        valid = (
            jnp.arange(QLEN, dtype=jnp.int32)[None, None, None, :] < lens[..., None]
        ).astype(F32)
        up = swap_t(
            jnp.take(score_grad[0], z_rel, axis=0).reshape(n_pa, n_ta, q_here, n_p).transpose(1, 0, 2, 3)
        )
        token_grad = (up[:, :, :, None, :] * valid[..., None]).reshape(n_asked, n_p)
        member = (
            pid[slots:half_rows, None] == jnp.arange(n_p, dtype=jnp.int32)[None, :]
        ).astype(F32)
        powers = jnp.exp(nt(asked, passages) * (1.0 / SHARP))
        sums = jnp.dot(powers, member, precision=lax.Precision.HIGHEST)
        theirs = py(sums.reshape(n_ta, n_asked // n_ta, n_p)[::-1])
        sums = sums + theirs.reshape(n_asked, n_p)
        soft = (SHARP * jnp.log(sums)).reshape(n_ta, n_pa, q_here, QLEN, n_p)
        scores = jnp.sum(soft[0] * valid[0][..., None], axis=2)
        scores = jnp.take(scores, z_rel, axis=0)[None]
        coef = token_grad / sums
        coef_j = sum(coef[:, i : i + 1] * member[:, i][None, :] for i in range(n_p))
        sim_grad = (powers * coef_j).astype(BF)
        ask_grad = nn(sim_grad, passages).astype(BF).reshape(n_ta, n_pa * slots, width)
        ask_sum = add(ask_grad[0], py(swapped(ask_grad[1])))
        passage_grad = tn(sim_grad, asked)
        unit_grad = jnp.concatenate(
            [reduce_z(ask_sum.reshape(n_pa, slots, width)), passage_grad], axis=0
        )

        raw_grad = inv * (unit_grad - unit * jnp.sum(unit * unit_grad, axis=-1, keepdims=True))
        g_b_head = in_order(jnp.sum(raw_grad, axis=0))
        raw_low = raw_grad.astype(BF)
        output_grad = mm_out(
            raw_low, half_rows, h_e, r_e, ff_half, head_half, heads_half // 2, lambda acc: acc, (), F32
        )
        h_two_grad, g_g2, g_be2 = norm_back(output_grad, v2, r2, g2)
        g_b_fin = jnp.sum(h_two_grad, axis=0)
        branch_low = h_two_grad.astype(BF)
        away_fin = away_part(branch_low, active)
        away_head = away_part(output_low, raw_low)
        inner_low, sums_in = mm_in(
            branch_low, h_e, r_e, 0, ff_half, ff_half // 4, put_sloped, (slope,),
            ((half_rows, BF), (8, F32)), row_of_zeros, put_sum,
        )
        part_fin = core_part(branch_low, active, away_fin)
        part_head = core_part(output_low, raw_low, away_head)
        sent_f = p1_send([part_fin, part_head])
        got_f = p1_go(sent_f)
        away_in = away_part(normed_low, inner_low)
        normed_grad = mm_out(
            inner_low, half_rows, h_m, r_m, 0, ff_half, heads_half // 2,
            lambda acc, res: acc + res, (h_two_grad,), F32, (sent_f[0][-1], sent_f[2]),
        )
        h_one_grad, g_g1, g_be1 = norm_back(normed_grad, v1, r1, g1)
        g_b_out = jnp.sum(h_one_grad, axis=0)
        attended_low = h_one_grad.astype(BF)
        away_out = away_part(attended_low, ctx)
        (d_ctx,) = mm_in(
            attended_low, h_m, r_m, ff_half, heads_half, heads_half, put_plain, (), ((half_rows, BF),)
        )
        part_in = core_part(normed_low, inner_low, away_in)
        part_out = core_part(attended_low, ctx, away_out)
        sent_m = p1_send([part_in, part_out])
        got_m = p1_go(sent_m)
        state_f = p1_end(sent_f, got_f)
        got_f = p2_go(state_f)

        back = lambda i, kept, deps: attend_back(
            qkv, ctx, d_ctx, logs, aug_k, slots, toks // 5, scale,
            ((i + 2) % 4) * n_call, n_call, kept, deps,
        )
        quarter = qkv_half // 2
        columns = lambda a, i: a[:, i * quarter : (i + 1) * quarter]
        rows_x = width // (cores * n_x)
        x_blocks = lambda part: [part[k * rows_x : (k + 1) * rows_x] for k in range(n_x)]
        x_go = lambda blocks_of: [px(blocks_of[k], k) for k in range(1, n_x)]

        def x_end(blocks_of, got):
            total = blocks_of[0]
            for g in got:
                total = add(total, g)
            return total

        kept = back(0, (), (sent_m[0][-1], sent_m[2], state_f[1], state_f[2][-1]))
        cur_f = tie(p2_end(state_f, got_f, block), kept[1])
        keep_f, give_f = z_split(cur_f)
        z_f = pz(give_f, 1)
        kept = back(1, kept, (give_f,))
        away_1 = away_part(rows, kept[0][:, qkv_half:])
        state_m = p1_end(sent_m, [[tie(g, kept[1]) for g in got_m[0]], tie(got_m[1], kept[1])])
        got_m = p2_go(state_m)
        cur_f = tie(add(keep_f, z_f), kept[1])
        part_1 = core_part(rows, kept[0][:, qkv_half:], away_1)
        sent_1 = x_blocks(part_1)
        got_1 = x_go(sent_1)
        kept = back(2, kept, (state_m[1], state_m[2][-1], cur_f, sent_1[1]))
        away_2 = away_part(rows, columns(kept[0], 0))
        cur_m = tie(p2_end(state_m, got_m, block), kept[1])
        keep_m, give_m = z_split(cur_m)
        z_m = pz(give_m, 1)
        out_f = reduce_z(cur_f, 1)
        y_1 = x_end(sent_1, [tie(g, kept[1]) for g in got_1])
        part_2 = core_part(rows, columns(kept[0], 0), away_2)
        sent_2 = x_blocks(part_2)
        got_2 = x_go(sent_2)
        kept = back(3, kept, (give_m, y_1, sent_2[1]))
        d_qkv, sums_qv = kept
        y_1 = tie(py(y_1), sums_qv)
        to_other = mm_out(
            d_qkv[half_rows:], toks, h_q, r_q, 0, qkv_half, heads_half // 2, lambda acc: acc, (), BF
        )
        to_other = py(to_other)
        away_3 = away_part(rows, columns(d_qkv, 1))
        out_m = reduce_z(add(keep_m, z_m), 1)
        part_3 = core_part(rows, columns(d_qkv, 1), away_3)
        sent_3 = x_blocks(part_3)
        got_3 = x_go(sent_3)
        grad_rows = mm_out(
            d_qkv, half_rows, h_q, r_q, 0, qkv_half, heads_half // 2,
            lambda acc, res: acc + res, (h_one_grad,), F32,
        )
        as_z = lambda a: a.reshape(n_pa, block, -1)
        out_2 = reduce_z(as_z(add(x_end(sent_2, got_2), y_1[:, :quarter])))
        out_3 = reduce_z(as_z(add(x_end(sent_3, got_3), y_1[:, quarter:])))
        out_q = jnp.concatenate([out_2, out_3], axis=1)
        g_w_qkv = out_q.reshape(block, pairs, 3, LANES).transpose(2, 0, 1, 3).reshape(3, block, heads_half)
        g_w_fin, g_head = out_f[:, :ff_half], out_f[:, ff_half:]
        g_w_in, g_w_out = out_m[:, :ff_half], out_m[:, ff_half:]
        n_h = block // n_ta
        head_keep = jnp.where(first_t, g_head[:n_h], g_head[n_h:])
        head_got = py(jnp.where(first_t, g_head[n_h:], g_head[:n_h]))
        g_w_head = in_order(jnp.concatenate([head_keep, head_got], axis=1))
        grad_rows = grad_rows + jnp.concatenate(
            [jnp.zeros((slots, width), F32), to_other.astype(F32)], axis=0
        )
        grad_rows = permute(grad_rows, back_info, (half_rows,), block, low_bits)

        rel = jnp.arange(blocks, dtype=jnp.int32)
        rel_c, rel_x, rel_z = rel // (n_x * n_pa), (rel // n_pa) % n_x, rel % n_pa
        source = ((rel_x ^ x0) * cores + (rel_c ^ c0)) * n_pa + (rel_z ^ z0)
        by_block = lambda v: v.reshape(blocks, n_ta, -1)
        absolute = jnp.concatenate(
            [by_block(in_order(v)) for v in (sums_in[0], sums_qv[0], sums_qv[1])] + [by_block(g_b_head)],
            axis=2,
        )
        absolute = jnp.take(absolute, source, axis=0)
        vec = jnp.concatenate(
            [absolute] + [by_block(v) for v in (g_b_out, g_g1, g_be1, g_b_fin, g_g2, g_be2)], axis=2
        )
        vec = jnp.where(first_t, vec, vec[:, ::-1]).reshape(cores, blocks // cores, n_ta, -1)
        vec = vec[0] + pc(vec[1])
        vec = vec.reshape(n_x, n_pa, n_ta, -1)
        total = vec[0]
        for k in range(1, n_x):
            total = total + px(vec[k], k)
        vec = reduce_z(total[:, 0] + py(total[:, 1]))
        w32 = width // (blocks * n_ta)
        sizes = [n_ta * ff_half // (blocks * n_ta)] + [w32] * 9
        offs = [sum(sizes[:i]) for i in range(len(sizes) + 1)]
        (o_b_in, o_bq, o_bv, o_b_head, o_b_out, o_g1, o_be1, o_b_fin, o_g2, o_be2) = (
            vec[offs[i] : offs[i + 1]] for i in range(10)
        )
        return (
            scores, grad_rows, g_w_qkv, jnp.stack([o_bq, o_bv]), g_w_out.T, o_b_out, o_g1, o_be1,
            g_w_in, o_b_in, g_w_fin.T, o_b_fin, o_g2, o_be2, g_w_head, o_b_head,
        )

    return on_device


def solution(mesh):
    both = ("pb", "pa")
    every = ("pb", "pa", "ta")
    in_specs = (
        P(both, None), P(None, both, "ta"), P(None, "ta"), P("ta", both), P(), P(), P(),
        P(both, "ta"), P("ta"), P("ta", both), P(), P(), P(), P(both, None), P(),
        P(both, None), P("pb", None), P("pb", None, None, "pa"),
    )
    out_specs = (
        P("pb", None, "ta", "pa"), P(every, None), P(None, both, "ta"), P(None, every),
        P("ta", both), P(every), P(every), P(every), P(both, "ta"), P(every), P("ta", both),
        P(every), P(every), P(every), P(every, None), P(every),
    )
    step = make(mesh.shape["pb"], mesh.shape["pa"], mesh.shape["ta"])
    return jax.shard_map(step, mesh=mesh, in_specs=in_specs, out_specs=out_specs, check_vma=False)
```

time: 1950 us -> 756 us (0.39)
  waiting for transfers between devices: 1270 us -> 215 us
  matrix products: 404 us -> 67.5 us
  Pallas kernels: 0 us -> 230 us
  starting transfers between devices: 1.28 us -> 66 us
  blocking collectives: 49.1 us -> 0 us
  local copies, waits for them, and re-layouts: 103 us -> 64.6 us
    reduce_scatter x9 -> x0, waiting for transfers between devices: 769 us -> none  [the longest x1 143 us: on_device(): lax.psum_scatter(grad_w_head, ('pb', 'pa', 'ta'), scatter_dimension=0, ti...]
    dot_general x76 -> x18, matrix products: 404 us -> 67.5 us  [the longest x15 61.3 us: tn(): lax.dot_general(a, b, (((0,), (0,)), ((), ())), preferred_element_type=F32)]
    all_gather x9 -> x0, waiting for transfers between devices: 314 us -> none  [the longest x1 47 us: on_device(): lax.all_gather(w_qkv, ('pb', 'pa'), axis=1, tiled=True)]
    pallas_call x0 -> x41, Pallas kernels: none -> 230 us  [the longest x4 61.4 us: attend_back(): pl.pallas_call(functools.partial(attend_back_kernel, slots, tile_k, scale...]
    ppermute x0 -> x64, waiting for transfers between devices: none -> 215 us  [the longest x20 85.4 us: pz(): return lax.ppermute(v, 'pa', [(i, i ^ k) for i in range(n_pa)])]
    unnamed x22 -> x0, waiting for transfers between devices: 185 us -> none
    ppermute x0 -> x64, starting transfers between devices: none -> 66 us  [the longest x20 29.2 us: pz(): return lax.ppermute(v, 'pa', [(i, i ^ k) for i in range(n_pa)])]
    unnamed x1 -> x0, blocking collectives: 40.2 us -> none
  transfers between devices with their start and end apart: 20 -> 64, of which waited for: 19 -> 29; matrix products, arithmetic and copies ran while one was open for 13% -> 23% of each run, Pallas kernels for 0% -> 24%
where the time goes in v1:
time: 756 us; the launch traced here: 745 us
  Pallas kernels  230 us (30%)
  waiting for transfers between devices  215 us (28%)
  other arithmetic  98.8 us (13%)
  matrix products  67.5 us (9%)
  starting transfers between devices  66 us (9%)
  local copies, waits for them, and re-layouts  64.6 us (9%)
    ppermute x20, waiting for transfers between devices, pz(): return lax.ppermute(v, 'pa', [(i, i ^ k) for i in range(n_pa)])  85.4 us
    ppermute x19, waiting for transfers between devices, py(): return lax.ppermute(v, 'ta', [(i, i ^ 1) for i in range(n_ta)])  81.2 us
    pallas_call x4, Pallas kernels, attend_back(): pl.pallas_call(functools.partial(attend_back_kernel, slots, tile_k, scale...  61.4 us
    dot_general x15, matrix products, tn(): lax.dot_general(a, b, (((0,), (0,)), ((), ())), preferred_element_type=F32)  61.3 us
    pallas_call x6, Pallas kernels, mm_out(): pl.pallas_call(functools.partial(mm_out_kernel, chunk_of(m), half, len(ex...  57.9 us
    pallas_call x5, Pallas kernels, mm_in(): pl.pallas_call(functools.partial(mm_in_kernel, chunk_of(m), epilogue, sta...  56.9 us
    pallas_call x4, Pallas kernels, attend(): pl.pallas_call(functools.partial(attend_kernel, slots, tile_q, len(deps))...  43.9 us
    ppermute x14, waiting for transfers between devices, px(): return lax.ppermute(v, 'pb', [(i, i ^ cores * k) for i in range(n_pb)])  41.7 us
  transfers between devices with their start and end apart: 64, of which 29 were waited for; matrix products, arithmetic and copies ran while one was open for 23% of the time, Pallas kernels for 24%

profile of v1, /device:TPU:0, one launch (start us, length us, event | category | flops | bytes accessed | tf_op | source)
XLA Modules:
  0.0 745.3 jit_solution(17837761621858473427)
XLA Ops:
  9.8 6.8 collective-permute-done
  20.2 6.5 collective-permute-done.1
  33.3 12.4 %collective-permute-done.3 = bf16[1,64,2560]{2,1,0:T(8,128)(2,1)S(1)} collective-permute-done((bf16[1,64,2560]{2,1,0:T(8,128)(2,1)}, bf16[1,64,2560]{2,1,0:T(8,128)(2,1)S(1)}, u32[]{:S(2)}, u32[]{:S(2)}) %collective-permute-start.3) | collective-permute-done | bytes 327712 | tf_op jit(solution)/shard_map/ppermute | solution.py:439
  52.6 11.0 %collective-permute-done.7 = bf16[2,64,2560]{2,1,0:T(8,128)(2,1)S(1)} collective-permute-done((bf16[2,64,2560]{2,1,0:T(8,128)(2,1)}, bf16[2,64,2560]{2,1,0:T(8,128)(2,1)S(1)}, u32[]{:S(2)}, u32[]{:S(2)}) %collective-permute-start.7) | collective-permute-done | bytes 655392 | tf_op jit(solution)/shard_map/ppermute | solution.py:439
  89.3 10.4 %collective-permute-done.12 = bf16[1,64,2560]{2,1,0:T(8,128)(2,1)S(1)} collective-permute-done((bf16[1,64,2560]{2,1,0:T(8,128)(2,1)}, bf16[1,64,2560]{2,1,0:T(8,128)(2,1)S(1)}, u32[]{:S(2)}, u32[]{:S(2)}) %collective-permute-start.12) | collective-permute-done | bytes 327712 | tf_op jit(solution)/shard_map/ppermute | solution.py:439
  106.3 14.5 %shard_map.310.refs_1_.q_ref.k_ref.v_ref = bf16[1344,3072]{1,0:T(8,128)(2,1)} custom-call(bf16[1344,1024]{1,0:T(8,128)(2,1)} %shard_map.306.a_ref, bf16[1024,1536]{1,0:T(8,128)(2,1)} %shard_map.309.h_ref.h0_ref.h1_ref, bf16[1024,1536]{1,0:T(8,128)(2,1)} %copy-done.8, f32[8,3072]{1,0:T(8,128)} %maximum_maximum_fusion.5.rest_0_), custom_call_target="tpu_custom_call" | custom-call | flops 8455716864 | bytes 17301504 | tf_op jit(solution)/shard_map/pallas_call | solution.py:294
  123.8 10.9 %shard_map.315 = (bf16[704,1024]{1,0:T(8,128)(2,1)}, bf16[704,1024]{1,0:T(8,128)(2,1)}) custom-call(bf16[1344,3072]{1,0:T(8,128)(2,1)} %shard_map.310.refs_1_.q_ref.k_ref.v_ref, bf16[1344,3072]{1,0:T(8,128)(2,1)} %shard_map.310.refs_1_.q_ref.k_ref.v_ref, bf16[1344,3072]{1,0:T(8,128)(2,1)} %shard_map.310.refs_1_.q_ref.k_ref.v_ref, ...), custom_call_target="tpu_custom_call" | custom-call | flops 3875536896 | bytes 2457600 | tf_op jit(solution)/shard_map/pallas_call | solution.py:130
  134.7 10.9 %shard_map.316 = (bf16[704,1024]{1,0:T(8,128)(2,1)}, bf16[704,1024]{1,0:T(8,128)(2,1)}) custom-call(bf16[1344,3072]{1,0:T(8,128)(2,1)} %shard_map.310.refs_1_.q_ref.k_ref.v_ref, bf16[1344,3072]{1,0:T(8,128)(2,1)} %shard_map.310.refs_1_.q_ref.k_ref.v_ref, ...), custom_call_target="tpu_custom_call", output_to_operand_aliasing={{0}: (5, {}), {1}: (6, {})} | custom-call | flops 3875536896 | bytes 2457600 | tf_op jit(solution)/shard_map/pallas_call | solution.py:130
  148.0 11.1 %shard_map.318 = (bf16[704,1024]{1,0:T(8,128)(2,1)}, bf16[704,1024]{1,0:T(8,128)(2,1)}) custom-call(bf16[1344,3072]{1,0:T(8,128)(2,1)} %shard_map.310.refs_1_.q_ref.k_ref.v_ref, bf16[1344,3072]{1,0:T(8,128)(2,1)} %shard_map.310.refs_1_.q_ref.k_ref.v_ref, ...), custom_call_target="tpu_custom_call", output_to_operand_aliasing={{0}: (5, {}), {1}: (6, {})} | custom-call | flops 3875536896 | bytes 2457600 | tf_op jit(solution)/shard_map/pallas_call | solution.py:130
  169.9 10.9 %shard_map.319 = (bf16[704,1024]{1,0:T(8,128)(2,1)}, bf16[704,1024]{1,0:T(8,128)(2,1)}) custom-call(bf16[1344,3072]{1,0:T(8,128)(2,1)} %shard_map.310.refs_1_.q_ref.k_ref.v_ref, bf16[1344,3072]{1,0:T(8,128)(2,1)} %shard_map.310.refs_1_.q_ref.k_ref.v_ref, ...), custom_call_target="tpu_custom_call", output_to_operand_aliasing={{0}: (5, {}), {1}: (6, {})} | custom-call | flops 3875536896 | bytes 2457600 | tf_op jit(solution)/shard_map/pallas_call | solution.py:130
  197.7 16.3 %collective-permute-done.20 = bf16[1,256,2560]{2,1,0:T(8,128)(2,1)S(1)} collective-permute-done((bf16[1,256,2560]{2,1,0:T(8,128)(2,1)S(1)}, bf16[1,256,2560]{2,1,0:T(8,128)(2,1)S(1)}, u32[]{:S(2)}, u32[]{:S(2)}) %collective-permute-start.20) | collective-permute-done | bytes 1310752 | tf_op jit(solution)/shard_map/ppermute | solution.py:433
  214.3 7.4 collective-permute-done.21
  236.4 19.4 %shard_map.325 = (bf16[704,4096]{1,0:T(8,128)(2,1)}, bf16[704,4096]{1,0:T(8,128)(2,1)}) custom-call(bf16[704,1024]{1,0:T(8,128)(2,1)} %get-tuple-element.82.a_ref, bf16[1024,2560]{1,0:T(8,128)(2,1)} %shard_map.320.h0_ref.h1_ref.h_ref, bf16[1024,2560]{1,0:T(8,128)(2,1)} %collective-permute-done.16.r0_ref.r1_ref.r_ref, f32[8,4096]{1,0:T(8,128)} %concatenate.234.rest_0_), custom_call_target="tpu_custom_call" | custom-call | flops 5905580032 | bytes 21364736 | tf_op jit(solution)/shard_map/pallas_call | solution.py:294
  264.8 13.0 %shard_map.327 = f32[704,1024]{1,0:T(8,128)} custom-call(bf16[704,4096]{1,0:T(8,128)(2,1)} %get-tuple-element.43.refs_1_.a0_ref.a1_ref, bf16[704,4096]{1,0:T(8,128)(2,1)} %get-tuple-element.43.refs_1_.a0_ref.a1_ref, bf16[1024,2560]{1,0:T(8,128)(2,1)} %shard_map.326.h0_ref.h1_ref.h_ref, bf16[1024,2560]{1,0:T(8,128)(2,1)} %shard_map.326.h0_ref.h1_ref.h_ref, ...), custom_call_target="tpu_custom_call" | custom-call | flops 5905580032 | bytes 17039360 | tf_op jit(solution)/shard_map/pallas_call | solution.py:343
  294.9 7.7 %collective-permute-done.23 = bf16[1,64,1024]{2,1,0:T(8,128)(2,1)S(1)} collective-permute-done((bf16[1,64,1024]{2,1,0:T(8,128)(2,1)S(1)}, bf16[1,64,1024]{2,1,0:T(8,128)(2,1)S(1)}, u32[]{:S(2)}, u32[]{:S(2)}) %collective-permute-start.23) | collective-permute-done | bytes 131104 | tf_op jit(solution)/shard_map/ppermute | solution.py:439
  314.3 11.0 %collective-permute-done.25 = bf16[256,1024]{1,0:T(8,128)(2,1)} collective-permute-done((bf16[256,1024]{1,0:T(8,128)(2,1)S(1)}, bf16[256,1024]{1,0:T(8,128)(2,1)}, u32[]{:S(2)}, u32[]{:S(2)}) %collective-permute-start.25) | collective-permute-done | bytes 524320 | tf_op jit(solution)/shard_map/ppermute | solution.py:442
  339.0 9.6 %collective-permute-done.27 = bf16[256,1024]{1,0:T(8,128)(2,1)S(1)} collective-permute-done((bf16[256,1024]{1,0:T(8,128)(2,1)S(1)}, bf16[256,1024]{1,0:T(8,128)(2,1)S(1)}, u32[]{:S(2)}, u32[]{:S(2)}) %collective-permute-start.27) | collective-permute-done | bytes 524320 | tf_op jit(solution)/shard_map/ppermute | solution.py:442
  392.2 13.5 %shard_map.330 = (bf16[704,4096]{1,0:T(8,128)(2,1)}, f32[8,4096]{1,0:T(8,128)}) custom-call(bf16[704,1024]{1,0:T(8,128)(2,1)} %copy-done.32, bf16[1024,2560]{1,0:T(8,128)(2,1)} %shard_map.326.h0_ref.h1_ref.h_ref, bf16[1024,2560]{1,0:T(8,128)(2,1)} %collective-permute-done.22.r0_ref.r1_ref.r_ref, bf16[704,4096]{1,0:T(8,128)(2,1)} %get-tuple-element.44.rest_0_), custom_call_target="tpu_custom_call" | custom-call | flops 5905580032 | bytes 15663104 | tf_op jit(solution)/shard_map/pallas_call | solution.py:294
  405.7 7.7 %convolution_convert_fusion = bf16[512,4096]{1,0:T(8,128)(2,1)} fusion(bf16[704,4096]{1,0:T(8,128)(2,1)} %get-tuple-element.45.a0_ref.a1_ref, bf16[704,1024]{1,0:T(8,128)(2,1)S(1)} %copy-done.30), kind=kOutput, calls=%fused_computation.6 | convolution fusion | flops 2954887168 | bytes 10682368 | tf_op jit(solution)/shard_map/dot_general | solution.py:32
  422.5 7.0 add_convert_fusion.1
  434.3 12.8 %shard_map.331 = f32[704,1024]{1,0:T(8,128)} custom-call(bf16[704,4096]{1,0:T(8,128)(2,1)} %get-tuple-element.45.a0_ref.a1_ref, bf16[704,4096]{1,0:T(8,128)(2,1)} %get-tuple-element.45.a0_ref.a1_ref, bf16[1024,2560]{1,0:T(8,128)(2,1)} %shard_map.320.h0_ref.h1_ref.h_ref, bf16[1024,2560]{1,0:T(8,128)(2,1)} %shard_map.320.h0_ref.h1_ref.h_ref, ...), custom_call_target="tpu_custom_call" | custom-call | flops 5905580032 | bytes 17039360 | tf_op jit(solution)/shard_map/pallas_call | solution.py:343
  483.6 15.5 %shard_map.333 = (bf16[1344,3072]{1,0:T(8,128)(2,1)}, f32[8,1024]{1,0:T(8,128)}) custom-call(bf16[1344,3072]{1,0:T(8,128)(2,1)} %shard_map.310.refs_1_.q_ref.k_ref.v_ref, bf16[1344,3072]{1,0:T(8,128)(2,1)} %shard_map.310.refs_1_.q_ref.k_ref.v_ref, bf16[1344,3072]{1,0:T(8,128)(2,1)} %shard_map.310.refs_1_.q_ref.k_ref.v_ref, ...), custom_call_target="tpu_custom_call" | custom-call | flops 9688842240 | bytes 4915200 | tf_op jit(solution)/shard_map/pallas_call | solution.py:223
  499.2 23.1 %collective-permute-done.36 = bf16[128,2560]{1,0:T(8,128)(2,1)S(1)} collective-permute-done((bf16[128,2560]{1,0:T(8,128)(2,1)S(1)}, bf16[128,2560]{1,0:T(8,128)(2,1)S(1)}, u32[]{:S(2)}, u32[]{:S(2)}) %collective-permute-start.36) | collective-permute-done | bytes 655392 | tf_op jit(solution)/shard_map/ppermute | solution.py:442
  525.7 15.3 %shard_map.335 = (bf16[1344,3072]{1,0:T(8,128)(2,1)}, f32[8,1024]{1,0:T(8,128)}) custom-call(bf16[1344,3072]{1,0:T(8,128)(2,1)} %shard_map.310.refs_1_.q_ref.k_ref.v_ref, bf16[1344,3072]{1,0:T(8,128)(2,1)} %shard_map.310.refs_1_.q_ref.k_ref.v_ref, ...), custom_call_target="tpu_custom_call", output_to_operand_aliasing={{0}: (7, {}), {1}: (8, {})} | custom-call | flops 9688842240 | bytes 4915200 | tf_op jit(solution)/shard_map/pallas_call | solution.py:223
  561.4 11.2 %collective-permute-done.62 = bf16[1,64,2560]{2,1,0:T(8,128)(2,1)S(1)} collective-permute-done((bf16[1,64,2560]{2,1,0:T(8,128)(2,1)S(1)}, bf16[1,64,2560]{2,1,0:T(8,128)(2,1)S(1)}, u32[]{:S(2)}, u32[]{:S(2)}) %collective-permute-start.62) | collective-permute-done | bytes 327712 | tf_op jit(solution)/shard_map/ppermute | solution.py:439
  584.8 15.3 %shard_map.339 = (bf16[1344,3072]{1,0:T(8,128)(2,1)}, f32[8,1024]{1,0:T(8,128)}) custom-call(bf16[1344,3072]{1,0:T(8,128)(2,1)} %shard_map.310.refs_1_.q_ref.k_ref.v_ref, bf16[1344,3072]{1,0:T(8,128)(2,1)} %shard_map.310.refs_1_.q_ref.k_ref.v_ref, ...), custom_call_target="tpu_custom_call", output_to_operand_aliasing={{0}: (7, {}), {1}: (8, {})} | custom-call | flops 9688842240 | bytes 4915200 | tf_op jit(solution)/shard_map/pallas_call | solution.py:223
  612.4 12.6 %collective-permute-done.44.refs_0_ = bf16[256,1536]{1,0:T(8,128)(2,1)} collective-permute-done((bf16[256,1536]{1,0:T(8,128)(2,1)}, bf16[256,1536]{1,0:T(8,128)(2,1)}, u32[]{:S(2)}, u32[]{:S(2)}) %collective-permute-start.44) | collective-permute-done | bytes 786464 | tf_op jit(solution)/shard_map/ppermute | solution.py:433
  627.3 15.3 %shard_map.342 = (bf16[1344,3072]{1,0:T(8,128)(2,1)}, f32[8,1024]{1,0:T(8,128)}) custom-call(bf16[1344,3072]{1,0:T(8,128)(2,1)} %shard_map.310.refs_1_.q_ref.k_ref.v_ref, bf16[1344,3072]{1,0:T(8,128)(2,1)} %shard_map.310.refs_1_.q_ref.k_ref.v_ref, ...), custom_call_target="tpu_custom_call", output_to_operand_aliasing={{0}: (7, {}), {1}: (8, {})} | custom-call | flops 9688842240 | bytes 4915200 | tf_op jit(solution)/shard_map/pallas_call | solution.py:223
  657.2 12.5 %collective-permute-done.57 = f32[4,416]{1,0:T(4,128)S(1)} collective-permute-done((f32[4,416]{1,0:T(4,128)S(1)}, f32[4,416]{1,0:T(4,128)S(1)}, u32[]{:S(2)}, u32[]{:S(2)}) %collective-permute-start.57) | collective-permute-done | bytes 6688 | tf_op jit(solution)/shard_map/ppermute | solution.py:442
  671.0 10.8 %shard_map.343 = f32[704,1024]{1,0:T(8,128)} custom-call(bf16[1344,3072]{1,0:T(8,128)(2,1)} %get-tuple-element.53.a0_ref.a1_ref, bf16[1344,3072]{1,0:T(8,128)(2,1)} %get-tuple-element.53.a0_ref.a1_ref, bf16[1024,1536]{1,0:T(8,128)(2,1)} %shard_map.309.h_ref.h0_ref.h1_ref, bf16[1024,1536]{1,0:T(8,128)(2,1)} %shard_map.309.h_ref.h0_ref.h1_ref, ...), custom_call_target="tpu_custom_call" | custom-call | flops 4429185024 | bytes 13500416 | tf_op jit(solution)/shard_map/pallas_call | solution.py:343
  688.4 9.3 %shard_map.344 = bf16[640,1024]{1,0:T(8,128)(2,1)} custom-call(bf16[640,3072]{1,0:T(8,128)(2,1)} %slice.675.a0_ref.a1_ref, bf16[640,3072]{1,0:T(8,128)(2,1)} %slice.675.a0_ref.a1_ref, bf16[1024,1536]{1,0:T(8,128)(2,1)} %shard_map.309.h_ref.h0_ref.h1_ref, bf16[1024,1536]{1,0:T(8,128)(2,1)} %shard_map.309.h_ref.h0_ref.h1_ref, bf16[1024,1536]{1,0:T(8,128)(2,1)} %copy-done.8, ...), custom_call_target="tpu_custom_call" | custom-call | flops 4026531840 | bytes 12845056 | tf_op jit(solution)/shard_map/pallas_call | solution.py:343
  717.9 8.9 %collective-permute-done.46 = bf16[640,1024]{1,0:T(8,128)(2,1)} collective-permute-done((bf16[640,1024]{1,0:T(8,128)(2,1)}, bf16[640,1024]{1,0:T(8,128)(2,1)}, u32[]{:S(2)}, u32[]{:S(2)}) %collective-permute-start.46) | collective-permute-done | bytes 1310752 | tf_op jit(solution)/shard_map/ppermute | solution.py:442
  (649 shorter events, 361.4 us)
Async XLA Ops:
  0.7 81.1 %collective-permute-start.9 = (f32[2,512]{1,0:T(2,128)}, f32[2,512]{1,0:T(2,128)S(1)}, u32[]{:S(2)}, u32[]{:S(2)}) collective-permute-start(f32[2,512]{1,0:T(2,128)} %param.21), channel_id=1, source_target_pairs={{0,1},{1,0},{2,3},{3,2},{4,5},{5,4},{6,7},{7,6},{8,9},{9,8},{10,11... | collective-permute-start | bytes 12296 | tf_op jit(solution)/shard_map/ppermute | solution.py:442
  48.4 19.2 %collective-permute-start.5 = (bf16[1,256,1536]{2,1,0:T(8,128)(2,1)S(1)}, bf16[1,256,1536]{2,1,0:T(8,128)(2,1)S(1)}, u32[]{:S(2)}, u32[]{:S(2)}) collective-permute-start(bf16[1,256,1536]{2,1,0:T(8,128)(2,1)S(1)} %maximum_bitcast_fusion.2), channel_id=1, source_target_pairs={{0,16},{8,24},{16,0},{24,8},{1,17},{9,25},{17,1},{25,9},{2,18},{10... | collective-permute-start | bytes 2359304 | tf_op jit(solution)/shard_map/ppermute | solution.py:433
  52.0 19.1 %collective-permute-start.6 = (bf16[2,128,1536]{2,1,0:T(8,128)(2,1)}, bf16[2,128,1536]{2,1,0:T(8,128)(2,1)S(1)}, u32[]{:S(2)}, u32[]{:S(2)}) collective-permute-start(bf16[2,128,1536]{2,1,0:T(8,128)(2,1)} %shard_map.308), channel_id=1, source_target_pairs={{0,1},{1,0},{2,3},{3,2},{4,5},{5,4},{6,7},{7,6},{8,9},{9,8},{10,11... | collective-permute-start | bytes 2359304 | tf_op jit(solution)/shard_map/ppermute | solution.py:442
  73.1 31.6 %collective-permute-start.8 = (bf16[1024,1536]{1,0:T(8,128)(2,1)}, bf16[1024,1536]{1,0:T(8,128)(2,1)S(1)}, u32[]{:S(2)}, u32[]{:S(2)}) collective-permute-start(bf16[1024,1536]{1,0:T(8,128)(2,1)} %shard_map.309.h_ref.h0_ref.h1_ref), channel_id=1, source_target_pairs={{0,8},{8,0},{16,24},{24,16},{1,9},{9,1},{17,25},{25,17},{2,10},{10... | collective-permute-start | bytes 9437192 | tf_op jit(solution)/shard_map/ppermute | solution.py:436
  88.8 32.1 %collective-permute-start.10 = (bf16[128,2560]{1,0:T(8,128)(2,1)}, bf16[128,2560]{1,0:T(8,128)(2,1)}, u32[]{:S(2)}, u32[]{:S(2)}) collective-permute-start(bf16[128,2560]{1,0:T(8,128)(2,1)} %bitcast.42), channel_id=1, source_target_pairs={{0,1},{1,0},{2,3},{3,2},{4,5},{5,4},{6,7},{7,6},{8,9},{9,8},{10,11... | collective-permute-start | bytes 1966088 | tf_op jit(solution)/shard_map/ppermute | solution.py:442
  122.4 23.3 %collective-permute-start.13 = (bf16[2,64,2560]{2,1,0:T(8,128)(2,1)}, bf16[2,64,2560]{2,1,0:T(8,128)(2,1)S(1)}, u32[]{:S(2)}, u32[]{:S(2)}) collective-permute-start(bf16[2,64,2560]{2,1,0:T(8,128)(2,1)} %shard_map.314.rest_2_), channel_id=1, source_target_pairs={{0,2},{2,0},{4,6},{6,4},{1,3},{3,1},{5,7},{7,5},{8,10},{10,8},{12,... | collective-permute-start | bytes 1966088 | tf_op jit(solution)/shard_map/ppermute | solution.py:439
  122.7 36.5 %collective-permute-start.14 = (bf16[1,256,2560]{2,1,0:T(8,128)(2,1)S(1)}, bf16[1,256,2560]{2,1,0:T(8,128)(2,1)}, u32[]{:S(2)}, u32[]{:S(2)}) collective-permute-start(bf16[1,256,2560]{2,1,0:T(8,128)(2,1)S(1)} %maximum_bitcast_fusion), channel_id=1, source_target_pairs={{0,16},{8,24},{16,0},{24,8},{1,17},{9,25},{17,1},{25,9},{2,18},{10... | collective-permute-start | bytes 3932168 | tf_op jit(solution)/shard_map/ppermute | solution.py:433
  123.3 37.6 %collective-permute-start.15 = (bf16[2,128,2560]{2,1,0:T(8,128)(2,1)S(1)}, bf16[2,128,2560]{2,1,0:T(8,128)(2,1)}, u32[]{:S(2)}, u32[]{:S(2)}) collective-permute-start(bf16[2,128,2560]{2,1,0:T(8,128)(2,1)S(1)} %copy-done.14), channel_id=1, source_target_pairs={{0,1},{1,0},{2,3},{3,2},{4,5},{5,4},{6,7},{7,6},{8,9},{9,8},{10,11... | collective-permute-start | bytes 3932168 | tf_op jit(solution)/shard_map/ppermute | solution.py:442
  165.4 59.1 %collective-permute-start.16 = (bf16[1024,2560]{1,0:T(8,128)(2,1)}, bf16[1024,2560]{1,0:T(8,128)(2,1)}, u32[]{:S(2)}, u32[]{:S(2)}) collective-permute-start(bf16[1024,2560]{1,0:T(8,128)(2,1)} %shard_map.320.h0_ref.h1_ref.h_ref), channel_id=1, source_target_pairs={{0,8},{8,0},{16,24},{24,16},{1,9},{9,1},{17,25},{25,17},{2,10},{10... | collective-permute-start | bytes 15728648 | tf_op jit(solution)/shard_map/ppermute | solution.py:436
  168.4 22.3 %collective-permute-start.17 = (bf16[1,128,2560]{2,1,0:T(8,128)(2,1)S(1)}, bf16[1,128,2560]{2,1,0:T(8,128)(2,1)}, u32[]{:S(2)}, u32[]{:S(2)}) collective-permute-start(bf16[1,128,2560]{2,1,0:T(8,128)(2,1)S(1)} %get-tuple-element.105), channel_id=1, source_target_pairs={{0,16},{8,24},{16,0},{24,8},{1,17},{9,25},{17,1},{25,9},{2,18},{10... | collective-permute-start | bytes 1966088 | tf_op jit(solution)/shard_map/ppermute | solution.py:433
  184.9 29.1 %collective-permute-start.20 = (bf16[1,256,2560]{2,1,0:T(8,128)(2,1)S(1)}, bf16[1,256,2560]{2,1,0:T(8,128)(2,1)S(1)}, u32[]{:S(2)}, u32[]{:S(2)}) collective-permute-start(bf16[1,256,2560]{2,1,0:T(8,128)(2,1)S(1)} %maximum_bitcast_fusion.1), channel_id=1, source_target_pairs={{0,16},{8,24},{16,0},{24,8},{1,17},{9,25},{17,1},{25,9},{2,18},{10... | collective-permute-start | bytes 3932168 | tf_op jit(solution)/shard_map/ppermute | solution.py:433
  193.0 28.7 %collective-permute-start.21 = (bf16[2,128,2560]{2,1,0:T(8,128)(2,1)}, bf16[2,128,2560]{2,1,0:T(8,128)(2,1)S(1)}, u32[]{:S(2)}, u32[]{:S(2)}) collective-permute-start(bf16[2,128,2560]{2,1,0:T(8,128)(2,1)} %shard_map.322.rest_2_), channel_id=1, source_target_pairs={{0,1},{1,0},{2,3},{3,2},{4,5},{5,4},{6,7},{7,6},{8,9},{9,8},{10,11... | collective-permute-start | bytes 3932168 | tf_op jit(solution)/shard_map/ppermute | solution.py:442
  385.2 37.3 %collective-permute-start.30 = (bf16[512,4096]{1,0:T(8,128)(2,1)}, bf16[512,4096]{1,0:T(8,128)(2,1)}, u32[]{:S(2)}, u32[]{:S(2)}) collective-permute-start(bf16[512,4096]{1,0:T(8,128)(2,1)} %convolution_convert_fusion.1), channel_id=1, source_target_pairs={{0,8},{8,0},{16,24},{24,16},{1,9},{9,1},{17,25},{25,17},{2,10},{10... | collective-permute-start | bytes 12582920 | tf_op jit(solution)/shard_map/ppermute | solution.py:436
  391.7 27.0 %collective-permute-start.31 = (bf16[512,1024]{1,0:T(8,128)(2,1)}, bf16[512,1024]{1,0:T(8,128)(2,1)}, u32[]{:S(2)}, u32[]{:S(2)}) collective-permute-start(bf16[512,1024]{1,0:T(8,128)(2,1)} %convolution_convert_fusion.3), channel_id=1, source_target_pairs={{0,8},{8,0},{16,24},{24,16},{1,9},{9,1},{17,25},{25,17},{2,10},{10... | collective-permute-start | bytes 3145736 | tf_op jit(solution)/shard_map/ppermute | solution.py:436
  416.5 40.4 %collective-permute-start.32 = (bf16[512,4096]{1,0:T(8,128)(2,1)}, bf16[512,4096]{1,0:T(8,128)(2,1)S(1)}, u32[]{:S(2)}, u32[]{:S(2)}) collective-permute-start(bf16[512,4096]{1,0:T(8,128)(2,1)} %convolution_convert_fusion), channel_id=1, source_target_pairs={{0,8},{8,0},{16,24},{24,16},{1,9},{9,1},{17,25},{25,17},{2,10},{10... | collective-permute-start | bytes 12582920 | tf_op jit(solution)/shard_map/ppermute | solution.py:436
  432.1 46.5 %collective-permute-start.34 = (bf16[128,5120]{1,0:T(8,128)(2,1)}, bf16[128,5120]{1,0:T(8,128)(2,1)}, u32[]{:S(2)}, u32[]{:S(2)}) collective-permute-start(bf16[128,5120]{1,0:T(8,128)(2,1)} %pad_maximum_fusion.11.rest_1_), channel_id=1, source_target_pairs={{0,16},{8,24},{16,0},{24,8},{1,17},{9,25},{17,1},{25,9},{2,18},{10... | collective-permute-start | bytes 3932168 | tf_op jit(solution)/shard_map/ppermute | solution.py:433
  433.8 47.2 %collective-permute-start.35 = (bf16[256,2560]{1,0:T(8,128)(2,1)}, bf16[256,2560]{1,0:T(8,128)(2,1)}, u32[]{:S(2)}, u32[]{:S(2)}) collective-permute-start(bf16[256,2560]{1,0:T(8,128)(2,1)} %maximum_maximum_fusion.rest_2_), channel_id=1, source_target_pairs={{0,1},{1,0},{2,3},{3,2},{4,5},{5,4},{6,7},{7,6},{8,9},{9,8},{10,11... | collective-permute-start | bytes 3932168 | tf_op jit(solution)/shard_map/ppermute | solution.py:442
  474.4 72.7 %collective-permute-start.38 = (bf16[128,5120]{1,0:T(8,128)(2,1)}, bf16[128,5120]{1,0:T(8,128)(2,1)}, u32[]{:S(2)}, u32[]{:S(2)}) collective-permute-start(bf16[128,5120]{1,0:T(8,128)(2,1)} %pad_maximum_fusion.12.rest_0_), channel_id=1, source_target_pairs={{0,16},{8,24},{16,0},{24,8},{1,17},{9,25},{17,1},{25,9},{2,18},{10... | collective-permute-start | bytes 3932168 | tf_op jit(solution)/shard_map/ppermute | solution.py:433
  477.1 70.0 %collective-permute-start.39 = (bf16[256,2560]{1,0:T(8,128)(2,1)}, bf16[256,2560]{1,0:T(8,128)(2,1)}, u32[]{:S(2)}, u32[]{:S(2)}) collective-permute-start(bf16[256,2560]{1,0:T(8,128)(2,1)} %maximum_maximum_fusion.1.rest_1_), channel_id=1, source_target_pairs={{0,1},{1,0},{2,3},{3,2},{4,5},{5,4},{6,7},{7,6},{8,9},{9,8},{10,11... | collective-permute-start | bytes 3932168 | tf_op jit(solution)/shard_map/ppermute | solution.py:442
  480.4 41.8 %collective-permute-start.36 = (bf16[128,2560]{1,0:T(8,128)(2,1)S(1)}, bf16[128,2560]{1,0:T(8,128)(2,1)S(1)}, u32[]{:S(2)}, u32[]{:S(2)}) collective-permute-start(bf16[128,2560]{1,0:T(8,128)(2,1)S(1)} %slice.822.rest_2_), channel_id=1, source_target_pairs={{0,1},{1,0},{2,3},{3,2},{4,5},{5,4},{6,7},{7,6},{8,9},{9,8},{10,11... | collective-permute-start | bytes 1966088 | tf_op jit(solution)/shard_map/ppermute | solution.py:442
  482.7 39.6 %collective-permute-start.37 = (bf16[128,2560]{1,0:T(8,128)(2,1)S(1)}, bf16[128,2560]{1,0:T(8,128)(2,1)S(1)}, u32[]{:S(2)}, u32[]{:S(2)}) collective-permute-start(bf16[128,2560]{1,0:T(8,128)(2,1)S(1)} %slice.827.rest_3_), channel_id=1, source_target_pairs={{0,16},{8,24},{16,0},{24,8},{1,17},{9,25},{17,1},{25,9},{2,18},{10... | collective-permute-start | bytes 1966088 | tf_op jit(solution)/shard_map/ppermute | solution.py:433
  524.9 26.2 %collective-permute-start.40 = (bf16[2,64,2560]{2,1,0:T(8,128)(2,1)S(1)}, bf16[2,64,2560]{2,1,0:T(8,128)(2,1)}, u32[]{:S(2)}, u32[]{:S(2)}) collective-permute-start(bf16[2,64,2560]{2,1,0:T(8,128)(2,1)S(1)} %slice_bitcast_fusion.3.rest_2_), channel_id=1, source_target_pairs={{0,2},{2,0},{4,6},{6,4},{1,3},{3,1},{5,7},{7,5},{8,10},{10,8},{12,... | collective-permute-start | bytes 1966088 | tf_op jit(solution)/shard_map/ppermute | solution.py:439
  547.1 31.5 %collective-permute-start.41 = (bf16[512,1536]{1,0:T(8,128)(2,1)}, bf16[512,1536]{1,0:T(8,128)(2,1)}, u32[]{:S(2)}, u32[]{:S(2)}) collective-permute-start(bf16[512,1536]{1,0:T(8,128)(2,1)} %fusion.13), channel_id=1, source_target_pairs={{0,8},{8,0},{16,24},{24,16},{1,9},{9,1},{17,25},{25,17},{2,10},{10... | collective-permute-start | bytes 4718600 | tf_op jit(solution)/shard_map/ppermute | solution.py:436
  572.7 31.3 %collective-permute-start.63 = (f32[32,512]{1,0:T(8,128)S(1)}, f32[32,512]{1,0:T(8,128)S(1)}, u32[]{:S(2)}, u32[]{:S(2)}) collective-permute-start(f32[32,512]{1,0:T(8,128)S(1)} %get-tuple-element.131), channel_id=1, source_target_pairs={{0,1},{1,0},{2,3},{3,2},{4,5},{5,4},{6,7},{7,6},{8,9},{9,8},{10,11... | collective-permute-start | bytes 196616 | tf_op jit(solution)/shard_map/ppermute | solution.py:442
  604.7 20.3 %collective-permute-start.44 = (bf16[256,1536]{1,0:T(8,128)(2,1)}, bf16[256,1536]{1,0:T(8,128)(2,1)}, u32[]{:S(2)}, u32[]{:S(2)}) collective-permute-start(bf16[256,1536]{1,0:T(8,128)(2,1)} %slice.844.rest_5_), channel_id=1, source_target_pairs={{0,16},{8,24},{16,0},{24,8},{1,17},{9,25},{17,1},{25,9},{2,18},{10... | collective-permute-start | bytes 2359304 | tf_op jit(solution)/shard_map/ppermute | solution.py:433
  607.3 39.0 %collective-permute-start.60 = (bf16[2,64,2560]{2,1,0:T(8,128)(2,1)S(1)}, bf16[2,64,2560]{2,1,0:T(8,128)(2,1)}, u32[]{:S(2)}, u32[]{:S(2)}) collective-permute-start(bf16[2,64,2560]{2,1,0:T(8,128)(2,1)S(1)} %slice_bitcast_fusion.1.rest_2_), channel_id=1, source_target_pairs={{0,2},{2,0},{4,6},{6,4},{1,3},{3,1},{5,7},{7,5},{8,10},{10,8},{12,... | collective-permute-start | bytes 1966088 | tf_op jit(solution)/shard_map/ppermute | solution.py:439
  649.4 56.9 %collective-permute-start.61 = (bf16[1,64,2560]{2,1,0:T(8,128)(2,1)S(1)}, bf16[1,64,2560]{2,1,0:T(8,128)(2,1)S(1)}, u32[]{:S(2)}, u32[]{:S(2)}) collective-permute-start(bf16[1,64,2560]{2,1,0:T(8,128)(2,1)S(1)} %slice_bitcast_fusion.8), channel_id=1, source_target_pairs={{0,4},{2,6},{4,0},{6,2},{1,5},{3,7},{5,1},{7,3},{8,12},{10,14},{12... | collective-permute-start | bytes 983048 | tf_op jit(solution)/shard_map/ppermute | solution.py:439
  649.8 58.1 %collective-permute-start.47 = (bf16[256,768]{1,0:T(8,128)(2,1)}, bf16[256,768]{1,0:T(8,128)(2,1)S(1)}, u32[]{:S(2)}, u32[]{:S(2)}) collective-permute-start(bf16[256,768]{1,0:T(8,128)(2,1)} %slice.849.rest_4_), channel_id=1, source_target_pairs={{0,16},{8,24},{16,0},{24,8},{1,17},{9,25},{17,1},{25,9},{2,18},{10... | collective-permute-start | bytes 1179656 | tf_op jit(solution)/shard_map/ppermute | solution.py:433
  650.3 57.5 %collective-permute-start.48 = (bf16[256,1536]{1,0:T(8,128)(2,1)}, bf16[256,1536]{1,0:T(8,128)(2,1)}, u32[]{:S(2)}, u32[]{:S(2)}) collective-permute-start(bf16[256,1536]{1,0:T(8,128)(2,1)} %add_convert_fusion.11.rest_3_), channel_id=1, source_target_pairs={{0,1},{1,0},{2,3},{3,2},{4,5},{5,4},{6,7},{7,6},{8,9},{9,8},{10,11... | collective-permute-start | bytes 2359304 | tf_op jit(solution)/shard_map/ppermute | solution.py:442
  657.2 43.7 %collective-permute-start.51 = (bf16[512,768]{1,0:T(8,128)(2,1)}, bf16[512,768]{1,0:T(8,128)(2,1)S(1)}, u32[]{:S(2)}, u32[]{:S(2)}) collective-permute-start(bf16[512,768]{1,0:T(8,128)(2,1)} %fusion.41), channel_id=1, source_target_pairs={{0,8},{8,0},{16,24},{24,16},{1,9},{9,1},{17,25},{25,17},{2,10},{10... | collective-permute-start | bytes 2359304 | tf_op jit(solution)/shard_map/ppermute | solution.py:436
  697.6 29.2 %collective-permute-start.46 = (bf16[640,1024]{1,0:T(8,128)(2,1)}, bf16[640,1024]{1,0:T(8,128)(2,1)}, u32[]{:S(2)}, u32[]{:S(2)}) collective-permute-start(bf16[640,1024]{1,0:T(8,128)(2,1)} %shard_map.344), channel_id=1, source_target_pairs={{0,1},{1,0},{2,3},{3,2},{4,5},{5,4},{6,7},{7,6},{8,9},{9,8},{10,11... | collective-permute-start | bytes 3932168 | tf_op jit(solution)/shard_map/ppermute | solution.py:442
  715.8 18.6 %collective-permute-start.49 = (bf16[2,64,768]{2,1,0:T(8,128)(2,1)S(1)}, bf16[2,64,768]{2,1,0:T(8,128)(2,1)S(1)}, u32[]{:S(2)}, u32[]{:S(2)}) collective-permute-start(bf16[2,64,768]{2,1,0:T(8,128)(2,1)S(1)} %slice_bitcast_fusion.14), channel_id=1, source_target_pairs={{0,2},{2,0},{4,6},{6,4},{1,3},{3,1},{5,7},{7,5},{8,10},{10,8},{12,... | collective-permute-start | bytes 589832 | tf_op jit(solution)/shard_map/ppermute | solution.py:439
  (151 other events, 1460.1 us)

commit v2 on v1

--- a/solution.py
+++ b/solution.py
@@ -32,7 +32,8 @@
     return lax.dot_general(a, b, (((0,), (0,)), ((), ())), preferred_element_type=F32)
 
 
-def permute_kernel(segments, block, low_bits, info, x_ref, o_ref):
+def permute_kernel(segments, block, low_bits, skip, info, x_ref, *rest):
+    o_ref = rest[-1]
     tiles = x_ref.shape[1] // LANES
     lane = lax.broadcasted_iota(jnp.int32, (1, LANES), 1)
     low = info[tiles]
@@ -42,6 +43,9 @@
         for i, length in enumerate(segments):
             start = pl.multiple_of(info[tiles + 1 + i], 16)
             part = x_ref[pl.ds(start, length), pl.ds(source, LANES)]
+            if skip is not None:
+                more = rest[0][:, pl.ds(source, LANES)].astype(F32)
+                part = jnp.concatenate([part[:skip], part[skip:] + more], axis=0)
             if low_bits:
                 part = part.astype(F32)
                 for bit in range(low_bits):
@@ -55,21 +59,22 @@
             row += length
 
 
-def permute(x, info, segments, block, low_bits):
+def permute(x, info, segments, block, low_bits, skip=None, more=()):
     rows = sum(segments)
     return pl.pallas_call(
-        functools.partial(permute_kernel, segments, block, low_bits),
+        functools.partial(permute_kernel, segments, block, low_bits, skip),
         out_shape=jax.ShapeDtypeStruct((rows, x.shape[1]), x.dtype),
         in_specs=[
             pl.BlockSpec(memory_space=pltpu.SMEM),
             pl.BlockSpec(memory_space=pltpu.VMEM),
-        ],
+        ]
+        + [pl.BlockSpec(memory_space=pltpu.VMEM)] * len(more),
         out_specs=pl.BlockSpec(memory_space=pltpu.VMEM),
         compiler_params=pltpu.CompilerParams(vmem_limit_bytes=56 * MIB),
         cost_estimate=pl.CostEstimate(
             flops=rows * x.shape[1], bytes_accessed=4 * rows * x.shape[1], transcendentals=0
         ),
-    )(info, x)
+    )(info, x, *more)
 
 
 def pick(sel, a, b):
@@ -261,6 +266,57 @@
     )(x, *deps)
 
 
+def assemble_kernel(n_in, n_deps, n_out, copies, *refs):
+    ins, outs, sem = refs[:n_in], refs[n_in + n_deps : n_in + n_deps + n_out], refs[-1]
+    started = []
+    for i, (source, at, target, to) in enumerate(copies):
+        src = ins[source].at[at] if at else ins[source]
+        dst = outs[target].at[to] if to else outs[target]
+        started.append(pltpu.make_async_copy(src, dst, sem.at[i]))
+    for c in started:
+        c.start()
+    for c in started:
+        c.wait()
+
+
+def assemble(arrays, shapes, copies, deps=()):
+    anywhere = pl.BlockSpec(memory_space=pl.ANY)
+    vmem = pl.BlockSpec(memory_space=pltpu.VMEM)
+    size = sum(math.prod(s) for s in shapes)
+    return pl.pallas_call(
+        functools.partial(assemble_kernel, len(arrays), len(deps), len(shapes), copies),
+        out_shape=tuple(jax.ShapeDtypeStruct(s, arrays[0].dtype) for s in shapes),
+        in_specs=[anywhere] * (len(arrays) + len(deps)),
+        out_specs=tuple(vmem for _ in shapes),
+        scratch_shapes=[pltpu.SemaphoreType.DMA((len(copies),))],
+        compiler_params=pltpu.CompilerParams(vmem_limit_bytes=56 * MIB),
+        cost_estimate=pl.CostEstimate(flops=0, bytes_accessed=4 * size, transcendentals=0),
+    )(*arrays, *deps)
+
+
+def sums_kernel(n_in, n_deps, n_out, pieces, *refs):
+    ins, outs = refs[:n_in], refs[n_in + n_deps : n_in + n_deps + n_out]
+    for target, to, terms in pieces:
+        total = ins[terms[0][0]][terms[0][1]].astype(F32)
+        for source, at in terms[1:]:
+            total = total + ins[source][at].astype(F32)
+        outs[target][to] = total.astype(outs[target].dtype)
+
+
+def sums(arrays, outs, pieces, deps=()):
+    anywhere = pl.BlockSpec(memory_space=pl.ANY)
+    vmem = pl.BlockSpec(memory_space=pltpu.VMEM)
+    size = sum(a.size for a in arrays)
+    return pl.pallas_call(
+        functools.partial(sums_kernel, len(arrays), len(deps), len(outs), pieces),
+        out_shape=tuple(jax.ShapeDtypeStruct(s, dt) for s, dt in outs),
+        in_specs=[vmem] * len(arrays) + [anywhere] * len(deps),
+        out_specs=tuple(vmem for _ in outs),
+        compiler_params=pltpu.CompilerParams(vmem_limit_bytes=56 * MIB),
+        cost_estimate=pl.CostEstimate(flops=size, bytes_accessed=4 * size, transcendentals=0),
+    )(*arrays, *deps)
+
+
 def chunk_of(m):
     return m if m <= 704 else m // 2
 
@@ -332,14 +388,16 @@
         run(r0_ref, r1_ref)
 
 
-def mm_out(a, m, h, r, col, width, td, epilogue, extra, dtype, deps=()):
+def mm_out(a, m, h, r, col, width, td, epilogue, extra, dtype, deps=(), row=0):
     k = h.shape[0] // 2
     half = k // td
     at = col // width
     lhs = lambda t: pl.BlockSpec((m, width), lambda i: (0, t))
+    if row:
+        lhs = lambda t: pl.BlockSpec((pl.Element(m), pl.Element(width)), lambda i: (row, t * width))
     own = lambda t: pl.BlockSpec((td, width), lambda i: (t * half + jnp.minimum(i, half - 1), at))
     oth = lambda t: pl.BlockSpec((td, width), lambda i: (t * half + jnp.maximum(i - half, 0), at))
-    wide = lambda n: pl.BlockSpec((n, td), lambda i: (0, i))
+    wide = lambda n: pl.BlockSpec((min(n, m), td), lambda i: (0, i))
     return pl.pallas_call(
         functools.partial(mm_out_kernel, chunk_of(m), half, len(extra), epilogue),
         grid=(2 * half,),
@@ -375,9 +433,9 @@
 
 def put_gelu(acc, rows, extra, outs, carry):
     inner = acc + extra[0][pl.ds(0, 1), :]
-    cdf, pdf = normal_parts(inner)
-    outs[0][rows, :] = (inner * cdf).astype(BF)
-    outs[1][rows, :] = (cdf + inner * pdf).astype(BF)
+    out, slope = gelu_parts(inner)
+    outs[0][rows, :] = out.astype(BF)
+    outs[1][rows, :] = slope.astype(BF)
     return carry
 
 
@@ -399,13 +457,15 @@
     return jnp.concatenate([jnp.stack(rows), jnp.zeros((8 - len(rows), rows[0].shape[0]), F32)])
 
 
-def normal_parts(v):
-    t = 1.0 / (1.0 + (0.3275911 * math.sqrt(0.5)) * jnp.abs(v))
-    bell = jnp.exp(-0.5 * v * v)
-    poly = 0.5 * 1.061405429 * t - 0.5 * 1.453152027
+def gelu_parts(v):
+    size = jnp.abs(v)
+    t = 1.0 / ((0.3275911 * math.sqrt(0.5)) * size + 1.0)
+    bell = jnp.exp(-0.5 * (v * v))
+    poly = (0.5 * 1.061405429) * t - 0.5 * 1.453152027
     poly = (poly * t + 0.5 * 1.421413741) * t - 0.5 * 0.284496736
-    tail = ((poly * t + 0.5 * 0.254829592) * t) * bell
-    return jnp.where(v < 0.0, tail, 1.0 - tail), bell * (1.0 / math.sqrt(2.0 * math.pi))
+    poly = (poly * t + 0.5 * 0.254829592) * t
+    low = bell * (poly - size * (1.0 / math.sqrt(2.0 * math.pi)))
+    return jnp.maximum(v, 0.0) - size * (poly * bell), jnp.where(v < 0.0, low, 1.0 - low)
 
 
 def norm_parts(v):
@@ -444,39 +504,83 @@
     x_bits = n_x.bit_length() - 1
     z_bits = n_pa.bit_length() - 1
 
-    def gather_z_step(have, bit):
-        other = pz(have, 1 << bit)
-        return jnp.stack([have, other], axis=1).reshape((-1,) + have.shape[1:])
-
-    def gather_z_rest(have):
-        for bit in reversed(range(z_bits - 1)):
-            have = gather_z_step(have, bit)
+    def after(v, *deps):
+        return tie(v, *deps) if deps else v
+
+    every = slice(None)
+
+    def z_go(have, bit):
+        return pz(have, 1 << bit)
+
+    def z_end(have, other, deps=()):
+        n, w, cols = have.shape
+        (out,) = assemble(
+            (have, other), ((n, 2, w, cols),), ((0, (), 0, (every, 0)), (1, (), 0, (every, 1))), deps
+        )
+        return out.reshape(2 * n, w, cols)
+
+    def z_last(have, other, deps=()):
+        n, w, cols = have.shape
+        h = n // 2
+        near, far = assemble(
+            (have, other), ((h, 2, w, cols), (h, 2, w, cols)),
+            tuple(
+                (source, (pl.ds(s * h, h),), s, (every, source)) for s in range(2) for source in range(2)
+            ),
+            deps,
+        )
+        return near.reshape(n, w, cols), far.reshape(n, w, cols)
+
+    def z_rest(have, other):
+        have = z_end(have, other)
+        for bit in reversed(range(1, z_bits - 1)):
+            have = z_end(have, z_go(have, bit))
+        return have, z_go(have, 0)
+
+    def gather_z(shard):
+        have = shard[None]
+        for bit in reversed(range(z_bits)):
+            have = z_end(have, z_go(have, bit))
         return have.reshape(-1, have.shape[-1])
 
-    def gather_z(shard):
-        return gather_z_rest(gather_z_step(shard[None], z_bits - 1))
-
-    def gather_x(a):
-        have = a[None]
+    def joined(parts, deps=()):
+        (out,) = assemble(
+            tuple(parts), ((len(parts),) + parts[0].shape,),
+            tuple((i, (), 0, (i,)) for i in range(len(parts))), deps,
+        )
+        return out
+
+    def spread_x(a):
+        have, arrays = [(0, None)], [a]
         for bit in range(x_bits):
-            have = jnp.concatenate([have, px(have, 1 << bit)], axis=0)
-        return have
-
-    def halves_of(a):
-        n = a.shape[0] // 2
-        return a[:n], a[n:]
-
-    def gather_xy_one(near, far):
-        return gather_x(near), py(far)
-
-    def gather_xy_two(near, far, far_oth):
-        n = far.shape[0]
-        both = gather_x(jnp.concatenate([far, far_oth], axis=0))
-        near_oth = py(near)
-        own = jnp.concatenate([near, both[:, :n]], axis=1)
-        oth = jnp.concatenate([near_oth, both[:, n:]], axis=1)
-        cols = far.shape[1]
-        return jnp.concatenate([own.reshape(-1, cols), oth.reshape(-1, cols)], axis=0)
+            whole = arrays[0] if bit == 0 else joined([arrays[i] if p is None else arrays[i][p] for i, p in have])
+            arrays.append(px(whole, 1 << bit))
+            last = len(arrays) - 1
+            have = have + ([(last, None)] if bit == 0 else [(last, p) for p in range(len(have))])
+        return [arrays[i] if p is None else arrays[i][p] for i, p in have]
+
+    def xy_go(near, far):
+        return spread_x(near), [far, py(far)]
+
+    def xy_one(going, deps=()):
+        near_xs, far_ts = going
+        return joined(near_xs, deps), joined(far_ts, deps)
+
+    def xy_two_go(near_x, far_t):
+        return near_x, py(near_x), spread_x(far_t)
+
+    def xy_two(going, deps=()):
+        near_x, near_oth, far_x = going
+        _, h, w, cols = near_x.shape
+        copies = []
+        for x in range(n_x):
+            for t in range(n_ta):
+                copies.append((t, (x,), 0, (t, x, 0)))
+                copies.append((n_ta + x, (t,), 0, (t, x, 1)))
+        (out,) = assemble(
+            (near_x, near_oth, *far_x), ((n_ta, n_x, 2, h, w, cols),), tuple(copies), deps
+        )
+        return out.reshape(-1, cols)
 
     def add(a, b):
         return (a.astype(F32) + b.astype(F32)).astype(a.dtype)
@@ -487,57 +591,90 @@
     def core_part(lhs, rhs, away):
         return (tn(lhs[:, : lhs.shape[1] // 2], rhs) + away.astype(F32)).astype(BF)
 
-    def cut(parts, x, s, sides):
-        size = parts[0].shape[0] // n_x
+    def p1_send(parts, deps=()):
+        rows = parts[0].shape[0]
+        size = rows // n_x
         half = size // 2
-        row = x * size + s * half
-        out = []
-        for t in sides:
-            for r in parts:
-                n = r.shape[1] // n_ta
-                out.append(r[row : row + half, t * n : (t + 1) * n])
-        return jnp.concatenate(out, axis=1) if len(out) > 1 else out[0]
-
-    def p1_send(parts):
-        near = [cut(parts, k, 0, (0, 1)) for k in range(n_x)]
-        far_own = jnp.concatenate([cut(parts, k, 1, (0,)) for k in range(n_x)], axis=0)
-        far_oth = jnp.concatenate([cut(parts, k, 1, (1,)) for k in range(n_x)], axis=0)
-        return near, far_own, far_oth
+        widths = [r.shape[1] // n_ta for r in parts]
+        cols = sum(widths)
+        copies = []
+        for i, n in enumerate(widths):
+            at = sum(widths[:i])
+            for t in range(n_ta):
+                for x in range(n_x):
+                    copies.append((
+                        i, (pl.ds(x * size, half), pl.ds(t * n, n)), x, (every, pl.ds(t * cols + at, n)),
+                    ))
+                    copies.append((
+                        i, (pl.ds(x * size + half, half), pl.ds(t * n, n)),
+                        n_x + t, (pl.ds(x * half, half), pl.ds(at, n)),
+                    ))
+        shapes = ((half, n_ta * cols),) * n_x + ((n_x * half, cols),) * n_ta
+        out = assemble(tuple(parts), shapes, tuple(copies), deps)
+        return out[:n_x], out[n_x], out[n_x + 1]
 
     def p1_go(sent):
         near, far_own, far_oth = sent
         return [px(near[k], k) for k in range(1, n_x)], py(far_oth)
 
-    def p1_end(sent, got):
-        near = sent[0][0]
-        for g in got[0]:
-            near = add(near, g)
-        far = add(sent[1], got[1])
-        n = near.shape[1] // 2
-        half = far.shape[0] // n_x
-        return near[:, :n], near[:, n:], [far[k * half : (k + 1) * half] for k in range(n_x)]
+    def p1_end(sent, got, deps=()):
+        near, far_own, _ = sent
+        half, cols = near[0].shape[0], far_own.shape[1]
+        n = len(got[0])
+        pieces = []
+        for t in range(n_ta):
+            at = (every, pl.ds(t * cols, cols))
+            pieces.append((t, (), [(i, at) for i in range(n + 1)]))
+        for x in range(n_x):
+            at = (pl.ds(x * half, half), every)
+            pieces.append((n_ta + x, (), [(n + 1, at), (n + 2, at)]))
+        pieces = [(o, to or (every, every), terms) for o, to, terms in pieces]
+        out = sums(
+            (near[0], *got[0], far_own, got[1]), (((half, cols), BF),) * (n_ta + n_x), pieces, deps
+        )
+        return out[0], out[1], out[2:]
 
     def p2_go(state):
         near_own, near_oth, far = state
         return py(near_oth), [px(far[k], k) for k in range(1, n_x)]
 
-    def p2_end(state, got, w):
-        near = add(state[0], got[0])
-        far = state[2][0]
-        for g in got[1]:
-            far = add(far, g)
-        return jnp.concatenate([near, far], axis=0).reshape(n_pa, w, -1)
+    def p2_end(state, got, w, deps=()):
+        half, cols = state[0].shape
+        h = half // w
+        pieces = []
+        for b in range(2 * h):
+            at = (pl.ds((b % h) * w, w), every)
+            terms = [(0, at), (1, at)] if b < h else [(i, at) for i in range(2, 3 + len(got[1]))]
+            pieces.append((b % 2, (b // 2,), terms))
+        return sums(
+            (state[0], got[0], state[2][0], *got[1]), (((h, w, cols), BF),) * 2, pieces, deps
+        )
+
+    def z_next(keep, got, deps=()):
+        n, w, cols = keep.shape
+        pieces = [(b % 2, (b // 2,), [(0, (b,)), (1, (b,))]) for b in range(n)]
+        return sums((keep, got), (((n // 2, w, cols), BF),) * 2, pieces, deps)
+
+    def z_done(keep, got, deps=()):
+        _, w, cols = keep.shape
+        (out,) = sums((keep, got), (((1, w, cols), F32),), [(0, (0,), [(0, (0,)), (1, (0,))])], deps)
+        return out[0]
 
     def z_split(cur):
         cur = cur.reshape((cur.shape[0] // 2, 2) + cur.shape[1:])
         return cur[:, 0], cur[:, 1]
 
-    def reduce_z(cur, first=0):
-        for bit in range(first, z_bits):
+    def reduce_z(cur):
+        for bit in range(z_bits):
             keep, give = z_split(cur)
             got = pz(give, 1 << bit)
-            cur = add(keep, got) if bit < z_bits - 1 else keep.astype(F32) + got.astype(F32)
+            cur = keep.astype(F32) + got.astype(F32) if bit == z_bits - 1 else add(keep, got)
         return cur[0]
+
+    def reduce_z_from(keep, give, first):
+        for bit in range(first, z_bits - 1):
+            keep, give = z_next(keep, pz(give, 1 << bit))
+        return z_done(keep, pz(give, 1 << (z_bits - 1)))
 
     def on_device(
         rows_in, w_qkv, b_qv, w_out, b_out, ln1_gain, ln1_bias, w_in, b_in, w_fin, b_fin,
@@ -590,27 +727,6 @@
         swapped = lambda v: jnp.concatenate([v[..., v.shape[-1] // 2 :], v[..., : v.shape[-1] // 2]], axis=-1)
         in_order = lambda v: jnp.where(first_t, v, swapped(v))
 
-        packed = lambda v: v.reshape(v.shape[0], 3, pairs, LANES).transpose(0, 2, 1, 3)
-        shard_q = packed(w_qkv.transpose(1, 0, 2).reshape(block, qkv_half)).reshape(block, -1)
-        shard_m = jnp.concatenate([w_in, w_out.T], axis=1)
-        head_mine = lax.dynamic_slice_in_dim(w_head, t0 * head_half, head_half, 1)
-        shard_e = jnp.concatenate([w_fin.T, head_mine], axis=1)
-
-        zq = gather_z(shard_q)
-        near, far = halves_of(zq)
-        zm_1 = gather_z_step(tie(shard_m, zq)[None], z_bits - 1)
-        near_q, oth_q = gather_xy_one(near, far)
-        near_q = tie(near_q, zm_1)
-        zm = gather_z_rest(zm_1)
-        h_q = tie(gather_xy_two(near_q, far, oth_q), zm)
-        r_q = pc(h_q)
-        near, far_m = halves_of(zm)
-        near_m, oth_m = gather_xy_one(near, far_m)
-        ze_1 = gather_z_step(tie(shard_e, zm)[None], z_bits - 1)
-        bias_of = lambda b: packed(jnp.concatenate([b[0], jnp.zeros_like(b[0]), b[1]])[None]).reshape(-1)
-        qkv_bias = jnp.concatenate([bias_of(b_qv), bias_of(py(b_qv))])
-        b_in_r = jnp.concatenate([b_in, py(b_in)])
-
         row_id = jnp.arange(half_rows + toks, dtype=jnp.int32)
         is_slot = row_id < slots
         token = jnp.where(
@@ -637,36 +753,55 @@
         aug_k = aug_k.astype(BF)
         aug_q = jnp.where((lane_c < 7) & ~same[:half_rows], BIG, 0.0).astype(BF)
 
+        packed = lambda v: v.reshape(v.shape[0], 3, pairs, LANES).transpose(0, 2, 1, 3)
+        shard_q = packed(w_qkv.transpose(1, 0, 2).reshape(block, qkv_half)).reshape(block, -1)
+        shard_m = jnp.concatenate([w_in, w_out.T], axis=1)
+        head_mine = lax.dynamic_slice_in_dim(w_head, t0 * head_half, head_half, 1)
+        shard_e = jnp.concatenate([w_fin.T, head_mine], axis=1)
+
+        q_0 = shard_q[None]
+        q_1 = z_go(q_0, z_bits - 1)
+        m_0 = tie(shard_m[None], q_1)
+        m_1 = z_go(m_0, z_bits - 1)
+        q_2, q_3 = z_rest(q_0, q_1)
+        near_q, far_q = z_last(q_2, q_3, (m_1,))
+        e_0 = tie(shard_e[None], m_1)
+        e_1 = z_go(e_0, z_bits - 1)
+        near_q, far_q = xy_one(xy_go(near_q, far_q), (rows, aug_q, aug_k))
+        near_m, far_m = z_last(*z_rest(m_0, m_1))
+        h_q = xy_two(xy_two_go(near_q, far_q), (near_m, e_1))
+        r_q = pc(h_q)
+        bias_of = lambda b: packed(jnp.concatenate([b[0], jnp.zeros_like(b[0]), b[1]])[None]).reshape(-1)
+        qkv_bias = jnp.concatenate([bias_of(b_qv), bias_of(py(b_qv))])
+        b_in_r = jnp.concatenate([b_in, py(b_in)])
+
         col_scale = jnp.tile(jnp.repeat(jnp.array([scale, 1.0, 1.0], F32), LANES), all_pairs)
         (qkv,) = mm_in(
             rows, h_q, r_q, 0, qkv_half, qkv_half // 3, put_scaled, (eight(qkv_bias, col_scale),),
-            ((half_rows + toks, BF),),
-        )
-        oth_m, near_m = tie(oth_m, qkv), tie(near_m, qkv)
-        h_m = gather_xy_two(near_m, far_m, oth_m)
-        ze_1 = tie(ze_1, qkv)
-        ze = gather_z_rest(ze_1)
-        kept, n_call = (), all_pairs // 4
-        for i in range(4):
-            kept = attend(
-                qkv, half_rows, aug_q, aug_k, slots, toks // 2, i * n_call, n_call, kept,
-                ((oth_m, near_m, ze_1), (), (ze,), ())[i],
-            )
-            if i == 1:
-                ze = tie(ze, kept[0])
-                near, far_e = halves_of(ze)
-                near_e, oth_e = gather_xy_one(near, far_e)
-            if i == 2:
-                h_m = tie(h_m, kept[0])
-                r_m = pc(h_m)
+            ((half_rows + toks, BF),), deps=(near_m,),
+        )
+        near_m, far_m = xy_one(xy_go(near_m, far_m), (qkv,))
+        n_call = all_pairs // 4
+        part = lambda i, kept, deps: attend(
+            qkv, half_rows, aug_q, aug_k, slots, toks, i * n_call, n_call, kept, deps
+        )
+        e_2, e_3 = z_rest(e_0, e_1)
+        going = xy_two_go(near_m, far_m)
+        kept = part(0, (), (near_m, far_m, e_2))
+        near_e, far_e = z_last(e_2, e_3, (kept[0],))
+        kept = part(1, kept, (near_e,))
+        kept = part(2, kept, ())
+        h_m = xy_two(going, (kept[0],))
+        r_m = pc(h_m)
+        kept = part(3, kept, (h_m,))
+        r_m = tie(r_m, kept[0])
+        near_e, far_e = xy_one(xy_go(near_e, far_e), (kept[0],))
         ctx, logs = kept
-        near_e, oth_e = tie(near_e, kept[0]), tie(oth_e, kept[0])
         h_one = mm_out(
             ctx, half_rows, h_m, r_m, ff_half, heads_half, heads_half // 2,
-            lambda acc, res, b: acc + res.astype(F32) + b, (rows[:half_rows], eight(b_out_r)), F32,
-            (near_e, oth_e),
-        )
-        h_e = gather_xy_two(near_e, far_e, oth_e)
+            lambda acc, res, b: acc + res.astype(F32) + b, (rows, eight(b_out_r)), F32,
+            (near_e, far_e),
+        )
         v1, r1 = norm_parts(h_one)
         normed = v1 * g1 + be1
         normed_low = normed.astype(BF)
@@ -674,7 +809,7 @@
             normed_low, h_m, r_m, 0, ff_half, ff_half // 4, put_gelu, (eight(b_in_r),),
             ((half_rows, BF), (half_rows, BF)),
         )
-        h_e = tie(h_e, active)
+        h_e = xy_two(xy_two_go(near_e, far_e), (active,))
         r_e = pc(h_e)
         h_two = mm_out(
             active, half_rows, h_e, r_e, 0, ff_half, heads_half // 2,
@@ -741,8 +876,8 @@
             branch_low, h_e, r_e, 0, ff_half, ff_half // 4, put_sloped, (slope,),
             ((half_rows, BF), (8, F32)), row_of_zeros, put_sum,
         )
-        part_fin = core_part(branch_low, active, away_fin)
-        part_head = core_part(output_low, raw_low, away_head)
+        part_fin = core_part(branch_low, active, tie(away_fin, inner_low))
+        part_head = core_part(output_low, raw_low, tie(away_head, inner_low))
         sent_f = p1_send([part_fin, part_head])
         got_f = p1_go(sent_f)
         away_in = away_part(normed_low, inner_low)
@@ -757,15 +892,15 @@
         (d_ctx,) = mm_in(
             attended_low, h_m, r_m, ff_half, heads_half, heads_half, put_plain, (), ((half_rows, BF),)
         )
-        part_in = core_part(normed_low, inner_low, away_in)
-        part_out = core_part(attended_low, ctx, away_out)
+        part_in = core_part(normed_low, inner_low, tie(away_in, d_ctx))
+        part_out = core_part(attended_low, ctx, tie(away_out, d_ctx))
         sent_m = p1_send([part_in, part_out])
         got_m = p1_go(sent_m)
-        state_f = p1_end(sent_f, got_f)
+        state_f = p1_end(sent_f, got_f, (sent_m[2],))
         got_f = p2_go(state_f)
 
         back = lambda i, kept, deps: attend_back(
-            qkv, ctx, d_ctx, logs, aug_k, slots, toks // 5, scale,
+            qkv, ctx, d_ctx, logs, aug_k, slots, 2 * toks // 5, scale,
             ((i + 2) % 4) * n_call, n_call, kept, deps,
         )
         quarter = qkv_half // 2
@@ -781,42 +916,48 @@
             return total
 
         kept = back(0, (), (sent_m[0][-1], sent_m[2], state_f[1], state_f[2][-1]))
-        cur_f = tie(p2_end(state_f, got_f, block), kept[1])
-        keep_f, give_f = z_split(cur_f)
+        keep_f, give_f = p2_end(state_f, got_f, block, (kept[1],))
         z_f = pz(give_f, 1)
         kept = back(1, kept, (give_f,))
         away_1 = away_part(rows, kept[0][:, qkv_half:])
-        state_m = p1_end(sent_m, [[tie(g, kept[1]) for g in got_m[0]], tie(got_m[1], kept[1])])
-        got_m = p2_go(state_m)
-        cur_f = tie(add(keep_f, z_f), kept[1])
-        part_1 = core_part(rows, kept[0][:, qkv_half:], away_1)
+        keep_f, give_f = z_next(keep_f, z_f, (kept[1],))
+        z_f = pz(give_f, 2)
+        part_1 = core_part(rows, kept[0][:, qkv_half:], tie(away_1, give_f))
         sent_1 = x_blocks(part_1)
         got_1 = x_go(sent_1)
-        kept = back(2, kept, (state_m[1], state_m[2][-1], cur_f, sent_1[1]))
+        kept = back(2, kept, (give_f, sent_1[1]))
+        state_m = p1_end(sent_m, got_m, (kept[1],))
         away_2 = away_part(rows, columns(kept[0], 0))
-        cur_m = tie(p2_end(state_m, got_m, block), kept[1])
-        keep_m, give_m = z_split(cur_m)
-        z_m = pz(give_m, 1)
-        out_f = reduce_z(cur_f, 1)
+        got_m = p2_go(state_m)
         y_1 = x_end(sent_1, [tie(g, kept[1]) for g in got_1])
-        part_2 = core_part(rows, columns(kept[0], 0), away_2)
+        part_2 = core_part(rows, columns(kept[0], 0), tie(away_2, y_1))
         sent_2 = x_blocks(part_2)
         got_2 = x_go(sent_2)
-        kept = back(3, kept, (give_m, y_1, sent_2[1]))
+        if z_bits == 2:
+            out_f = z_done(keep_f, z_f, (kept[1],))
+        else:
+            out_f = reduce_z_from(*z_next(keep_f, z_f), 2)
+        kept = back(3, kept, (y_1, sent_2[1], state_m[1], state_m[2][-1]))
         d_qkv, sums_qv = kept
-        y_1 = tie(py(y_1), sums_qv)
+        y_1 = py(y_1)
+        away_3 = away_part(rows, columns(d_qkv, 1))
         to_other = mm_out(
-            d_qkv[half_rows:], toks, h_q, r_q, 0, qkv_half, heads_half // 2, lambda acc: acc, (), BF
-        )
-        to_other = py(to_other)
-        away_3 = away_part(rows, columns(d_qkv, 1))
-        out_m = reduce_z(add(keep_m, z_m), 1)
+            d_qkv, toks, h_q, r_q, 0, qkv_half, heads_half // 2, lambda acc: acc, (), BF,
+            (away_3,), row=half_rows,
+        )
+        d_qkv = tie(d_qkv, to_other)
+        sums_qv = tie(sums_qv, to_other)
         part_3 = core_part(rows, columns(d_qkv, 1), away_3)
         sent_3 = x_blocks(part_3)
         got_3 = x_go(sent_3)
+        to_other = py(to_other)
+        keep_m, give_m = p2_end(state_m, got_m, block, (sums_qv,))
+        out_m = reduce_z_from(keep_m, give_m, 0)
+        y_1 = tie(y_1, sums_qv)
+        got_2 = [tie(g, sums_qv) for g in got_2]
         grad_rows = mm_out(
             d_qkv, half_rows, h_q, r_q, 0, qkv_half, heads_half // 2,
-            lambda acc, res: acc + res, (h_one_grad,), F32,
+            lambda acc, res: acc + res, (h_one_grad,), F32, (sent_3[1],),
         )
         as_z = lambda a: a.reshape(n_pa, block, -1)
         out_2 = reduce_z(as_z(add(x_end(sent_2, got_2), y_1[:, :quarter])))
@@ -829,38 +970,33 @@
         head_keep = jnp.where(first_t, g_head[:n_h], g_head[n_h:])
         head_got = py(jnp.where(first_t, g_head[n_h:], g_head[:n_h]))
         g_w_head = in_order(jnp.concatenate([head_keep, head_got], axis=1))
-        grad_rows = grad_rows + jnp.concatenate(
-            [jnp.zeros((slots, width), F32), to_other.astype(F32)], axis=0
-        )
-        grad_rows = permute(grad_rows, back_info, (half_rows,), block, low_bits)
-
-        rel = jnp.arange(blocks, dtype=jnp.int32)
-        rel_c, rel_x, rel_z = rel // (n_x * n_pa), (rel // n_pa) % n_x, rel % n_pa
-        source = ((rel_x ^ x0) * cores + (rel_c ^ c0)) * n_pa + (rel_z ^ z0)
-        by_block = lambda v: v.reshape(blocks, n_ta, -1)
-        absolute = jnp.concatenate(
-            [by_block(in_order(v)) for v in (sums_in[0], sums_qv[0], sums_qv[1])] + [by_block(g_b_head)],
-            axis=2,
-        )
-        absolute = jnp.take(absolute, source, axis=0)
+        grad_rows = permute(
+            grad_rows, back_info, (half_rows,), block, low_bits, slots, (to_other,)
+        )
+
+        d_vecs = permute(
+            eight(g_b_out, g_g1, g_be1, g_b_fin, g_g2, g_be2), back_info, (8,), block, low_bits
+        )
         vec = jnp.concatenate(
-            [absolute] + [by_block(v) for v in (g_b_out, g_g1, g_be1, g_b_fin, g_g2, g_be2)], axis=2
-        )
-        vec = jnp.where(first_t, vec, vec[:, ::-1]).reshape(cores, blocks // cores, n_ta, -1)
-        vec = vec[0] + pc(vec[1])
-        vec = vec.reshape(n_x, n_pa, n_ta, -1)
-        total = vec[0]
-        for k in range(1, n_x):
-            total = total + px(vec[k], k)
-        vec = reduce_z(total[:, 0] + py(total[:, 1]))
+            [d_vecs, in_order(sums_in[0]).reshape(-1, width), g_b_head[None], in_order(sums_qv[:2])]
+        )
+        vec = vec + pc(vec)
+        for bit in range(x_bits):
+            vec = vec + px(vec, 1 << bit)
+        vec = vec + py(vec)
+        for bit in range(z_bits):
+            vec = vec + pz(vec, 1 << bit)
+        place = (p0 * n_pa + z0) * n_ta + t0
         w32 = width // (blocks * n_ta)
-        sizes = [n_ta * ff_half // (blocks * n_ta)] + [w32] * 9
-        offs = [sum(sizes[:i]) for i in range(len(sizes) + 1)]
-        (o_b_in, o_bq, o_bv, o_b_head, o_b_out, o_g1, o_be1, o_b_fin, o_g2, o_be2) = (
-            vec[offs[i] : offs[i + 1]] for i in range(10)
+        ff_rows = n_ta * ff_half // width
+        mine = lax.dynamic_slice_in_dim(vec, place * w32, w32, 1)
+        o_b_out, o_g1, o_be1, o_b_fin, o_g2, o_be2 = (mine[i] for i in range(6))
+        o_b_head, o_bqv = mine[8 + ff_rows], mine[9 + ff_rows : 11 + ff_rows]
+        o_b_in = lax.dynamic_slice_in_dim(
+            vec[8 : 8 + ff_rows].reshape(-1), place * (ff_rows * w32), ff_rows * w32, 0
         )
         return (
-            scores, grad_rows, g_w_qkv, jnp.stack([o_bq, o_bv]), g_w_out.T, o_b_out, o_g1, o_be1,
+            scores, grad_rows, g_w_qkv, o_bqv, g_w_out.T, o_b_out, o_g1, o_be1,
             g_w_in, o_b_in, g_w_fin.T, o_b_fin, o_g2, o_be2, g_w_head, o_b_head,
         )
 

time: 756 us -> 689 us (0.911)
  waiting for transfers between devices: 215 us -> 143 us
  Pallas kernels: 230 us -> 292 us
  other arithmetic: 98.8 us -> 43.9 us
  local copies, waits for them, and re-layouts: 64.6 us -> 52.9 us
    pallas_call x0 -> x27, Pallas kernels: none -> 75.6 us  [the longest x19 53 us: assemble(): pl.pallas_call(functools.partial(assemble_kernel, len(arrays), len(deps),...]
    ppermute x19, waiting for transfers between devices: 81.2 us -> 26 us  [py(): return lax.ppermute(v, 'ta', [(i, i ^ 1) for i in range(n_ta)])]
    ppermute x14, waiting for transfers between devices: 41.7 us -> 7.7 us  [px(): return lax.ppermute(v, 'pb', [(i, i ^ cores * k) for i in range(n_pb)])]
    concatenate x24 -> x1, other arithmetic: 26.4 us -> 0.02 us  [on_device(): jnp.concatenate([d_vecs, in_order(sums_in[0]).reshape(-1, width), g_b_hea...]
    ppermute x20, waiting for transfers between devices: 85.4 us -> 102 us  [pz(): return lax.ppermute(v, 'pa', [(i, i ^ k) for i in range(n_pa)])]
    slice x18 -> x1, local copies, waits for them, and re-layouts: 13.8 us -> 0.64 us  [on_device(): o_b_head, o_bqv = (mine[8 + ff_rows], mine[9 + ff_rows:11 + ff_rows])]
    unnamed x243 -> x193, local copies, waits for them, and re-layouts: 17.5 us -> 29.8 us
    convert_element_type x12 -> x3, other arithmetic: 15.3 us -> 4.4 us  [add(): return (a.astype(F32) + b.astype(F32)).astype(a.dtype)]
  transfers between devices with their start and end apart: 64 -> 64, of which waited for: 29 -> 25; matrix products, arithmetic and copies ran while one was open for 23% -> 14% of each run, Pallas kernels for 24% -> 31%
where the time goes in v2:
time: 689 us; the launch traced here: 679 us
  Pallas kernels  292 us (42%)
  waiting for transfers between devices  143 us (21%)
  matrix products  73.9 us (11%)
  starting transfers between devices  70.4 us (10%)
  local copies, waits for them, and re-layouts  52.9 us (8%)
  other arithmetic  43.9 us (6%)
    ppermute x20, waiting for transfers between devices, pz(): return lax.ppermute(v, 'pa', [(i, i ^ k) for i in range(n_pa)])  102 us
    dot_general x15, matrix products, tn(): lax.dot_general(a, b, (((0,), (0,)), ((), ())), preferred_element_type=F32)  67.5 us
    pallas_call x6, Pallas kernels, mm_out(): pl.pallas_call(functools.partial(mm_out_kernel, chunk_of(m), half, len(ex...  57.8 us
    pallas_call x5, Pallas kernels, mm_in(): pl.pallas_call(functools.partial(mm_in_kernel, chunk_of(m), epilogue, sta...  57.5 us
    pallas_call x19, Pallas kernels, assemble(): pl.pallas_call(functools.partial(assemble_kernel, len(arrays), len(deps),...  53 us
    pallas_call x4, Pallas kernels, attend_back(): pl.pallas_call(functools.partial(attend_back_kernel, slots, tile_k, scale...  50.9 us
    pallas_call x4, Pallas kernels, attend(): pl.pallas_call(functools.partial(attend_kernel, slots, tile_q, len(deps))...  38.1 us
    ppermute x20, starting transfers between devices, pz(): return lax.ppermute(v, 'pa', [(i, i ^ k) for i in range(n_pa)])  31.4 us
  transfers between devices with their start and end apart: 64, of which 25 were waited for; matrix products, arithmetic and copies ran while one was open for 14% of the time, Pallas kernels for 31%

profile of v2, /device:TPU:0, one launch (start us, length us, event | category | flops | bytes accessed | tf_op | source)
XLA Modules:
  0.0 679.0 jit_solution(2708484202134205869)
XLA Ops:
  21.9 12.5 %collective-permute-done.2.refs_2_.refs_1_ = bf16[1,64,2560]{2,1,0:T(8,128)(2,1)S(1)} collective-permute-done((bf16[1,64,2560]{2,1,0:T(8,128)(2,1)}, bf16[1,64,2560]{2,1,0:T(8,128)(2,1)S(1)}, u32[]{:S(2)}, u32[]{:S(2)}) %collective-permute-start.2) | collective-permute-done | bytes 327712 | tf_op jit(solution)/shard_map/ppermute | solution.py:499
  64.7 19.0 %collective-permute-done.7.refs_1_ = bf16[2,64,2560]{2,1,0:T(8,128)(2,1)S(1)} collective-permute-done((bf16[2,64,2560]{2,1,0:T(8,128)(2,1)}, bf16[2,64,2560]{2,1,0:T(8,128)(2,1)S(1)}, u32[]{:S(2)}, u32[]{:S(2)}) %collective-permute-start.7) | collective-permute-done | bytes 655392 | tf_op jit(solution)/shard_map/ppermute | solution.py:499
  102.1 14.5 %shard_map.316.refs_2_.q_ref.k_ref.v_ref = bf16[1344,3072]{1,0:T(8,128)(2,1)} custom-call(bf16[1344,1024]{1,0:T(8,128)(2,1)} %shard_map.306.refs_2_.a_ref.rest_0_, bf16[1024,1536]{1,0:T(8,128)(2,1)} %bitcast.231, bf16[1024,1536]{1,0:T(8,128)(2,1)} %copy-done.8, f32[8,3072]{1,0:T(8,128)} %maximum_maximum_fusion.3.rest_0_, bf16[2,64,2560]{2,1,0:T(8,128)(2,1)} %bitcast.247), custom_call_target="tpu_custom_call" | custom-call | flops 8455716864 | bytes 17301504 | tf_op jit(solution)/shard_map/pallas_call | solution.py:350
  125.2 9.5 %shard_map.320 = (bf16[704,1024]{1,0:T(8,128)(2,1)}, bf16[704,1024]{1,0:T(8,128)(2,1)}) custom-call(bf16[1344,3072]{1,0:T(8,128)(2,1)} %shard_map.316.refs_2_.q_ref.k_ref.v_ref, bf16[1344,3072]{1,0:T(8,128)(2,1)} %shard_map.316.refs_2_.q_ref.k_ref.v_ref, bf16[1344,3072]{1,0:T(8,128)(2,1)} %shard_map.316.refs_2_.q_ref.k_ref.v_ref, ...), custom_call_target="tpu_custom_call" | custom-call | flops 3875536896 | bytes 2457600 | tf_op jit(solution)/shard_map/pallas_call | solution.py:135
  137.9 9.5 %shard_map.322 = (bf16[704,1024]{1,0:T(8,128)(2,1)}, bf16[704,1024]{1,0:T(8,128)(2,1)}) custom-call(bf16[1344,3072]{1,0:T(8,128)(2,1)} %shard_map.316.refs_2_.q_ref.k_ref.v_ref, bf16[1344,3072]{1,0:T(8,128)(2,1)} %shard_map.316.refs_2_.q_ref.k_ref.v_ref, ...), custom_call_target="tpu_custom_call", output_to_operand_aliasing={{0}: (5, {}), {1}: (6, {})} | custom-call | flops 3875536896 | bytes 2457600 | tf_op jit(solution)/shard_map/pallas_call | solution.py:135
  147.4 9.7 %shard_map.323 = (bf16[704,1024]{1,0:T(8,128)(2,1)}, bf16[704,1024]{1,0:T(8,128)(2,1)}) custom-call(bf16[1344,3072]{1,0:T(8,128)(2,1)} %shard_map.316.refs_2_.q_ref.k_ref.v_ref, bf16[1344,3072]{1,0:T(8,128)(2,1)} %shard_map.316.refs_2_.q_ref.k_ref.v_ref, ...), custom_call_target="tpu_custom_call", output_to_operand_aliasing={{0}: (5, {}), {1}: (6, {})} | custom-call | flops 3875536896 | bytes 2457600 | tf_op jit(solution)/shard_map/pallas_call | solution.py:135
  172.3 9.4 %shard_map.325 = (bf16[704,1024]{1,0:T(8,128)(2,1)}, bf16[704,1024]{1,0:T(8,128)(2,1)}) custom-call(bf16[1344,3072]{1,0:T(8,128)(2,1)} %shard_map.316.refs_2_.q_ref.k_ref.v_ref, bf16[1344,3072]{1,0:T(8,128)(2,1)} %shard_map.316.refs_2_.q_ref.k_ref.v_ref, ...), custom_call_target="tpu_custom_call", output_to_operand_aliasing={{0}: (5, {}), {1}: (6, {})} | custom-call | flops 3875536896 | bytes 2457600 | tf_op jit(solution)/shard_map/pallas_call | solution.py:135
  194.0 6.0 shard_map.330
  205.8 20.2 %shard_map.331 = (bf16[704,4096]{1,0:T(8,128)(2,1)}, bf16[704,4096]{1,0:T(8,128)(2,1)}) custom-call(bf16[704,1024]{1,0:T(8,128)(2,1)} %get-tuple-element.138.a_ref, bf16[1024,2560]{1,0:T(8,128)(2,1)} %bitcast.217, bf16[1024,2560]{1,0:T(8,128)(2,1)} %shard_map.326.r0_ref.r1_ref.r_ref, f32[8,4096]{1,0:T(8,128)} %concatenate.101.rest_0_), custom_call_target="tpu_custom_call" | custom-call | flops 5905580032 | bytes 21364736 | tf_op jit(solution)/shard_map/pallas_call | solution.py:350
  233.0 7.0 %collective-permute-done.22.r0_ref.r1_ref.r_ref = bf16[1024,2560]{1,0:T(8,128)(2,1)} collective-permute-done((bf16[1024,2560]{1,0:T(8,128)(2,1)}, bf16[1024,2560]{1,0:T(8,128)(2,1)}, u32[]{:S(2)}, u32[]{:S(2)}) %collective-permute-start.22) | collective-permute-done | bytes 5242912 | tf_op jit(solution)/shard_map/ppermute | solution.py:496
  240.1 13.0 %shard_map.333 = f32[704,1024]{1,0:T(8,128)} custom-call(bf16[704,4096]{1,0:T(8,128)(2,1)} %get-tuple-element.79.refs_4_.a0_ref.a1_ref, bf16[704,4096]{1,0:T(8,128)(2,1)} %get-tuple-element.79.refs_4_.a0_ref.a1_ref, bf16[1024,2560]{1,0:T(8,128)(2,1)} %bitcast.222, bf16[1024,2560]{1,0:T(8,128)(2,1)} %bitcast.223, ...), custom_call_target="tpu_custom_call" | custom-call | flops 5905580032 | bytes 17039360 | tf_op jit(solution)/shard_map/pallas_call | solution.py:401
  270.8 7.0 %collective-permute-done.23.refs_1_ = bf16[1,64,1024]{2,1,0:T(8,128)(2,1)S(1)} collective-permute-done((bf16[1,64,1024]{2,1,0:T(8,128)(2,1)S(1)}, bf16[1,64,1024]{2,1,0:T(8,128)(2,1)S(1)}, u32[]{:S(2)}, u32[]{:S(2)}) %collective-permute-start.23) | collective-permute-done | bytes 131104 | tf_op jit(solution)/shard_map/ppermute | solution.py:499
  280.9 7.0 %collective-permute-done.24.refs_1_ = bf16[2,64,1024]{2,1,0:T(8,128)(2,1)S(1)} collective-permute-done((bf16[2,64,1024]{2,1,0:T(8,128)(2,1)}, bf16[2,64,1024]{2,1,0:T(8,128)(2,1)S(1)}, u32[]{:S(2)}, u32[]{:S(2)}) %collective-permute-start.24) | collective-permute-done | bytes 262176 | tf_op jit(solution)/shard_map/ppermute | solution.py:499
  292.9 10.1 %collective-permute-done.25 = bf16[256,1024]{1,0:T(8,128)(2,1)S(1)} collective-permute-done((bf16[256,1024]{1,0:T(8,128)(2,1)}, bf16[256,1024]{1,0:T(8,128)(2,1)S(1)}, u32[]{:S(2)}, u32[]{:S(2)}) %collective-permute-start.25) | collective-permute-done | bytes 524320 | tf_op jit(solution)/shard_map/ppermute | solution.py:502
  316.7 8.6 %collective-permute-done.27 = bf16[256,1024]{1,0:T(8,128)(2,1)S(1)} collective-permute-done((bf16[256,1024]{1,0:T(8,128)(2,1)S(1)}, bf16[256,1024]{1,0:T(8,128)(2,1)S(1)}, u32[]{:S(2)}, u32[]{:S(2)}) %collective-permute-start.27) | collective-permute-done | bytes 524320 | tf_op jit(solution)/shard_map/ppermute | solution.py:502
  326.5 6.9 %collective-permute-done.28 = bf16[2,64,1024]{2,1,0:T(8,128)(2,1)S(1)} collective-permute-done((bf16[2,64,1024]{2,1,0:T(8,128)(2,1)S(1)}, bf16[2,64,1024]{2,1,0:T(8,128)(2,1)S(1)}, u32[]{:S(2)}, u32[]{:S(2)}) %collective-permute-start.28) | collective-permute-done | bytes 262176 | tf_op jit(solution)/shard_map/ppermute | solution.py:499
  343.0 6.0 shard_map.337
  363.3 13.4 %shard_map.338 = (bf16[704,4096]{1,0:T(8,128)(2,1)}, f32[8,4096]{1,0:T(8,128)}) custom-call(bf16[704,1024]{1,0:T(8,128)(2,1)} %copy-done.20, bf16[1024,2560]{1,0:T(8,128)(2,1)} %bitcast.227, bf16[1024,2560]{1,0:T(8,128)(2,1)} %collective-permute-done.22.r0_ref.r1_ref.r_ref, bf16[704,4096]{1,0:T(8,128)(2,1)} %get-tuple-element.80.rest_0_), custom_call_target="tpu_custom_call" | custom-call | flops 5905580032 | bytes 15663104 | tf_op jit(solution)/shard_map/pallas_call | solution.py:350
  376.7 7.6 %convolution_convert_fusion = bf16[512,4096]{1,0:T(8,128)(2,1)} fusion(bf16[704,4096]{1,0:T(8,128)(2,1)} %get-tuple-element.81.refs_1_.a0_ref.a1_ref, bf16[704,1024]{1,0:T(8,128)(2,1)S(1)} %copy-done.18), kind=kOutput, calls=%fused_computation.5 | convolution fusion | flops 2954887168 | bytes 10682368 | tf_op jit(solution)/shard_map/dot_general | solution.py:32
  388.3 9.5 %add_convert_fusion.1.refs_0_ = bf16[512,4096]{1,0:T(8,128)(2,1)} fusion(bf16[512,4096]{1,0:T(8,128)(2,1)} %shard_map.339, bf16[704,4096]{1,0:T(8,128)(2,1)} %get-tuple-element.79.refs_4_.a0_ref.a1_ref, bf16[704,1024]{1,0:T(8,128)(2,1)} %copy-done.20), kind=kOutput, calls=%fused_computation.4 | convolution fusion | flops 2959081472 | bytes 14876672 | tf_op jit(solution)/shard_map/dot_general | solution.py:32
  406.2 12.8 %shard_map.342 = f32[704,1024]{1,0:T(8,128)} custom-call(bf16[704,4096]{1,0:T(8,128)(2,1)} %get-tuple-element.81.refs_1_.a0_ref.a1_ref, bf16[704,4096]{1,0:T(8,128)(2,1)} %get-tuple-element.81.refs_1_.a0_ref.a1_ref, bf16[1024,2560]{1,0:T(8,128)(2,1)} %bitcast.218, bf16[1024,2560]{1,0:T(8,128)(2,1)} %bitcast.219, ...), custom_call_target="tpu_custom_call" | custom-call | flops 5905580032 | bytes 17039360 | tf_op jit(solution)/shard_map/pallas_call | solution.py:401
  433.5 8.4 %add_convert_fusion.refs_0_ = bf16[512,4096]{1,0:T(8,128)(2,1)} fusion(bf16[512,4096]{1,0:T(8,128)(2,1)} %shard_map.344, bf16[704,4096]{1,0:T(8,128)(2,1)} %get-tuple-element.81.refs_1_.a0_ref.a1_ref, bf16[704,1024]{1,0:T(8,128)(2,1)S(1)} %copy-done.19), kind=kOutput, calls=%fused_computation.3 | convolution fusion | flops 2959081472 | bytes 14876672 | tf_op jit(solution)/shard_map/dot_general | solution.py:32
  456.3 12.9 %shard_map.348 = (bf16[1344,3072]{1,0:T(8,128)(2,1)}, f32[8,1024]{1,0:T(8,128)}) custom-call(bf16[1344,3072]{1,0:T(8,128)(2,1)} %shard_map.316.refs_2_.q_ref.k_ref.v_ref, bf16[1344,3072]{1,0:T(8,128)(2,1)} %shard_map.316.refs_2_.q_ref.k_ref.v_ref, bf16[1344,3072]{1,0:T(8,128)(2,1)} %shard_map.316.refs_2_.q_ref.k_ref.v_ref, ...), custom_call_target="tpu_custom_call" | custom-call | flops 9688842240 | bytes 4915200 | tf_op jit(solution)/shard_map/pallas_call | solution.py:228
  477.0 12.7 %shard_map.350 = (bf16[1344,3072]{1,0:T(8,128)(2,1)}, f32[8,1024]{1,0:T(8,128)}) custom-call(bf16[1344,3072]{1,0:T(8,128)(2,1)} %shard_map.316.refs_2_.q_ref.k_ref.v_ref, bf16[1344,3072]{1,0:T(8,128)(2,1)} %shard_map.316.refs_2_.q_ref.k_ref.v_ref, ...), custom_call_target="tpu_custom_call", output_to_operand_aliasing={{0}: (7, {}), {1}: (8, {})} | custom-call | flops 9688842240 | bytes 4915200 | tf_op jit(solution)/shard_map/pallas_call | solution.py:228
  489.7 5.9 fusion.7
  499.3 13.7 %collective-permute-done.38.refs_1_ = bf16[2,64,2560]{2,1,0:T(8,128)(2,1)S(1)} collective-permute-done((bf16[2,64,2560]{2,1,0:T(8,128)(2,1)}, bf16[2,64,2560]{2,1,0:T(8,128)(2,1)S(1)}, u32[]{:S(2)}, u32[]{:S(2)}) %collective-permute-start.38) | collective-permute-done | bytes 655392 | tf_op jit(solution)/shard_map/ppermute | solution.py:499
  525.6 12.6 %shard_map.353 = (bf16[1344,3072]{1,0:T(8,128)(2,1)}, f32[8,1024]{1,0:T(8,128)}) custom-call(bf16[1344,3072]{1,0:T(8,128)(2,1)} %shard_map.316.refs_2_.q_ref.k_ref.v_ref, bf16[1344,3072]{1,0:T(8,128)(2,1)} %shard_map.316.refs_2_.q_ref.k_ref.v_ref, ...), custom_call_target="tpu_custom_call", output_to_operand_aliasing={{0}: (7, {}), {1}: (8, {})} | custom-call | flops 9688842240 | bytes 4915200 | tf_op jit(solution)/shard_map/pallas_call | solution.py:228
  557.9 12.7 %shard_map.357 = (bf16[1344,3072]{1,0:T(8,128)(2,1)}, f32[8,1024]{1,0:T(8,128)}) custom-call(bf16[1344,3072]{1,0:T(8,128)(2,1)} %shard_map.316.refs_2_.q_ref.k_ref.v_ref, bf16[1344,3072]{1,0:T(8,128)(2,1)} %shard_map.316.refs_2_.q_ref.k_ref.v_ref, ...), custom_call_target="tpu_custom_call", output_to_operand_aliasing={{0}: (7, {}), {1}: (8, {})} | custom-call | flops 9688842240 | bytes 4915200 | tf_op jit(solution)/shard_map/pallas_call | solution.py:228
  579.7 9.3 %shard_map.358.refs_1_ = bf16[640,1024]{1,0:T(8,128)(2,1)} custom-call(bf16[1344,3072]{1,0:T(8,128)(2,1)} %get-tuple-element.106.a0_ref.a1_ref.refs_0_, bf16[1344,3072]{1,0:T(8,128)(2,1)} %get-tuple-element.106.a0_ref.a1_ref.refs_0_, bf16[1024,1536]{1,0:T(8,128)(2,1)} %bitcast.232, bf16[1024,1536]{1,0:T(8,128)(2,1)} %bitcast.233, ...), custom_call_target="tpu_custom_call" | custom-call | flops 4026531840 | bytes 12845056 | tf_op jit(solution)/shard_map/pallas_call | solution.py:401
  609.1 10.7 %shard_map.360.x_ref = f32[704,1024]{1,0:T(8,128)} custom-call(bf16[1344,3072]{1,0:T(8,128)(2,1)} %shard_map.359.a0_ref.a1_ref, bf16[1344,3072]{1,0:T(8,128)(2,1)} %shard_map.359.a0_ref.a1_ref, bf16[1024,1536]{1,0:T(8,128)(2,1)} %bitcast.234, bf16[1024,1536]{1,0:T(8,128)(2,1)} %bitcast.235, bf16[1024,1536]{1,0:T(8,128)(2,1)} %copy-done.8, ...), custom_call_target="tpu_custom_call" | custom-call | flops 4429185024 | bytes 13500416 | tf_op jit(solution)/shard_map/pallas_call | solution.py:401
  632.2 12.2 %collective-permute-done.48 = bf16[2,64,768]{2,1,0:T(8,128)(2,1)S(1)} collective-permute-done((bf16[2,64,768]{2,1,0:T(8,128)(2,1)S(1)}, bf16[2,64,768]{2,1,0:T(8,128)(2,1)S(1)}, u32[]{:S(2)}, u32[]{:S(2)}) %collective-permute-start.48) | collective-permute-done | bytes 196640 | tf_op jit(solution)/shard_map/ppermute | solution.py:499
  653.5 7.5 %collective-permute-done.49 = bf16[1,64,768]{2,1,0:T(8,128)(2,1)S(1)} collective-permute-done((bf16[1,64,768]{2,1,0:T(8,128)(2,1)S(1)}, bf16[1,64,768]{2,1,0:T(8,128)(2,1)S(1)}, u32[]{:S(2)}, u32[]{:S(2)}) %collective-permute-start.49) | collective-permute-done | bytes 98336 | tf_op jit(solution)/shard_map/ppermute | solution.py:499
  (527 shorter events, 338.2 us)
Async XLA Ops:
  17.7 17.6 %collective-permute-start.1 = (bf16[2,64,1536]{2,1,0:T(8,128)(2,1)}, bf16[2,64,1536]{2,1,0:T(8,128)(2,1)S(1)}, u32[]{:S(2)}, u32[]{:S(2)}) collective-permute-start(bf16[2,64,1536]{2,1,0:T(8,128)(2,1)} %bitcast.256), channel_id=1, source_target_pairs={{0,2},{2,0},{4,6},{6,4},{1,3},{3,1},{5,7},{7,5},{8,10},{10,8},{12,... | collective-permute-start | bytes 1179656 | tf_op jit(solution)/shard_map/ppermute | solution.py:499
  52.6 34.4 %collective-permute-start.4 = (bf16[2,2,64,1536]{3,2,1,0:T(8,128)(2,1)}, bf16[2,2,64,1536]{3,2,1,0:T(8,128)(2,1)S(1)}, u32[]{:S(2)}, u32[]{:S(2)}) collective-permute-start(bf16[2,2,64,1536]{3,2,1,0:T(8,128)(2,1)} %shard_map.310.refs_0_), channel_id=1, source_target_pairs={{0,1},{1,0},{2,3},{3,2},{4,5},{5,4},{6,7},{7,6},{8,9},{9,8},{10,11... | collective-permute-start | bytes 2359304 | tf_op jit(solution)/shard_map/ppermute | solution.py:502
  56.0 31.0 %collective-permute-start.6 = (bf16[2,2,64,1536]{3,2,1,0:T(8,128)(2,1)}, bf16[2,2,64,1536]{3,2,1,0:T(8,128)(2,1)S(1)}, u32[]{:S(2)}, u32[]{:S(2)}) collective-permute-start(bf16[2,2,64,1536]{3,2,1,0:T(8,128)(2,1)} %shard_map.311.refs_2_), channel_id=1, source_target_pairs={{0,16},{8,24},{16,0},{24,8},{1,17},{9,25},{17,1},{25,9},{2,18},{10... | collective-permute-start | bytes 2359304 | tf_op jit(solution)/shard_map/ppermute | solution.py:493
  59.5 24.2 %collective-permute-start.7 = (bf16[2,64,2560]{2,1,0:T(8,128)(2,1)}, bf16[2,64,2560]{2,1,0:T(8,128)(2,1)S(1)}, u32[]{:S(2)}, u32[]{:S(2)}) collective-permute-start(bf16[2,64,2560]{2,1,0:T(8,128)(2,1)} %bitcast.241), channel_id=1, source_target_pairs={{0,2},{2,0},{4,6},{6,4},{1,3},{3,1},{5,7},{7,5},{8,10},{10,8},{12,... | collective-permute-start | bytes 1966088 | tf_op jit(solution)/shard_map/ppermute | solution.py:499
  64.6 22.3 %collective-permute-start.8 = (bf16[1,64,2560]{2,1,0:T(8,128)(2,1)}, bf16[1,64,2560]{2,1,0:T(8,128)(2,1)S(1)}, u32[]{:S(2)}, u32[]{:S(2)}) collective-permute-start(bf16[1,64,2560]{2,1,0:T(8,128)(2,1)} %shard_map.314.refs_0_), channel_id=1, source_target_pairs={{0,4},{2,6},{4,0},{6,2},{1,5},{3,7},{5,1},{7,3},{8,12},{10,14},{12... | collective-permute-start | bytes 983048 | tf_op jit(solution)/shard_map/ppermute | solution.py:499
  98.3 36.4 %collective-permute-start.13 = (bf16[2,64,2560]{2,1,0:T(8,128)(2,1)}, bf16[2,64,2560]{2,1,0:T(8,128)(2,1)S(1)}, u32[]{:S(2)}, u32[]{:S(2)}) collective-permute-start(bf16[2,64,2560]{2,1,0:T(8,128)(2,1)} %bitcast.236), channel_id=1, source_target_pairs={{0,2},{2,0},{4,6},{6,4},{1,3},{3,1},{5,7},{7,5},{8,10},{10,8},{12,... | collective-permute-start | bytes 1966088 | tf_op jit(solution)/shard_map/ppermute | solution.py:499
  98.4 18.3 %collective-permute-start.11 = (bf16[2,64,2560]{2,1,0:T(8,128)(2,1)}, bf16[2,64,2560]{2,1,0:T(8,128)(2,1)S(1)}, u32[]{:S(2)}, u32[]{:S(2)}) collective-permute-start(bf16[2,64,2560]{2,1,0:T(8,128)(2,1)} %bitcast.246), channel_id=1, source_target_pairs={{0,16},{8,24},{16,0},{24,8},{1,17},{9,25},{17,1},{25,9},{2,18},{10... | collective-permute-start | bytes 1966088 | tf_op jit(solution)/shard_map/ppermute | solution.py:493
  99.0 21.4 %collective-permute-start.12 = (bf16[2,64,2560]{2,1,0:T(8,128)(2,1)}, bf16[2,64,2560]{2,1,0:T(8,128)(2,1)S(1)}, u32[]{:S(2)}, u32[]{:S(2)}) collective-permute-start(bf16[2,64,2560]{2,1,0:T(8,128)(2,1)} %bitcast.265), channel_id=1, source_target_pairs={{0,1},{1,0},{2,3},{3,2},{4,5},{5,4},{6,7},{7,6},{8,9},{9,8},{10,11... | collective-permute-start | bytes 1966088 | tf_op jit(solution)/shard_map/ppermute | solution.py:502
  119.8 37.3 %collective-permute-start.14 = (bf16[2,2,64,2560]{3,2,1,0:T(8,128)(2,1)}, bf16[2,2,64,2560]{3,2,1,0:T(8,128)(2,1)S(1)}, u32[]{:S(2)}, u32[]{:S(2)}) collective-permute-start(bf16[2,2,64,2560]{3,2,1,0:T(8,128)(2,1)} %shard_map.317.rest_0_.refs_0_), channel_id=1, source_target_pairs={{0,1},{1,0},{2,3},{3,2},{4,5},{5,4},{6,7},{7,6},{8,9},{9,8},{10,11... | collective-permute-start | bytes 3932168 | tf_op jit(solution)/shard_map/ppermute | solution.py:502
  123.6 33.5 %collective-permute-start.15 = (bf16[2,2,64,2560]{3,2,1,0:T(8,128)(2,1)}, bf16[2,2,64,2560]{3,2,1,0:T(8,128)(2,1)S(1)}, u32[]{:S(2)}, u32[]{:S(2)}) collective-permute-start(bf16[2,2,64,2560]{3,2,1,0:T(8,128)(2,1)} %shard_map.318.rest_1_.refs_2_), channel_id=1, source_target_pairs={{0,16},{8,24},{16,0},{24,8},{1,17},{9,25},{17,1},{25,9},{2,18},{10... | collective-permute-start | bytes 3932168 | tf_op jit(solution)/shard_map/ppermute | solution.py:493
  163.7 30.3 %collective-permute-start.16 = (bf16[1024,2560]{1,0:T(8,128)(2,1)}, bf16[1024,2560]{1,0:T(8,128)(2,1)}, u32[]{:S(2)}, u32[]{:S(2)}) collective-permute-start(bf16[1024,2560]{1,0:T(8,128)(2,1)} %bitcast.213), channel_id=1, source_target_pairs={{0,8},{8,0},{16,24},{24,16},{1,9},{9,1},{17,25},{25,17},{2,10},{10... | collective-permute-start | bytes 15728648 | tf_op jit(solution)/shard_map/ppermute | solution.py:496
  170.1 20.1 %collective-permute-start.18 = (bf16[2,64,2560]{2,1,0:T(8,128)(2,1)S(1)}, bf16[2,64,2560]{2,1,0:T(8,128)(2,1)S(1)}, u32[]{:S(2)}, u32[]{:S(2)}) collective-permute-start(bf16[2,64,2560]{2,1,0:T(8,128)(2,1)S(1)} %bitcast.264), channel_id=1, source_target_pairs={{0,1},{1,0},{2,3},{3,2},{4,5},{5,4},{6,7},{7,6},{8,9},{9,8},{10,11... | collective-permute-start | bytes 1966088 | tf_op jit(solution)/shard_map/ppermute | solution.py:502
  189.7 36.4 %collective-permute-start.20 = (bf16[2,2,64,2560]{3,2,1,0:T(8,128)(2,1)}, bf16[2,2,64,2560]{3,2,1,0:T(8,128)(2,1)}, u32[]{:S(2)}, u32[]{:S(2)}) collective-permute-start(bf16[2,2,64,2560]{3,2,1,0:T(8,128)(2,1)} %shard_map.328.rest_2_.refs_0_), channel_id=1, source_target_pairs={{0,1},{1,0},{2,3},{3,2},{4,5},{5,4},{6,7},{7,6},{8,9},{9,8},{10,11... | collective-permute-start | bytes 3932168 | tf_op jit(solution)/shard_map/ppermute | solution.py:502
  193.4 32.6 %collective-permute-start.21 = (bf16[2,2,64,2560]{3,2,1,0:T(8,128)(2,1)}, bf16[2,2,64,2560]{3,2,1,0:T(8,128)(2,1)}, u32[]{:S(2)}, u32[]{:S(2)}) collective-permute-start(bf16[2,2,64,2560]{3,2,1,0:T(8,128)(2,1)} %shard_map.329.rest_3_.refs_2_), channel_id=1, source_target_pairs={{0,16},{8,24},{16,0},{24,8},{1,17},{9,25},{17,1},{25,9},{2,18},{10... | collective-permute-start | bytes 3932168 | tf_op jit(solution)/shard_map/ppermute | solution.py:493
  361.7 26.6 %collective-permute-start.30 = (bf16[512,4096]{1,0:T(8,128)(2,1)}, bf16[512,4096]{1,0:T(8,128)(2,1)}, u32[]{:S(2)}, u32[]{:S(2)}) collective-permute-start(bf16[512,4096]{1,0:T(8,128)(2,1)} %convolution_convert_fusion.1), channel_id=1, source_target_pairs={{0,8},{8,0},{16,24},{24,16},{1,9},{9,1},{17,25},{25,17},{2,10},{10... | collective-permute-start | bytes 12582920 | tf_op jit(solution)/shard_map/ppermute | solution.py:496
  362.7 21.7 %collective-permute-start.31 = (bf16[512,1024]{1,0:T(8,128)(2,1)S(1)}, bf16[512,1024]{1,0:T(8,128)(2,1)}, u32[]{:S(2)}, u32[]{:S(2)}) collective-permute-start(bf16[512,1024]{1,0:T(8,128)(2,1)S(1)} %convolution_convert_fusion.3), channel_id=1, source_target_pairs={{0,8},{8,0},{16,24},{24,16},{1,9},{9,1},{17,25},{25,17},{2,10},{10... | collective-permute-start | bytes 3145736 | tf_op jit(solution)/shard_map/ppermute | solution.py:496
  384.4 47.8 %collective-permute-start.32 = (bf16[512,4096]{1,0:T(8,128)(2,1)}, bf16[512,4096]{1,0:T(8,128)(2,1)}, u32[]{:S(2)}, u32[]{:S(2)}) collective-permute-start(bf16[512,4096]{1,0:T(8,128)(2,1)} %convolution_convert_fusion), channel_id=1, source_target_pairs={{0,8},{8,0},{16,24},{24,16},{1,9},{9,1},{17,25},{25,17},{2,10},{10... | collective-permute-start | bytes 12582920 | tf_op jit(solution)/shard_map/ppermute | solution.py:496
  402.7 48.7 %collective-permute-start.34 = (bf16[128,5120]{1,0:T(8,128)(2,1)}, bf16[128,5120]{1,0:T(8,128)(2,1)}, u32[]{:S(2)}, u32[]{:S(2)}) collective-permute-start(bf16[128,5120]{1,0:T(8,128)(2,1)} %get-tuple-element.82.rest_1_), channel_id=1, source_target_pairs={{0,16},{8,24},{16,0},{24,8},{1,17},{9,25},{17,1},{25,9},{2,18},{10... | collective-permute-start | bytes 3932168 | tf_op jit(solution)/shard_map/ppermute | solution.py:493
  404.7 46.7 %collective-permute-start.35 = (bf16[256,2560]{1,0:T(8,128)(2,1)}, bf16[256,2560]{1,0:T(8,128)(2,1)}, u32[]{:S(2)}, u32[]{:S(2)}) collective-permute-start(bf16[256,2560]{1,0:T(8,128)(2,1)} %get-tuple-element.83.rest_2_), channel_id=1, source_target_pairs={{0,1},{1,0},{2,3},{3,2},{4,5},{5,4},{6,7},{7,6},{8,9},{9,8},{10,11... | collective-permute-start | bytes 3932168 | tf_op jit(solution)/shard_map/ppermute | solution.py:502
  495.6 22.2 %collective-permute-start.39 = (bf16[512,1536]{1,0:T(8,128)(2,1)}, bf16[512,1536]{1,0:T(8,128)(2,1)}, u32[]{:S(2)}, u32[]{:S(2)}) collective-permute-start(bf16[512,1536]{1,0:T(8,128)(2,1)} %fusion.7), channel_id=1, source_target_pairs={{0,8},{8,0},{16,24},{24,16},{1,9},{9,1},{17,25},{25,17},{2,10},{10... | collective-permute-start | bytes 4718600 | tf_op jit(solution)/shard_map/ppermute | solution.py:496
  495.6 17.4 %collective-permute-start.38 = (bf16[2,64,2560]{2,1,0:T(8,128)(2,1)}, bf16[2,64,2560]{2,1,0:T(8,128)(2,1)S(1)}, u32[]{:S(2)}, u32[]{:S(2)}) collective-permute-start(bf16[2,64,2560]{2,1,0:T(8,128)(2,1)} %get-tuple-element.95.rest_2_), channel_id=1, source_target_pairs={{0,2},{2,0},{4,6},{6,4},{1,3},{3,1},{5,7},{7,5},{8,10},{10,8},{12,... | collective-permute-start | bytes 1966088 | tf_op jit(solution)/shard_map/ppermute | solution.py:499
  497.4 49.0 %collective-permute-start.42 = (bf16[128,5120]{1,0:T(8,128)(2,1)}, bf16[128,5120]{1,0:T(8,128)(2,1)}, u32[]{:S(2)}, u32[]{:S(2)}) collective-permute-start(bf16[128,5120]{1,0:T(8,128)(2,1)} %get-tuple-element.85.rest_0_), channel_id=1, source_target_pairs={{0,16},{8,24},{16,0},{24,8},{1,17},{9,25},{17,1},{25,9},{2,18},{10... | collective-permute-start | bytes 3932168 | tf_op jit(solution)/shard_map/ppermute | solution.py:493
  497.8 48.7 %collective-permute-start.43 = (bf16[256,2560]{1,0:T(8,128)(2,1)}, bf16[256,2560]{1,0:T(8,128)(2,1)}, u32[]{:S(2)}, u32[]{:S(2)}) collective-permute-start(bf16[256,2560]{1,0:T(8,128)(2,1)} %get-tuple-element.86.refs_4_.rest_1_), channel_id=1, source_target_pairs={{0,1},{1,0},{2,3},{3,2},{4,5},{5,4},{6,7},{7,6},{8,9},{9,8},{10,11... | collective-permute-start | bytes 3932168 | tf_op jit(solution)/shard_map/ppermute | solution.py:502
  516.0 27.7 %collective-permute-start.62 = (bf16[1,64,2560]{2,1,0:T(8,128)(2,1)}, bf16[1,64,2560]{2,1,0:T(8,128)(2,1)S(1)}, u32[]{:S(2)}, u32[]{:S(2)}) collective-permute-start(bf16[1,64,2560]{2,1,0:T(8,128)(2,1)} %get-tuple-element.99.refs_1_.rest_2_), channel_id=1, source_target_pairs={{0,4},{2,6},{4,0},{6,2},{1,5},{3,7},{5,1},{7,3},{8,12},{10,14},{12... | collective-permute-start | bytes 983048 | tf_op jit(solution)/shard_map/ppermute | solution.py:499
  525.3 25.3 %collective-permute-start.40 = (bf16[256,1536]{1,0:T(8,128)(2,1)}, bf16[256,1536]{1,0:T(8,128)(2,1)}, u32[]{:S(2)}, u32[]{:S(2)}) collective-permute-start(bf16[256,1536]{1,0:T(8,128)(2,1)} %slice.416.rest_3_), channel_id=1, source_target_pairs={{0,16},{8,24},{16,0},{24,8},{1,17},{9,25},{17,1},{25,9},{2,18},{10... | collective-permute-start | bytes 2359304 | tf_op jit(solution)/shard_map/ppermute | solution.py:493
  578.2 30.4 %collective-permute-start.58 = (bf16[128,2560]{1,0:T(8,128)(2,1)}, bf16[128,2560]{1,0:T(8,128)(2,1)}, u32[]{:S(2)}, u32[]{:S(2)}) collective-permute-start(bf16[128,2560]{1,0:T(8,128)(2,1)} %get-tuple-element.104.rest_4_), channel_id=1, source_target_pairs={{0,1},{1,0},{2,3},{3,2},{4,5},{5,4},{6,7},{7,6},{8,9},{9,8},{10,11... | collective-permute-start | bytes 1966088 | tf_op jit(solution)/shard_map/ppermute | solution.py:502
  594.6 25.2 %collective-permute-start.59 = (bf16[128,2560]{1,0:T(8,128)(2,1)}, bf16[128,2560]{1,0:T(8,128)(2,1)}, u32[]{:S(2)}, u32[]{:S(2)}) collective-permute-start(bf16[128,2560]{1,0:T(8,128)(2,1)} %get-tuple-element.105.rest_5_), channel_id=1, source_target_pairs={{0,16},{8,24},{16,0},{24,8},{1,17},{9,25},{17,1},{25,9},{2,18},{10... | collective-permute-start | bytes 1966088 | tf_op jit(solution)/shard_map/ppermute | solution.py:493
  597.9 27.0 %collective-permute-start.46 = (bf16[256,768]{1,0:T(8,128)(2,1)}, bf16[256,768]{1,0:T(8,128)(2,1)S(1)}, u32[]{:S(2)}, u32[]{:S(2)}) collective-permute-start(bf16[256,768]{1,0:T(8,128)(2,1)} %slice.418.rest_3_), channel_id=1, source_target_pairs={{0,16},{8,24},{16,0},{24,8},{1,17},{9,25},{17,1},{25,9},{2,18},{10... | collective-permute-start | bytes 1179656 | tf_op jit(solution)/shard_map/ppermute | solution.py:493
  600.1 23.7 %collective-permute-start.47 = (bf16[256,1536]{1,0:T(8,128)(2,1)}, bf16[256,1536]{1,0:T(8,128)(2,1)}, u32[]{:S(2)}, u32[]{:S(2)}) collective-permute-start(bf16[256,1536]{1,0:T(8,128)(2,1)} %add_convert_fusion.7.refs_1_.rest_2_), channel_id=1, source_target_pairs={{0,1},{1,0},{2,3},{3,2},{4,5},{5,4},{6,7},{7,6},{8,9},{9,8},{10,11... | collective-permute-start | bytes 2359304 | tf_op jit(solution)/shard_map/ppermute | solution.py:502
  606.4 21.9 %collective-permute-start.50 = (bf16[256,768]{1,0:T(8,128)(2,1)S(1)}, bf16[256,768]{1,0:T(8,128)(2,1)}, u32[]{:S(2)}, u32[]{:S(2)}) collective-permute-start(bf16[256,768]{1,0:T(8,128)(2,1)S(1)} %slice.420.rest_1_), channel_id=1, source_target_pairs={{0,16},{8,24},{16,0},{24,8},{1,17},{9,25},{17,1},{25,9},{2,18},{10... | collective-permute-start | bytes 1179656 | tf_op jit(solution)/shard_map/ppermute | solution.py:493
  619.8 54.1 %collective-permute-start.45 = (bf16[640,1024]{1,0:T(8,128)(2,1)S(1)}, bf16[640,1024]{1,0:T(8,128)(2,1)}, u32[]{:S(2)}, u32[]{:S(2)}) collective-permute-start(bf16[640,1024]{1,0:T(8,128)(2,1)S(1)} %copy-done.14), channel_id=1, source_target_pairs={{0,1},{1,0},{2,3},{3,2},{4,5},{5,4},{6,7},{7,6},{8,9},{9,8},{10,11... | collective-permute-start | bytes 3932168 | tf_op jit(solution)/shard_map/ppermute | solution.py:502
  623.8 26.6 %collective-permute-start.60 = (bf16[2,64,2560]{2,1,0:T(8,128)(2,1)}, bf16[2,64,2560]{2,1,0:T(8,128)(2,1)}, u32[]{:S(2)}, u32[]{:S(2)}) collective-permute-start(bf16[2,64,2560]{2,1,0:T(8,128)(2,1)} %get-tuple-element.112), channel_id=1, source_target_pairs={{0,2},{2,0},{4,6},{6,4},{1,3},{3,1},{5,7},{7,5},{8,10},{10,8},{12,... | collective-permute-start | bytes 1966088 | tf_op jit(solution)/shard_map/ppermute | solution.py:499
  (126 other events, 996.5 us)

commit v3 on v2

--- a/solution.py
+++ b/solution.py
@@ -317,6 +317,72 @@
     )(*arrays, *deps)
 
 
+def own_kernel(n_x, tiles, n_deps, la_ref, lb_ref, ra_ref, rb_ref, ga_ref, gb_ref, *rest):
+    rest, (ta_ref, tb_ref) = rest[n_deps:-2], rest[-2:]
+    nears, far_own, far_oth = rest[:n_x], rest[n_x], rest[n_x + 1]
+    t, j = pl.program_id(0), pl.program_id(1)
+    size = ga_ref.shape[0] // n_x
+    half = size // 2
+
+    @pl.when((t == 0) & (j == 0))
+    def _():
+        ta_ref[...] = la_ref[...].astype(F32).T.astype(BF)
+        tb_ref[...] = lb_ref[...].astype(F32).T.astype(BF)
+
+    def run(l_ref, r_ref, g_ref):
+        part = (nn(l_ref[...], r_ref[...]) + g_ref[...].astype(F32)).astype(BF)
+        for x in range(n_x):
+            nears[x][...] = part[x * size : x * size + half]
+
+        @pl.when(t == 0)
+        def _():
+            for x in range(n_x):
+                far_own[pl.ds(x * half, half), :] = part[x * size + half : (x + 1) * size]
+
+        @pl.when(t > 0)
+        def _():
+            for x in range(n_x):
+                far_oth[pl.ds(x * half, half), :] = part[x * size + half : (x + 1) * size]
+
+    @pl.when(j < tiles)
+    def _():
+        run(ta_ref, ra_ref, ga_ref)
+
+    @pl.when(j == tiles)
+    def _():
+        run(tb_ref, rb_ref, gb_ref)
+
+
+def own_parts(n_x, lhs_a, rhs_a, away_a, lhs_b, rhs_b, away_b, deps=()):
+    m = lhs_a.shape[0]
+    k = away_a.shape[0]
+    tile = rhs_b.shape[1] // 2
+    tiles = rhs_a.shape[1] // (2 * tile)
+    cols = (tiles + 1) * tile
+    half = k // (2 * n_x)
+    left = pl.BlockSpec((m, k), lambda t, j: (0, 0))
+    first = lambda n: pl.BlockSpec((n, tile), lambda t, j: (0, t * tiles + jnp.minimum(j, tiles - 1)))
+    second = lambda n: pl.BlockSpec((n, tile), lambda t, j: (0, t))
+    return pl.pallas_call(
+        functools.partial(own_kernel, n_x, tiles, len(deps)),
+        grid=(2, tiles + 1),
+        out_shape=(jax.ShapeDtypeStruct((half, 2 * cols), BF),) * n_x
+        + (jax.ShapeDtypeStruct((n_x * half, cols), BF),) * 2,
+        in_specs=[left, left, first(m), second(m), first(k), second(k)]
+        + [pl.BlockSpec(memory_space=pl.ANY)] * len(deps),
+        out_specs=(pl.BlockSpec((half, tile), lambda t, j: (0, t * (tiles + 1) + j)),) * n_x
+        + (
+            pl.BlockSpec((n_x * half, tile), lambda t, j: (0, jnp.where(t == 0, j, tiles))),
+            pl.BlockSpec((n_x * half, tile), lambda t, j: (0, jnp.where(t == 0, 0, j))),
+        ),
+        scratch_shapes=[pltpu.VMEM((k, m), BF), pltpu.VMEM((k, m), BF)],
+        compiler_params=pltpu.CompilerParams(vmem_limit_bytes=56 * MIB),
+        cost_estimate=pl.CostEstimate(
+            flops=4 * m * k * cols, bytes_accessed=4 * (m + 2 * k) * cols, transcendentals=0
+        ),
+    )(lhs_a, lhs_b, rhs_a, rhs_b, away_a, away_b, *deps)
+
+
 def chunk_of(m):
     return m if m <= 704 else m // 2
 
@@ -761,16 +827,14 @@
 
         q_0 = shard_q[None]
         q_1 = z_go(q_0, z_bits - 1)
-        m_0 = tie(shard_m[None], q_1)
+        q_2, q_3 = z_rest(q_0, q_1)
+        near_q, far_q = z_last(q_2, q_3)
+        m_0 = tie(shard_m[None], near_q)
         m_1 = z_go(m_0, z_bits - 1)
-        q_2, q_3 = z_rest(q_0, q_1)
-        near_q, far_q = z_last(q_2, q_3, (m_1,))
-        e_0 = tie(shard_e[None], m_1)
-        e_1 = z_go(e_0, z_bits - 1)
         near_q, far_q = xy_one(xy_go(near_q, far_q), (rows, aug_q, aug_k))
-        near_m, far_m = z_last(*z_rest(m_0, m_1))
-        h_q = xy_two(xy_two_go(near_q, far_q), (near_m, e_1))
+        h_q = xy_two(xy_two_go(near_q, far_q), (m_1,))
         r_q = pc(h_q)
+        m_2, m_3 = z_rest(m_0, m_1)
         bias_of = lambda b: packed(jnp.concatenate([b[0], jnp.zeros_like(b[0]), b[1]])[None]).reshape(-1)
         qkv_bias = jnp.concatenate([bias_of(b_qv), bias_of(py(b_qv))])
         b_in_r = jnp.concatenate([b_in, py(b_in)])
@@ -778,24 +842,31 @@
         col_scale = jnp.tile(jnp.repeat(jnp.array([scale, 1.0, 1.0], F32), LANES), all_pairs)
         (qkv,) = mm_in(
             rows, h_q, r_q, 0, qkv_half, qkv_half // 3, put_scaled, (eight(qkv_bias, col_scale),),
-            ((half_rows + toks, BF),), deps=(near_m,),
-        )
-        near_m, far_m = xy_one(xy_go(near_m, far_m), (qkv,))
+            ((half_rows + toks, BF),), deps=(m_2,),
+        )
+        near_m, far_m = z_last(m_2, m_3, (qkv,))
+        e_0 = tie(shard_e[None], near_m)
+        e_1 = z_go(e_0, z_bits - 1)
         n_call = all_pairs // 4
         part = lambda i, kept, deps: attend(
             qkv, half_rows, aug_q, aug_k, slots, toks, i * n_call, n_call, kept, deps
         )
-        e_2, e_3 = z_rest(e_0, e_1)
+        going = xy_go(near_m, far_m)
+        kept = part(0, (), (near_m, e_0))
+        near_m, far_m = xy_one(going, (kept[0],))
         going = xy_two_go(near_m, far_m)
-        kept = part(0, (), (near_m, far_m, e_2))
+        e_2 = z_end(e_0, e_1, (kept[0],))
+        for bit in reversed(range(1, z_bits - 1)):
+            e_2 = z_end(e_2, z_go(e_2, bit))
+        e_3 = z_go(e_2, 0)
+        kept = part(1, kept, (near_m, far_m, e_2))
+        kept = part(2, kept, ())
         near_e, far_e = z_last(e_2, e_3, (kept[0],))
-        kept = part(1, kept, (near_e,))
-        kept = part(2, kept, ())
+        going_e = xy_go(near_e, far_e)
+        kept = part(3, kept, (near_e,))
         h_m = xy_two(going, (kept[0],))
         r_m = pc(h_m)
-        kept = part(3, kept, (h_m,))
-        r_m = tie(r_m, kept[0])
-        near_e, far_e = xy_one(xy_go(near_e, far_e), (kept[0],))
+        near_e, far_e = xy_one(going_e, (h_m,))
         ctx, logs = kept
         h_one = mm_out(
             ctx, half_rows, h_m, r_m, ff_half, heads_half, heads_half // 2,
@@ -876,28 +947,31 @@
             branch_low, h_e, r_e, 0, ff_half, ff_half // 4, put_sloped, (slope,),
             ((half_rows, BF), (8, F32)), row_of_zeros, put_sum,
         )
-        part_fin = core_part(branch_low, active, tie(away_fin, inner_low))
-        part_head = core_part(output_low, raw_low, tie(away_head, inner_low))
-        sent_f = p1_send([part_fin, part_head])
+        *near, far_own, far_oth = own_parts(
+            n_x, branch_low, active, away_fin, output_low, raw_low, away_head, (inner_low,)
+        )
+        sent_f = (near, far_own, far_oth)
         got_f = p1_go(sent_f)
         away_in = away_part(normed_low, inner_low)
         normed_grad = mm_out(
             inner_low, half_rows, h_m, r_m, 0, ff_half, heads_half // 2,
             lambda acc, res: acc + res, (h_two_grad,), F32, (sent_f[0][-1], sent_f[2]),
         )
+        state_f = p1_end(sent_f, got_f, (normed_grad,))
+        got_f = p2_go(state_f)
         h_one_grad, g_g1, g_be1 = norm_back(normed_grad, v1, r1, g1)
         g_b_out = jnp.sum(h_one_grad, axis=0)
         attended_low = h_one_grad.astype(BF)
         away_out = away_part(attended_low, ctx)
         (d_ctx,) = mm_in(
-            attended_low, h_m, r_m, ff_half, heads_half, heads_half, put_plain, (), ((half_rows, BF),)
-        )
-        part_in = core_part(normed_low, inner_low, tie(away_in, d_ctx))
-        part_out = core_part(attended_low, ctx, tie(away_out, d_ctx))
-        sent_m = p1_send([part_in, part_out])
+            attended_low, h_m, r_m, ff_half, heads_half, heads_half, put_plain, (), ((half_rows, BF),),
+            deps=(state_f[1], state_f[2][-1]),
+        )
+        *near, far_own, far_oth = own_parts(
+            n_x, normed_low, inner_low, away_in, attended_low, ctx, away_out, (d_ctx,)
+        )
+        sent_m = (near, far_own, far_oth)
         got_m = p1_go(sent_m)
-        state_f = p1_end(sent_f, got_f, (sent_m[2],))
-        got_f = p2_go(state_f)
 
         back = lambda i, kept, deps: attend_back(
             qkv, ctx, d_ctx, logs, aug_k, slots, 2 * toks // 5, scale,
@@ -915,60 +989,77 @@
                 total = add(total, g)
             return total
 
-        kept = back(0, (), (sent_m[0][-1], sent_m[2], state_f[1], state_f[2][-1]))
-        keep_f, give_f = p2_end(state_f, got_f, block, (kept[1],))
+        keep_f, give_f = p2_end(state_f, got_f, block, (sent_m[2],))
         z_f = pz(give_f, 1)
-        kept = back(1, kept, (give_f,))
-        away_1 = away_part(rows, kept[0][:, qkv_half:])
+        kept = back(0, (), (sent_m[0][-1], sent_m[2], give_f))
         keep_f, give_f = z_next(keep_f, z_f, (kept[1],))
         z_f = pz(give_f, 2)
-        part_1 = core_part(rows, kept[0][:, qkv_half:], tie(away_1, give_f))
+        state_m = p1_end(sent_m, got_m, (kept[1],))
+        got_m = p2_go(state_m)
+        kept = back(1, kept, (give_f, state_m[1], state_m[2][-1]))
+        if z_bits == 2:
+            out_f = z_done(keep_f, z_f, (kept[1],))
+        else:
+            out_f = reduce_z_from(*z_next(keep_f, z_f), 2)
+        keep_m, give_m = p2_end(state_m, got_m, block, (kept[1],))
+        z_m = pz(give_m, 1)
+        rows = tie(rows, give_m, out_f)
+        away_1 = away_part(rows, kept[0][:, qkv_half:])
+        part_1 = core_part(rows, kept[0][:, qkv_half:], away_1)
         sent_1 = x_blocks(part_1)
         got_1 = x_go(sent_1)
-        kept = back(2, kept, (give_f, sent_1[1]))
-        state_m = p1_end(sent_m, got_m, (kept[1],))
+        kept = back(2, kept, (sent_1[1], give_m))
+        keep_m, give_m = z_next(keep_m, z_m, (kept[1],))
+        z_m = pz(give_m, 2)
+        rows = tie(rows, give_m)
         away_2 = away_part(rows, columns(kept[0], 0))
-        got_m = p2_go(state_m)
         y_1 = x_end(sent_1, [tie(g, kept[1]) for g in got_1])
         part_2 = core_part(rows, columns(kept[0], 0), tie(away_2, y_1))
         sent_2 = x_blocks(part_2)
         got_2 = x_go(sent_2)
-        if z_bits == 2:
-            out_f = z_done(keep_f, z_f, (kept[1],))
-        else:
-            out_f = reduce_z_from(*z_next(keep_f, z_f), 2)
-        kept = back(3, kept, (y_1, sent_2[1], state_m[1], state_m[2][-1]))
+        g_w_fin, g_head = out_f[:, :ff_half], out_f[:, ff_half:]
+        n_h = block // n_ta
+        head_keep = jnp.where(first_t, g_head[:n_h], g_head[n_h:])
+        head_got = py(jnp.where(first_t, g_head[n_h:], g_head[:n_h]))
+        kept = back(3, kept, (y_1, sent_2[1], give_m))
+        head_got = tie(head_got, kept[1])
         d_qkv, sums_qv = kept
         y_1 = py(y_1)
+        if z_bits == 2:
+            out_m = z_done(keep_m, z_m, (sums_qv,))
+        else:
+            out_m = reduce_z_from(*z_next(keep_m, z_m), 2)
+        y_1 = tie(y_1, sums_qv)
+        rows = tie(rows, y_1, out_m, head_got)
         away_3 = away_part(rows, columns(d_qkv, 1))
         to_other = mm_out(
             d_qkv, toks, h_q, r_q, 0, qkv_half, heads_half // 2, lambda acc: acc, (), BF,
             (away_3,), row=half_rows,
         )
+        to_other_part = to_other
         d_qkv = tie(d_qkv, to_other)
-        sums_qv = tie(sums_qv, to_other)
         part_3 = core_part(rows, columns(d_qkv, 1), away_3)
         sent_3 = x_blocks(part_3)
         got_3 = x_go(sent_3)
         to_other = py(to_other)
-        keep_m, give_m = p2_end(state_m, got_m, block, (sums_qv,))
-        out_m = reduce_z_from(keep_m, give_m, 0)
-        y_1 = tie(y_1, sums_qv)
-        got_2 = [tie(g, sums_qv) for g in got_2]
+        q_2 = add(x_end(sent_2, [tie(g, to_other_part) for g in got_2]), y_1[:, :quarter]).reshape(n_pa, block, -1)
         grad_rows = mm_out(
             d_qkv, half_rows, h_q, r_q, 0, qkv_half, heads_half // 2,
-            lambda acc, res: acc + res, (h_one_grad,), F32, (sent_3[1],),
-        )
-        as_z = lambda a: a.reshape(n_pa, block, -1)
-        out_2 = reduce_z(as_z(add(x_end(sent_2, got_2), y_1[:, :quarter])))
-        out_3 = reduce_z(as_z(add(x_end(sent_3, got_3), y_1[:, quarter:])))
-        out_q = jnp.concatenate([out_2, out_3], axis=1)
+            lambda acc, res: acc + res, (h_one_grad,), F32, (sent_3[1], q_2),
+        )
+        to_other = tie(to_other, grad_rows)
+        got_3 = [tie(g, grad_rows) for g in got_3]
+        q_3 = add(x_end(sent_3, got_3), y_1[:, quarter:]).reshape(n_pa, block, -1)
+        keep_q, give_q = z_split(jnp.concatenate([q_2, q_3], axis=2))
+        keep_q, give_q = z_split(add(keep_q, pz(give_q, 1)))
+        to_other, keep_q = tie(to_other, give_q), tie(keep_q, to_other)
+        sums_qv = tie(sums_qv, to_other)
+        if z_bits == 2:
+            out_q = (keep_q.astype(F32) + pz(give_q, 2).astype(F32))[0]
+        else:
+            out_q = reduce_z_from(*z_next(keep_q, pz(give_q, 2)), 2)
         g_w_qkv = out_q.reshape(block, pairs, 3, LANES).transpose(2, 0, 1, 3).reshape(3, block, heads_half)
-        g_w_fin, g_head = out_f[:, :ff_half], out_f[:, ff_half:]
         g_w_in, g_w_out = out_m[:, :ff_half], out_m[:, ff_half:]
-        n_h = block // n_ta
-        head_keep = jnp.where(first_t, g_head[:n_h], g_head[n_h:])
-        head_got = py(jnp.where(first_t, g_head[n_h:], g_head[:n_h]))
         g_w_head = in_order(jnp.concatenate([head_keep, head_got], axis=1))
         grad_rows = permute(
             grad_rows, back_info, (half_rows,), block, low_bits, slots, (to_other,)

time: 689 us -> 677 us (0.983)
  matrix products: 73.9 us -> 47.9 us
  Pallas kernels: 292 us -> 308 us
  waiting for transfers between devices: 143 us -> 133 us
    ppermute x20 -> x18, waiting for transfers between devices: 102 us -> 62.7 us  [pz(): return lax.ppermute(v, 'pa', [(i, i ^ k) for i in range(n_pa)])]
    pallas_call x0 -> x2, Pallas kernels: none -> 26.3 us  [own_parts(): pl.pallas_call(functools.partial(own_kernel, n_x, tiles, len(deps)), grid...]
    dot_general x15 -> x11, matrix products: 67.5 us -> 41.6 us  [tn(): lax.dot_general(a, b, (((0,), (0,)), ((), ())), preferred_element_type=F32)]
    ppermute x19, waiting for transfers between devices: 26 us -> 39.8 us  [py(): return lax.ppermute(v, 'ta', [(i, i ^ 1) for i in range(n_ta)])]
    ppermute x14, waiting for transfers between devices: 7.7 us -> 20.5 us  [px(): return lax.ppermute(v, 'pb', [(i, i ^ cores * k) for i in range(n_pb)])]
    pallas_call x19 -> x17, Pallas kernels: 53 us -> 42.8 us  [assemble(): pl.pallas_call(functools.partial(assemble_kernel, len(arrays), len(deps),...]
    unnamed x193 -> x245, local copies, waits for them, and re-layouts: 29.8 us -> 36.5 us
    ppermute x20 -> x18, starting transfers between devices: 31.4 us -> 34.3 us  [pz(): return lax.ppermute(v, 'pa', [(i, i ^ k) for i in range(n_pa)])]
  transfers between devices with their start and end apart: 64 -> 62, of which waited for: 25 -> 25; matrix products, arithmetic and copies ran while one was open for 14% -> 11% of each run, Pallas kernels for 31% -> 39%
where the time goes in v3:
time: 677 us; the launch traced here: 666 us
  Pallas kernels  308 us (45%)
  waiting for transfers between devices  133 us (20%)
  starting transfers between devices  69.7 us (10%)
  local copies, waits for them, and re-layouts  57.7 us (9%)
  matrix products  47.9 us (7%)
  other arithmetic  47.3 us (7%)
    ppermute x18, waiting for transfers between devices, pz(): return lax.ppermute(v, 'pa', [(i, i ^ k) for i in range(n_pa)])  62.7 us
    pallas_call x6, Pallas kernels, mm_out(): pl.pallas_call(functools.partial(mm_out_kernel, chunk_of(m), half, len(ex...  57.7 us
    pallas_call x5, Pallas kernels, mm_in(): pl.pallas_call(functools.partial(mm_in_kernel, chunk_of(m), epilogue, sta...  57.5 us
    pallas_call x4, Pallas kernels, attend_back(): pl.pallas_call(functools.partial(attend_back_kernel, slots, tile_k, scale...  51 us
    pallas_call x17, Pallas kernels, assemble(): pl.pallas_call(functools.partial(assemble_kernel, len(arrays), len(deps),...  42.8 us
    dot_general x11, matrix products, tn(): lax.dot_general(a, b, (((0,), (0,)), ((), ())), preferred_element_type=F32)  41.6 us
    ppermute x19, waiting for transfers between devices, py(): return lax.ppermute(v, 'ta', [(i, i ^ 1) for i in range(n_ta)])  39.8 us
    pallas_call x4, Pallas kernels, attend(): pl.pallas_call(functools.partial(attend_kernel, slots, tile_q, len(deps))...  38 us
  transfers between devices with their start and end apart: 62, of which 25 were waited for; matrix products, arithmetic and copies ran while one was open for 11% of the time, Pallas kernels for 39%

profile of v3, /device:TPU:0, one launch (start us, length us, event | category | flops | bytes accessed | tf_op | source)
XLA Modules:
  0.0 666.3 jit_solution(6871915220059941652)
XLA Ops:
  7.1 8.2 %collective-permute-done.refs_1_ = bf16[1,64,1536]{2,1,0:T(8,128)(2,1)S(1)} collective-permute-done((bf16[1,64,1536]{2,1,0:T(8,128)(2,1)S(1)}, bf16[1,64,1536]{2,1,0:T(8,128)(2,1)S(1)}, u32[]{:S(2)}, u32[]{:S(2)}) %collective-permute-start) | collective-permute-done | bytes 196640 | tf_op jit(solution)/shard_map/ppermute | solution.py:565
  19.5 8.9 %collective-permute-done.1.refs_1_ = bf16[2,64,1536]{2,1,0:T(8,128)(2,1)S(1)} collective-permute-done((bf16[2,64,1536]{2,1,0:T(8,128)(2,1)}, bf16[2,64,1536]{2,1,0:T(8,128)(2,1)S(1)}, u32[]{:S(2)}, u32[]{:S(2)}) %collective-permute-start.1) | collective-permute-done | bytes 393248 | tf_op jit(solution)/shard_map/ppermute | solution.py:565
  54.6 13.1 %collective-permute-done.6.refs_4_.refs_1_ = bf16[1,64,2560]{2,1,0:T(8,128)(2,1)S(1)} collective-permute-done((bf16[1,64,2560]{2,1,0:T(8,128)(2,1)}, bf16[1,64,2560]{2,1,0:T(8,128)(2,1)S(1)}, u32[]{:S(2)}, u32[]{:S(2)}) %collective-permute-start.6) | collective-permute-done | bytes 327712 | tf_op jit(solution)/shard_map/ppermute | solution.py:565
  81.8 14.5 %shard_map.314.refs_2_.q_ref.k_ref.v_ref = bf16[1344,3072]{1,0:T(8,128)(2,1)} custom-call(bf16[1344,1024]{1,0:T(8,128)(2,1)} %shard_map.306.refs_2_.a_ref.rest_0_.refs_0_, bf16[1024,1536]{1,0:T(8,128)(2,1)} %bitcast.205, bf16[1024,1536]{1,0:T(8,128)(2,1)} %copy-done.11, f32[8,3072]{1,0:T(8,128)} %maximum_maximum_fusion.3.rest_0_, bf16[2,64,2560]{2,1,0:T(8,128)(2,1)} %bitcast.229), custom_call_target="tpu_custom_call" | custom-call | flops 8455716864 | bytes 17301504 | tf_op jit(solution)/shard_map/pallas_call | solution.py:416
  105.7 9.5 %shard_map.317 = (bf16[704,1024]{1,0:T(8,128)(2,1)}, bf16[704,1024]{1,0:T(8,128)(2,1)}) custom-call(bf16[1344,3072]{1,0:T(8,128)(2,1)} %shard_map.314.refs_2_.q_ref.k_ref.v_ref, bf16[1344,3072]{1,0:T(8,128)(2,1)} %shard_map.314.refs_2_.q_ref.k_ref.v_ref, bf16[1344,3072]{1,0:T(8,128)(2,1)} %shard_map.314.refs_2_.q_ref.k_ref.v_ref, ...), custom_call_target="tpu_custom_call" | custom-call | flops 3875536896 | bytes 2457600 | tf_op jit(solution)/shard_map/pallas_call | solution.py:135
  128.1 9.4 %shard_map.321 = (bf16[704,1024]{1,0:T(8,128)(2,1)}, bf16[704,1024]{1,0:T(8,128)(2,1)}) custom-call(bf16[1344,3072]{1,0:T(8,128)(2,1)} %shard_map.314.refs_2_.q_ref.k_ref.v_ref, bf16[1344,3072]{1,0:T(8,128)(2,1)} %shard_map.314.refs_2_.q_ref.k_ref.v_ref, ...), custom_call_target="tpu_custom_call", output_to_operand_aliasing={{0}: (5, {}), {1}: (6, {})} | custom-call | flops 3875536896 | bytes 2457600 | tf_op jit(solution)/shard_map/pallas_call | solution.py:135
  137.5 9.7 %shard_map.322 = (bf16[704,1024]{1,0:T(8,128)(2,1)}, bf16[704,1024]{1,0:T(8,128)(2,1)}) custom-call(bf16[1344,3072]{1,0:T(8,128)(2,1)} %shard_map.314.refs_2_.q_ref.k_ref.v_ref, bf16[1344,3072]{1,0:T(8,128)(2,1)} %shard_map.314.refs_2_.q_ref.k_ref.v_ref, ...), custom_call_target="tpu_custom_call", output_to_operand_aliasing={{0}: (5, {}), {1}: (6, {})} | custom-call | flops 3875536896 | bytes 2457600 | tf_op jit(solution)/shard_map/pallas_call | solution.py:135
  150.4 9.5 %shard_map.324 = (bf16[704,1024]{1,0:T(8,128)(2,1)}, bf16[704,1024]{1,0:T(8,128)(2,1)}) custom-call(bf16[1344,3072]{1,0:T(8,128)(2,1)} %shard_map.314.refs_2_.q_ref.k_ref.v_ref, bf16[1344,3072]{1,0:T(8,128)(2,1)} %shard_map.314.refs_2_.q_ref.k_ref.v_ref, ...), custom_call_target="tpu_custom_call", output_to_operand_aliasing={{0}: (5, {}), {1}: (6, {})} | custom-call | flops 3875536896 | bytes 2457600 | tf_op jit(solution)/shard_map/pallas_call | solution.py:135
  174.6 9.8 %collective-permute-done.19 = f32[2048]{0:T(1024)S(1)} collective-permute-done((f32[2048]{0:T(1024)S(1)}, f32[2048]{0:T(1024)S(1)}, u32[]{:S(2)}, u32[]{:S(2)}) %collective-permute-start.19) | collective-permute-done | bytes 8224 | tf_op jit(solution)/shard_map/ppermute | solution.py:568
  193.6 6.0 shard_map.329
  205.4 20.2 %shard_map.330 = (bf16[704,4096]{1,0:T(8,128)(2,1)}, bf16[704,4096]{1,0:T(8,128)(2,1)}) custom-call(bf16[704,1024]{1,0:T(8,128)(2,1)} %get-tuple-element.138.a_ref.la_ref, bf16[1024,2560]{1,0:T(8,128)(2,1)} %bitcast.191, bf16[1024,2560]{1,0:T(8,128)(2,1)} %collective-permute-done.16.r0_ref.r1_ref.r_ref, f32[8,4096]{1,0:T(8,128)} %concatenate.101.rest_0_), custom_call_target="tpu_custom_call" | custom-call | flops 5905580032 | bytes 21364736 | tf_op jit(solution)/shard_map/pallas_call | solution.py:416
  232.5 7.0 %collective-permute-done.22.r0_ref.r1_ref.r_ref = bf16[1024,2560]{1,0:T(8,128)(2,1)} collective-permute-done((bf16[1024,2560]{1,0:T(8,128)(2,1)}, bf16[1024,2560]{1,0:T(8,128)(2,1)}, u32[]{:S(2)}, u32[]{:S(2)}) %collective-permute-start.22) | collective-permute-done | bytes 5242912 | tf_op jit(solution)/shard_map/ppermute | solution.py:562
  239.6 12.8 %shard_map.332 = f32[704,1024]{1,0:T(8,128)} custom-call(bf16[704,4096]{1,0:T(8,128)(2,1)} %get-tuple-element.79.refs_4_.a0_ref.a1_ref.ra_ref, bf16[704,4096]{1,0:T(8,128)(2,1)} %get-tuple-element.79.refs_4_.a0_ref.a1_ref.ra_ref, bf16[1024,2560]{1,0:T(8,128)(2,1)} %bitcast.196, bf16[1024,2560]{1,0:T(8,128)(2,1)} %bitcast.197, ...), custom_call_target="tpu_custom_call" | custom-call | flops 5905580032 | bytes 17039360 | tf_op jit(solution)/shard_map/pallas_call | solution.py:467
  271.1 6.0 collective-permute-done.23.refs_1_
  280.5 6.9 %collective-permute-done.24.refs_1_ = bf16[2,64,1024]{2,1,0:T(8,128)(2,1)S(1)} collective-permute-done((bf16[2,64,1024]{2,1,0:T(8,128)(2,1)}, bf16[2,64,1024]{2,1,0:T(8,128)(2,1)S(1)}, u32[]{:S(2)}, u32[]{:S(2)}) %collective-permute-start.24) | collective-permute-done | bytes 262176 | tf_op jit(solution)/shard_map/ppermute | solution.py:565
  291.8 10.8 %collective-permute-done.25 = bf16[256,1024]{1,0:T(8,128)(2,1)S(1)} collective-permute-done((bf16[256,1024]{1,0:T(8,128)(2,1)}, bf16[256,1024]{1,0:T(8,128)(2,1)S(1)}, u32[]{:S(2)}, u32[]{:S(2)}) %collective-permute-start.25) | collective-permute-done | bytes 524320 | tf_op jit(solution)/shard_map/ppermute | solution.py:568
  315.7 9.5 %collective-permute-done.27 = bf16[256,1024]{1,0:T(8,128)(2,1)S(1)} collective-permute-done((bf16[256,1024]{1,0:T(8,128)(2,1)S(1)}, bf16[256,1024]{1,0:T(8,128)(2,1)S(1)}, u32[]{:S(2)}, u32[]{:S(2)}) %collective-permute-start.27) | collective-permute-done | bytes 524320 | tf_op jit(solution)/shard_map/ppermute | solution.py:568
  344.6 6.2 shard_map.336
  367.2 13.5 %shard_map.337 = (bf16[704,4096]{1,0:T(8,128)(2,1)}, f32[8,4096]{1,0:T(8,128)}) custom-call(bf16[704,1024]{1,0:T(8,128)(2,1)} %copy-done.22, bf16[1024,2560]{1,0:T(8,128)(2,1)} %bitcast.201, bf16[1024,2560]{1,0:T(8,128)(2,1)} %collective-permute-done.22.r0_ref.r1_ref.r_ref, bf16[704,4096]{1,0:T(8,128)(2,1)} %get-tuple-element.80.rest_0_), custom_call_target="tpu_custom_call" | custom-call | flops 5905580032 | bytes 15663104 | tf_op jit(solution)/shard_map/pallas_call | solution.py:416
  380.7 7.7 %convolution_convert_fusion = bf16[512,4096]{1,0:T(8,128)(2,1)} fusion(bf16[704,4096]{1,0:T(8,128)(2,1)} %get-tuple-element.81.rest_0_.a0_ref.a1_ref.ra_ref, bf16[704,1024]{1,0:T(8,128)(2,1)S(1)} %copy-done.21), kind=kOutput, calls=%fused_computation.3 | convolution fusion | flops 2954887168 | bytes 10682368 | tf_op jit(solution)/shard_map/dot_general | solution.py:32
  389.4 13.2 %shard_map.338 = (bf16[128,5120]{1,0:T(8,128)(2,1)}, bf16[128,5120]{1,0:T(8,128)(2,1)}, bf16[256,2560]{1,0:T(8,128)(2,1)}, bf16[256,2560]{1,0:T(8,128)(2,1)}) custom-call(bf16[704,1024]{1,0:T(8,128)(2,1)} %copy-done.22, bf16[704,1024]{1,0:T(8,128)(2,1)} %add_convert_fusion.a_ref.lb_ref, bf16[704,4096]{1,0:T(8,128)(2,1)} %get-tuple-element.79.refs_4_.a0_ref.a1_ref.ra_ref, ...), custom_call_target="tpu_custom_call" | custom-call | flops 3690987520 | bytes 17694720 | tf_op jit(solution)/shard_map/pallas_call | solution.py:366
  404.9 12.7 %shard_map.339.refs_4_ = f32[704,1024]{1,0:T(8,128)} custom-call(bf16[704,4096]{1,0:T(8,128)(2,1)} %get-tuple-element.81.rest_0_.a0_ref.a1_ref.ra_ref, bf16[704,4096]{1,0:T(8,128)(2,1)} %get-tuple-element.81.rest_0_.a0_ref.a1_ref.ra_ref, bf16[1024,2560]{1,0:T(8,128)(2,1)} %bitcast.192, bf16[1024,2560]{1,0:T(8,128)(2,1)} %bitcast.193, ...), custom_call_target="tpu_custom_call" | custom-call | flops 5905580032 | bytes 17039360 | tf_op jit(solution)/shard_map/pallas_call | solution.py:467
  426.0 8.0 %collective-permute-done.32.refs_1_ = bf16[128,5120]{1,0:T(8,128)(2,1)S(1)} collective-permute-done((bf16[128,5120]{1,0:T(8,128)(2,1)}, bf16[128,5120]{1,0:T(8,128)(2,1)S(1)}, u32[]{:S(2)}, u32[]{:S(2)}) %collective-permute-start.32) | collective-permute-done | bytes 1310752 | tf_op jit(solution)/shard_map/ppermute | solution.py:559
  447.2 13.2 %shard_map.342 = (bf16[128,5120]{1,0:T(8,128)(2,1)}, bf16[128,5120]{1,0:T(8,128)(2,1)}, bf16[256,2560]{1,0:T(8,128)(2,1)}, bf16[256,2560]{1,0:T(8,128)(2,1)}) custom-call(bf16[704,1024]{1,0:T(8,128)(2,1)} %get-tuple-element.138.a_ref.la_ref, bf16[704,1024]{1,0:T(8,128)(2,1)} %copy-done.17, bf16[704,4096]{1,0:T(8,128)(2,1)} %get-tuple-element.81.rest_0_.a0_ref.a1_ref.ra_ref, ...), custom_call_target="tpu_custom_call" | custom-call | flops 3690987520 | bytes 17694720 | tf_op jit(solution)/shard_map/pallas_call | solution.py:366
  466.6 12.6 %shard_map.344 = (bf16[1344,3072]{1,0:T(8,128)(2,1)}, f32[8,1024]{1,0:T(8,128)}) custom-call(bf16[1344,3072]{1,0:T(8,128)(2,1)} %shard_map.314.refs_2_.q_ref.k_ref.v_ref, bf16[1344,3072]{1,0:T(8,128)(2,1)} %shard_map.314.refs_2_.q_ref.k_ref.v_ref, bf16[1344,3072]{1,0:T(8,128)(2,1)} %shard_map.314.refs_2_.q_ref.k_ref.v_ref, ...), custom_call_target="tpu_custom_call" | custom-call | flops 9688842240 | bytes 4915200 | tf_op jit(solution)/shard_map/pallas_call | solution.py:228
  479.1 11.2 %collective-permute-done.39.refs_1_ = bf16[128,5120]{1,0:T(8,128)(2,1)S(1)} collective-permute-done((bf16[128,5120]{1,0:T(8,128)(2,1)}, bf16[128,5120]{1,0:T(8,128)(2,1)S(1)}, u32[]{:S(2)}, u32[]{:S(2)}) %collective-permute-start.39) | collective-permute-done | bytes 1310752 | tf_op jit(solution)/shard_map/ppermute | solution.py:559
  503.4 12.8 %shard_map.347 = (bf16[1344,3072]{1,0:T(8,128)(2,1)}, f32[8,1024]{1,0:T(8,128)}) custom-call(bf16[1344,3072]{1,0:T(8,128)(2,1)} %shard_map.314.refs_2_.q_ref.k_ref.v_ref, bf16[1344,3072]{1,0:T(8,128)(2,1)} %shard_map.314.refs_2_.q_ref.k_ref.v_ref, ...), custom_call_target="tpu_custom_call", output_to_operand_aliasing={{0}: (7, {}), {1}: (8, {})} | custom-call | flops 9688842240 | bytes 4915200 | tf_op jit(solution)/shard_map/pallas_call | solution.py:228
  538.6 13.0 %shard_map.351 = (bf16[1344,3072]{1,0:T(8,128)(2,1)}, f32[8,1024]{1,0:T(8,128)}) custom-call(bf16[1344,3072]{1,0:T(8,128)(2,1)} %shard_map.314.refs_2_.q_ref.k_ref.v_ref, bf16[1344,3072]{1,0:T(8,128)(2,1)} %shard_map.314.refs_2_.q_ref.k_ref.v_ref, ...), custom_call_target="tpu_custom_call", output_to_operand_aliasing={{0}: (7, {}), {1}: (8, {})} | custom-call | flops 9688842240 | bytes 4915200 | tf_op jit(solution)/shard_map/pallas_call | solution.py:228
  571.3 12.7 %shard_map.356 = (bf16[1344,3072]{1,0:T(8,128)(2,1)}, f32[8,1024]{1,0:T(8,128)}) custom-call(bf16[1344,3072]{1,0:T(8,128)(2,1)} %shard_map.314.refs_2_.q_ref.k_ref.v_ref, bf16[1344,3072]{1,0:T(8,128)(2,1)} %shard_map.314.refs_2_.q_ref.k_ref.v_ref, ...), custom_call_target="tpu_custom_call", output_to_operand_aliasing={{0}: (7, {}), {1}: (8, {})} | custom-call | flops 9688842240 | bytes 4915200 | tf_op jit(solution)/shard_map/pallas_call | solution.py:228
  595.1 9.3 %shard_map.361.refs_1_ = bf16[640,1024]{1,0:T(8,128)(2,1)} custom-call(bf16[1344,3072]{1,0:T(8,128)(2,1)} %get-tuple-element.112.a0_ref.a1_ref.refs_0_, bf16[1344,3072]{1,0:T(8,128)(2,1)} %get-tuple-element.112.a0_ref.a1_ref.refs_0_, bf16[1024,1536]{1,0:T(8,128)(2,1)} %bitcast.206, bf16[1024,1536]{1,0:T(8,128)(2,1)} %bitcast.207, ...), custom_call_target="tpu_custom_call" | custom-call | flops 4026531840 | bytes 12845056 | tf_op jit(solution)/shard_map/pallas_call | solution.py:467
  613.5 10.7 %shard_map.364.refs_1_.x_ref = f32[704,1024]{1,0:T(8,128)} custom-call(bf16[1344,3072]{1,0:T(8,128)(2,1)} %shard_map.362.a0_ref.a1_ref, bf16[1344,3072]{1,0:T(8,128)(2,1)} %shard_map.362.a0_ref.a1_ref, bf16[1024,1536]{1,0:T(8,128)(2,1)} %bitcast.208, bf16[1024,1536]{1,0:T(8,128)(2,1)} %bitcast.209, bf16[1024,1536]{1,0:T(8,128)(2,1)} %copy-done.11, ...), custom_call_target="tpu_custom_call" | custom-call | flops 4429185024 | bytes 13500416 | tf_op jit(solution)/shard_map/pallas_call | solution.py:467
  631.7 7.3 %collective-permute-done.55 = bf16[2,64,1536]{2,1,0:T(8,128)(2,1)S(1)} collective-permute-done((bf16[2,64,1536]{2,1,0:T(8,128)(2,1)S(1)}, bf16[2,64,1536]{2,1,0:T(8,128)(2,1)S(1)}, u32[]{:S(2)}, u32[]{:S(2)}) %collective-permute-start.55) | collective-permute-done | bytes 393248 | tf_op jit(solution)/shard_map/ppermute | solution.py:565
  (568 shorter events, 328.0 us)
Async XLA Ops:
  44.9 22.8 %collective-permute-start.3 = (bf16[2,2,64,1536]{3,2,1,0:T(8,128)(2,1)}, bf16[2,2,64,1536]{3,2,1,0:T(8,128)(2,1)S(1)}, u32[]{:S(2)}, u32[]{:S(2)}) collective-permute-start(bf16[2,2,64,1536]{3,2,1,0:T(8,128)(2,1)} %shard_map.309.refs_0_), channel_id=1, source_target_pairs={{0,1},{1,0},{2,3},{3,2},{4,5},{5,4},{6,7},{7,6},{8,9},{9,8},{10,11... | collective-permute-start | bytes 2359304 | tf_op jit(solution)/shard_map/ppermute | solution.py:568
  48.2 19.5 %collective-permute-start.5 = (bf16[2,2,64,1536]{3,2,1,0:T(8,128)(2,1)}, bf16[2,2,64,1536]{3,2,1,0:T(8,128)(2,1)S(1)}, u32[]{:S(2)}, u32[]{:S(2)}) collective-permute-start(bf16[2,2,64,1536]{3,2,1,0:T(8,128)(2,1)} %shard_map.310.refs_2_), channel_id=1, source_target_pairs={{0,16},{8,24},{16,0},{24,8},{1,17},{9,25},{17,1},{25,9},{2,18},{10... | collective-permute-start | bytes 2359304 | tf_op jit(solution)/shard_map/ppermute | solution.py:559
  100.1 19.2 %collective-permute-start.11 = (bf16[2,64,2560]{2,1,0:T(8,128)(2,1)}, bf16[2,64,2560]{2,1,0:T(8,128)(2,1)S(1)}, u32[]{:S(2)}, u32[]{:S(2)}) collective-permute-start(bf16[2,64,2560]{2,1,0:T(8,128)(2,1)} %bitcast.245), channel_id=1, source_target_pairs={{0,1},{1,0},{2,3},{3,2},{4,5},{5,4},{6,7},{7,6},{8,9},{9,8},{10,11... | collective-permute-start | bytes 1966088 | tf_op jit(solution)/shard_map/ppermute | solution.py:568
  102.4 21.7 %collective-permute-start.12 = (bf16[1,64,2560]{2,1,0:T(8,128)(2,1)}, bf16[1,64,2560]{2,1,0:T(8,128)(2,1)S(1)}, u32[]{:S(2)}, u32[]{:S(2)}) collective-permute-start(bf16[1,64,2560]{2,1,0:T(8,128)(2,1)} %shard_map.316.rest_1_.refs_0_), channel_id=1, source_target_pairs={{0,4},{2,6},{4,0},{6,2},{1,5},{3,7},{5,1},{7,3},{8,12},{10,14},{12... | collective-permute-start | bytes 983048 | tf_op jit(solution)/shard_map/ppermute | solution.py:565
  118.7 41.2 %collective-permute-start.14 = (bf16[2,2,64,2560]{3,2,1,0:T(8,128)(2,1)}, bf16[2,2,64,2560]{3,2,1,0:T(8,128)(2,1)S(1)}, u32[]{:S(2)}, u32[]{:S(2)}) collective-permute-start(bf16[2,2,64,2560]{3,2,1,0:T(8,128)(2,1)} %shard_map.318.rest_2_.refs_0_), channel_id=1, source_target_pairs={{0,1},{1,0},{2,3},{3,2},{4,5},{5,4},{6,7},{7,6},{8,9},{9,8},{10,11... | collective-permute-start | bytes 3932168 | tf_op jit(solution)/shard_map/ppermute | solution.py:568
  122.6 37.3 %collective-permute-start.15 = (bf16[2,2,64,2560]{3,2,1,0:T(8,128)(2,1)}, bf16[2,2,64,2560]{3,2,1,0:T(8,128)(2,1)S(1)}, u32[]{:S(2)}, u32[]{:S(2)}) collective-permute-start(bf16[2,2,64,2560]{3,2,1,0:T(8,128)(2,1)} %shard_map.319.rest_3_.refs_2_), channel_id=1, source_target_pairs={{0,16},{8,24},{16,0},{24,8},{1,17},{9,25},{17,1},{25,9},{2,18},{10... | collective-permute-start | bytes 3932168 | tf_op jit(solution)/shard_map/ppermute | solution.py:559
  126.8 20.4 %collective-permute-start.13 = (bf16[2,64,2560]{2,1,0:T(8,128)(2,1)}, bf16[2,64,2560]{2,1,0:T(8,128)(2,1)S(1)}, u32[]{:S(2)}, u32[]{:S(2)}) collective-permute-start(bf16[2,64,2560]{2,1,0:T(8,128)(2,1)} %bitcast.223), channel_id=1, source_target_pairs={{0,2},{2,0},{4,6},{6,4},{1,3},{3,1},{5,7},{7,5},{8,10},{10,8},{12,... | collective-permute-start | bytes 1966088 | tf_op jit(solution)/shard_map/ppermute | solution.py:565
  166.4 27.2 %collective-permute-start.16 = (bf16[1024,2560]{1,0:T(8,128)(2,1)}, bf16[1024,2560]{1,0:T(8,128)(2,1)}, u32[]{:S(2)}, u32[]{:S(2)}) collective-permute-start(bf16[1024,2560]{1,0:T(8,128)(2,1)} %bitcast.186), channel_id=1, source_target_pairs={{0,8},{8,0},{16,24},{24,16},{1,9},{9,1},{17,25},{25,17},{2,10},{10... | collective-permute-start | bytes 15728648 | tf_op jit(solution)/shard_map/ppermute | solution.py:562
  166.5 18.5 %collective-permute-start.17 = (bf16[2,64,2560]{2,1,0:T(8,128)(2,1)S(1)}, bf16[2,64,2560]{2,1,0:T(8,128)(2,1)S(1)}, u32[]{:S(2)}, u32[]{:S(2)}) collective-permute-start(bf16[2,64,2560]{2,1,0:T(8,128)(2,1)S(1)} %bitcast.233), channel_id=1, source_target_pairs={{0,16},{8,24},{16,0},{24,8},{1,17},{9,25},{17,1},{25,9},{2,18},{10... | collective-permute-start | bytes 1966088 | tf_op jit(solution)/shard_map/ppermute | solution.py:559
  167.4 22.5 %collective-permute-start.18 = (bf16[2,64,2560]{2,1,0:T(8,128)(2,1)S(1)}, bf16[2,64,2560]{2,1,0:T(8,128)(2,1)S(1)}, u32[]{:S(2)}, u32[]{:S(2)}) collective-permute-start(bf16[2,64,2560]{2,1,0:T(8,128)(2,1)S(1)} %bitcast.248), channel_id=1, source_target_pairs={{0,1},{1,0},{2,3},{3,2},{4,5},{5,4},{6,7},{7,6},{8,9},{9,8},{10,11... | collective-permute-start | bytes 1966088 | tf_op jit(solution)/shard_map/ppermute | solution.py:568
  188.2 37.4 %collective-permute-start.20 = (bf16[2,2,64,2560]{3,2,1,0:T(8,128)(2,1)}, bf16[2,2,64,2560]{3,2,1,0:T(8,128)(2,1)}, u32[]{:S(2)}, u32[]{:S(2)}) collective-permute-start(bf16[2,2,64,2560]{3,2,1,0:T(8,128)(2,1)} %shard_map.327.rest_2_.refs_0_), channel_id=1, source_target_pairs={{0,1},{1,0},{2,3},{3,2},{4,5},{5,4},{6,7},{7,6},{8,9},{9,8},{10,11... | collective-permute-start | bytes 3932168 | tf_op jit(solution)/shard_map/ppermute | solution.py:568
  193.0 32.6 %collective-permute-start.21 = (bf16[2,2,64,2560]{3,2,1,0:T(8,128)(2,1)}, bf16[2,2,64,2560]{3,2,1,0:T(8,128)(2,1)}, u32[]{:S(2)}, u32[]{:S(2)}) collective-permute-start(bf16[2,2,64,2560]{3,2,1,0:T(8,128)(2,1)} %shard_map.328.rest_3_.refs_2_), channel_id=1, source_target_pairs={{0,16},{8,24},{16,0},{24,8},{1,17},{9,25},{17,1},{25,9},{2,18},{10... | collective-permute-start | bytes 3932168 | tf_op jit(solution)/shard_map/ppermute | solution.py:559
  364.6 23.8 %collective-permute-start.30 = (bf16[512,4096]{1,0:T(8,128)(2,1)}, bf16[512,4096]{1,0:T(8,128)(2,1)}, u32[]{:S(2)}, u32[]{:S(2)}) collective-permute-start(bf16[512,4096]{1,0:T(8,128)(2,1)} %convolution_convert_fusion.1), channel_id=1, source_target_pairs={{0,8},{8,0},{16,24},{24,16},{1,9},{9,1},{17,25},{25,17},{2,10},{10... | collective-permute-start | bytes 12582920 | tf_op jit(solution)/shard_map/ppermute | solution.py:562
  366.7 21.7 %collective-permute-start.31 = (bf16[512,1024]{1,0:T(8,128)(2,1)}, bf16[512,1024]{1,0:T(8,128)(2,1)S(1)}, u32[]{:S(2)}, u32[]{:S(2)}) collective-permute-start(bf16[512,1024]{1,0:T(8,128)(2,1)} %convolution_convert_fusion.3), channel_id=1, source_target_pairs={{0,8},{8,0},{16,24},{24,16},{1,9},{9,1},{17,25},{25,17},{2,10},{10... | collective-permute-start | bytes 3145736 | tf_op jit(solution)/shard_map/ppermute | solution.py:562
  388.4 57.8 %collective-permute-start.34 = (bf16[512,4096]{1,0:T(8,128)(2,1)}, bf16[512,4096]{1,0:T(8,128)(2,1)}, u32[]{:S(2)}, u32[]{:S(2)}) collective-permute-start(bf16[512,4096]{1,0:T(8,128)(2,1)} %convolution_convert_fusion), channel_id=1, source_target_pairs={{0,8},{8,0},{16,24},{24,16},{1,9},{9,1},{17,25},{25,17},{2,10},{10... | collective-permute-start | bytes 12582920 | tf_op jit(solution)/shard_map/ppermute | solution.py:562
  402.6 31.4 %collective-permute-start.32 = (bf16[128,5120]{1,0:T(8,128)(2,1)}, bf16[128,5120]{1,0:T(8,128)(2,1)S(1)}, u32[]{:S(2)}, u32[]{:S(2)}) collective-permute-start(bf16[128,5120]{1,0:T(8,128)(2,1)} %get-tuple-element.82.rest_1_), channel_id=1, source_target_pairs={{0,16},{8,24},{16,0},{24,8},{1,17},{9,25},{17,1},{25,9},{2,18},{10... | collective-permute-start | bytes 3932168 | tf_op jit(solution)/shard_map/ppermute | solution.py:559
  404.3 31.2 %collective-permute-start.33 = (bf16[256,2560]{1,0:T(8,128)(2,1)}, bf16[256,2560]{1,0:T(8,128)(2,1)}, u32[]{:S(2)}, u32[]{:S(2)}) collective-permute-start(bf16[256,2560]{1,0:T(8,128)(2,1)} %get-tuple-element.83.rest_2_), channel_id=1, source_target_pairs={{0,1},{1,0},{2,3},{3,2},{4,5},{5,4},{6,7},{7,6},{8,9},{9,8},{10,11... | collective-permute-start | bytes 3932168 | tf_op jit(solution)/shard_map/ppermute | solution.py:568
  425.9 20.3 %collective-permute-start.35 = (bf16[512,1024]{1,0:T(8,128)(2,1)S(1)}, bf16[512,1024]{1,0:T(8,128)(2,1)S(1)}, u32[]{:S(2)}, u32[]{:S(2)}) collective-permute-start(bf16[512,1024]{1,0:T(8,128)(2,1)S(1)} %convolution_convert_fusion.2), channel_id=1, source_target_pairs={{0,8},{8,0},{16,24},{24,16},{1,9},{9,1},{17,25},{25,17},{2,10},{10... | collective-permute-start | bytes 3145736 | tf_op jit(solution)/shard_map/ppermute | solution.py:562
  439.7 22.7 %collective-permute-start.36 = (bf16[128,2560]{1,0:T(8,128)(2,1)}, bf16[128,2560]{1,0:T(8,128)(2,1)S(1)}, u32[]{:S(2)}, u32[]{:S(2)}) collective-permute-start(bf16[128,2560]{1,0:T(8,128)(2,1)} %get-tuple-element.86.rest_0_), channel_id=1, source_target_pairs={{0,1},{1,0},{2,3},{3,2},{4,5},{5,4},{6,7},{7,6},{8,9},{9,8},{10,11... | collective-permute-start | bytes 1966088 | tf_op jit(solution)/shard_map/ppermute | solution.py:568
  441.0 21.5 %collective-permute-start.37 = (bf16[128,2560]{1,0:T(8,128)(2,1)}, bf16[128,2560]{1,0:T(8,128)(2,1)S(1)}, u32[]{:S(2)}, u32[]{:S(2)}) collective-permute-start(bf16[128,2560]{1,0:T(8,128)(2,1)} %get-tuple-element.87.rest_1_), channel_id=1, source_target_pairs={{0,16},{8,24},{16,0},{24,8},{1,17},{9,25},{17,1},{25,9},{2,18},{10... | collective-permute-start | bytes 1966088 | tf_op jit(solution)/shard_map/ppermute | solution.py:559
  460.4 30.0 %collective-permute-start.39 = (bf16[128,5120]{1,0:T(8,128)(2,1)}, bf16[128,5120]{1,0:T(8,128)(2,1)S(1)}, u32[]{:S(2)}, u32[]{:S(2)}) collective-permute-start(bf16[128,5120]{1,0:T(8,128)(2,1)} %get-tuple-element.89.rest_0_), channel_id=1, source_target_pairs={{0,16},{8,24},{16,0},{24,8},{1,17},{9,25},{17,1},{25,9},{2,18},{10... | collective-permute-start | bytes 3932168 | tf_op jit(solution)/shard_map/ppermute | solution.py:559
  461.6 29.9 %collective-permute-start.40 = (bf16[256,2560]{1,0:T(8,128)(2,1)}, bf16[256,2560]{1,0:T(8,128)(2,1)S(1)}, u32[]{:S(2)}, u32[]{:S(2)}) collective-permute-start(bf16[256,2560]{1,0:T(8,128)(2,1)} %get-tuple-element.90.refs_4_.rest_1_), channel_id=1, source_target_pairs={{0,1},{1,0},{2,3},{3,2},{4,5},{5,4},{6,7},{7,6},{8,9},{9,8},{10,11... | collective-permute-start | bytes 3932168 | tf_op jit(solution)/shard_map/ppermute | solution.py:568
  466.4 32.2 %collective-permute-start.38 = (bf16[2,64,2560]{2,1,0:T(8,128)(2,1)}, bf16[2,64,2560]{2,1,0:T(8,128)(2,1)S(1)}, u32[]{:S(2)}, u32[]{:S(2)}) collective-permute-start(bf16[2,64,2560]{2,1,0:T(8,128)(2,1)} %get-tuple-element.93.rest_2_), channel_id=1, source_target_pairs={{0,2},{2,0},{4,6},{6,4},{1,3},{3,1},{5,7},{7,5},{8,10},{10,8},{12,... | collective-permute-start | bytes 1966088 | tf_op jit(solution)/shard_map/ppermute | solution.py:565
  496.7 23.0 %collective-permute-start.41 = (bf16[128,2560]{1,0:T(8,128)(2,1)}, bf16[128,2560]{1,0:T(8,128)(2,1)S(1)}, u32[]{:S(2)}, u32[]{:S(2)}) collective-permute-start(bf16[128,2560]{1,0:T(8,128)(2,1)} %get-tuple-element.100.rest_3_), channel_id=1, source_target_pairs={{0,1},{1,0},{2,3},{3,2},{4,5},{5,4},{6,7},{7,6},{8,9},{9,8},{10,11... | collective-permute-start | bytes 1966088 | tf_op jit(solution)/shard_map/ppermute | solution.py:568
  497.3 22.4 %collective-permute-start.42 = (bf16[128,2560]{1,0:T(8,128)(2,1)}, bf16[128,2560]{1,0:T(8,128)(2,1)S(1)}, u32[]{:S(2)}, u32[]{:S(2)}) collective-permute-start(bf16[128,2560]{1,0:T(8,128)(2,1)} %get-tuple-element.101.rest_4_), channel_id=1, source_target_pairs={{0,16},{8,24},{16,0},{24,8},{1,17},{9,25},{17,1},{25,9},{2,18},{10... | collective-permute-start | bytes 1966088 | tf_op jit(solution)/shard_map/ppermute | solution.py:559
  529.2 22.4 %collective-permute-start.46 = (bf16[2,64,2560]{2,1,0:T(8,128)(2,1)S(1)}, bf16[2,64,2560]{2,1,0:T(8,128)(2,1)S(1)}, u32[]{:S(2)}, u32[]{:S(2)}) collective-permute-start(bf16[2,64,2560]{2,1,0:T(8,128)(2,1)S(1)} %copy-done.26), channel_id=1, source_target_pairs={{0,2},{2,0},{4,6},{6,4},{1,3},{3,1},{5,7},{7,5},{8,10},{10,8},{12,... | collective-permute-start | bytes 1966088 | tf_op jit(solution)/shard_map/ppermute | solution.py:565
  537.5 24.4 %collective-permute-start.45 = (bf16[256,1536]{1,0:T(8,128)(2,1)S(1)}, bf16[256,1536]{1,0:T(8,128)(2,1)S(1)}, u32[]{:S(2)}, u32[]{:S(2)}) collective-permute-start(bf16[256,1536]{1,0:T(8,128)(2,1)S(1)} %slice.392.rest_2_), channel_id=1, source_target_pairs={{0,16},{8,24},{16,0},{24,8},{1,17},{9,25},{17,1},{25,9},{2,18},{10... | collective-permute-start | bytes 2359304 | tf_op jit(solution)/shard_map/ppermute | solution.py:559
  560.4 25.6 %collective-permute-start.50 = (f32[32,512]{1,0:T(8,128)S(1)}, f32[32,512]{1,0:T(8,128)S(1)}, u32[]{:S(2)}, u32[]{:S(2)}) collective-permute-start(f32[32,512]{1,0:T(8,128)S(1)} %get-tuple-element.145), channel_id=1, source_target_pairs={{0,1},{1,0},{2,3},{3,2},{4,5},{5,4},{6,7},{7,6},{8,9},{9,8},{10,11... | collective-permute-start | bytes 196616 | tf_op jit(solution)/shard_map/ppermute | solution.py:568
  561.5 22.5 %collective-permute-start.49 = (bf16[1,64,2560]{2,1,0:T(8,128)(2,1)}, bf16[1,64,2560]{2,1,0:T(8,128)(2,1)}, u32[]{:S(2)}, u32[]{:S(2)}) collective-permute-start(bf16[1,64,2560]{2,1,0:T(8,128)(2,1)} %get-tuple-element.111.refs_1_.rest_4_), channel_id=1, source_target_pairs={{0,4},{2,6},{4,0},{6,2},{1,5},{3,7},{5,1},{7,3},{8,12},{10,14},{12... | collective-permute-start | bytes 983048 | tf_op jit(solution)/shard_map/ppermute | solution.py:565
  565.4 21.2 %collective-permute-start.48 = (bf16[256,1536]{1,0:T(8,128)(2,1)}, bf16[256,1536]{1,0:T(8,128)(2,1)}, u32[]{:S(2)}, u32[]{:S(2)}) collective-permute-start(bf16[256,1536]{1,0:T(8,128)(2,1)} %add_convert_fusion.3.refs_1_.rest_2_), channel_id=1, source_target_pairs={{0,1},{1,0},{2,3},{3,2},{4,5},{5,4},{6,7},{7,6},{8,9},{9,8},{10,11... | collective-permute-start | bytes 2359304 | tf_op jit(solution)/shard_map/ppermute | solution.py:568
  593.1 18.3 %collective-permute-start.52 = (bf16[256,768]{1,0:T(8,128)(2,1)}, bf16[256,768]{1,0:T(8,128)(2,1)}, u32[]{:S(2)}, u32[]{:S(2)}) collective-permute-start(bf16[256,768]{1,0:T(8,128)(2,1)} %slice.396.rest_3_), channel_id=1, source_target_pairs={{0,16},{8,24},{16,0},{24,8},{1,17},{9,25},{17,1},{25,9},{2,18},{10... | collective-permute-start | bytes 1179656 | tf_op jit(solution)/shard_map/ppermute | solution.py:559
  604.4 35.5 %collective-permute-start.53 = (bf16[640,1024]{1,0:T(8,128)(2,1)}, bf16[640,1024]{1,0:T(8,128)(2,1)}, u32[]{:S(2)}, u32[]{:S(2)}) collective-permute-start(bf16[640,1024]{1,0:T(8,128)(2,1)} %shard_map.361.refs_1_), channel_id=1, source_target_pairs={{0,1},{1,0},{2,3},{3,2},{4,5},{5,4},{6,7},{7,6},{8,9},{9,8},{10,11... | collective-permute-start | bytes 3932168 | tf_op jit(solution)/shard_map/ppermute | solution.py:568
  (150 other events, 1095.5 us)

commit v4 on v3

--- a/solution.py
+++ b/solution.py
@@ -825,10 +825,8 @@
         head_mine = lax.dynamic_slice_in_dim(w_head, t0 * head_half, head_half, 1)
         shard_e = jnp.concatenate([w_fin.T, head_mine], axis=1)
 
-        q_0 = shard_q[None]
-        q_1 = z_go(q_0, z_bits - 1)
-        q_2, q_3 = z_rest(q_0, q_1)
-        near_q, far_q = z_last(q_2, q_3)
+        q_all = [shard_q] + [pz(shard_q, k) for k in range(1, n_pa)]
+        near_q, far_q = joined(q_all[: n_pa // 2]), joined(q_all[n_pa // 2 :])
         m_0 = tie(shard_m[None], near_q)
         m_1 = z_go(m_0, z_bits - 1)
         near_q, far_q = xy_one(xy_go(near_q, far_q), (rows, aug_q, aug_k))
@@ -841,7 +839,7 @@
 
         col_scale = jnp.tile(jnp.repeat(jnp.array([scale, 1.0, 1.0], F32), LANES), all_pairs)
         (qkv,) = mm_in(
-            rows, h_q, r_q, 0, qkv_half, qkv_half // 3, put_scaled, (eight(qkv_bias, col_scale),),
+            rows, h_q, r_q, 0, qkv_half, qkv_half // 2, put_scaled, (eight(qkv_bias, col_scale),),
             ((half_rows + toks, BF),), deps=(m_2,),
         )
         near_m, far_m = z_last(m_2, m_3, (qkv,))
@@ -897,8 +895,9 @@
         unit_low = unit.astype(BF)
 
         passages = unit_low[slots:]
-        mine = gather_z(unit_low[:slots])
-        asked = jnp.concatenate([mine, swapped(py(mine))], axis=0)
+        own = unit_low[:slots]
+        others = joined([pz(own, k)[None] for k in range(1, n_pa)]).reshape(-1, width)
+        asked = jnp.concatenate([own, others, swapped(py(own)), swapped(py(others))], axis=0)
         n_asked = asked.shape[0]
         z_rel = jnp.arange(n_pa, dtype=jnp.int32) ^ z0
         swap_t = lambda a: jnp.where(first_t, a, a[::-1])
@@ -928,9 +927,10 @@
         ask_grad = nn(sim_grad, passages).astype(BF).reshape(n_ta, n_pa * slots, width)
         ask_sum = add(ask_grad[0], py(swapped(ask_grad[1])))
         passage_grad = tn(sim_grad, asked)
-        unit_grad = jnp.concatenate(
-            [reduce_z(ask_sum.reshape(n_pa, slots, width)), passage_grad], axis=0
-        )
+        own_grad = ask_sum[:slots].astype(F32)
+        for k in range(1, n_pa):
+            own_grad = own_grad + pz(ask_sum[k * slots : (k + 1) * slots], k).astype(F32)
+        unit_grad = jnp.concatenate([own_grad, passage_grad], axis=0)
 
         raw_grad = inv * (unit_grad - unit * jnp.sum(unit * unit_grad, axis=-1, keepdims=True))
         g_b_head = in_order(jnp.sum(raw_grad, axis=0))
@@ -944,7 +944,7 @@
         away_fin = away_part(branch_low, active)
         away_head = away_part(output_low, raw_low)
         inner_low, sums_in = mm_in(
-            branch_low, h_e, r_e, 0, ff_half, ff_half // 4, put_sloped, (slope,),
+            branch_low, h_e, r_e, 0, ff_half, ff_half // 2, put_sloped, (slope,),
             ((half_rows, BF), (8, F32)), row_of_zeros, put_sum,
         )
         *near, far_own, far_oth = own_parts(
@@ -1053,7 +1053,7 @@
         keep_q, give_q = z_split(jnp.concatenate([q_2, q_3], axis=2))
         keep_q, give_q = z_split(add(keep_q, pz(give_q, 1)))
         to_other, keep_q = tie(to_other, give_q), tie(keep_q, to_other)
-        sums_qv = tie(sums_qv, to_other)
+        sums_qv = tie(sums_qv, part_3)
         if z_bits == 2:
             out_q = (keep_q.astype(F32) + pz(give_q, 2).astype(F32))[0]
         else:
@@ -1074,6 +1074,7 @@
         vec = vec + pc(vec)
         for bit in range(x_bits):
             vec = vec + px(vec, 1 << bit)
+        vec = tie(vec, to_other)
         vec = vec + py(vec)
         for bit in range(z_bits):
             vec = vec + pz(vec, 1 << bit)

time: 677 us -> 650 us (0.960)
  waiting for transfers between devices: 133 us -> 107 us
    ppermute x18 -> x21, waiting for transfers between devices: 62.7 us -> 48.1 us  [pz(): return lax.ppermute(v, 'pa', [(i, i ^ k) for i in range(n_pa)])]
    ppermute x19 -> x20, waiting for transfers between devices: 39.8 us -> 31.7 us  [py(): return lax.ppermute(v, 'ta', [(i, i ^ 1) for i in range(n_ta)])]
    ppermute x19 -> x20, starting transfers between devices: 18.8 us -> 25 us  [py(): return lax.ppermute(v, 'ta', [(i, i ^ 1) for i in range(n_ta)])]
    ppermute x18 -> x21, starting transfers between devices: 34.3 us -> 29.2 us  [pz(): return lax.ppermute(v, 'pa', [(i, i ^ k) for i in range(n_pa)])]
    pallas_call x17 -> x16, Pallas kernels: 42.8 us -> 40.7 us  [assemble(): pl.pallas_call(functools.partial(assemble_kernel, len(arrays), len(deps),...]
    unnamed x245 -> x267, local copies, waits for them, and re-layouts: 36.5 us -> 36.2 us
  transfers between devices with their start and end apart: 62 -> 66, of which waited for: 25 -> 23; matrix products, arithmetic and copies ran while one was open for 11% -> 12% of each run, Pallas kernels for 39% -> 41%
where the time goes in v4:
time: 650 us; the launch traced here: 640 us
  Pallas kernels  305 us (47%)
  waiting for transfers between devices  107 us (16%)
  starting transfers between devices  71.4 us (11%)
  local copies, waits for them, and re-layouts  57.1 us (9%)
  matrix products  48.8 us (8%)
  other arithmetic  48.7 us (7%)
    pallas_call x6, Pallas kernels, mm_out(): pl.pallas_call(functools.partial(mm_out_kernel, chunk_of(m), half, len(ex...  57.8 us
    pallas_call x5, Pallas kernels, mm_in(): pl.pallas_call(functools.partial(mm_in_kernel, chunk_of(m), epilogue, sta...  55.7 us
    pallas_call x4, Pallas kernels, attend_back(): pl.pallas_call(functools.partial(attend_back_kernel, slots, tile_k, scale...  50.8 us
    ppermute x21, waiting for transfers between devices, pz(): return lax.ppermute(v, 'pa', [(i, i ^ k) for i in range(n_pa)])  48.1 us
    dot_general x11, matrix products, tn(): lax.dot_general(a, b, (((0,), (0,)), ((), ())), preferred_element_type=F32)  43.1 us
    pallas_call x16, Pallas kernels, assemble(): pl.pallas_call(functools.partial(assemble_kernel, len(arrays), len(deps),...  40.7 us
    pallas_call x4, Pallas kernels, attend(): pl.pallas_call(functools.partial(attend_kernel, slots, tile_q, len(deps))...  38.1 us
    unnamed x267, local copies, waits for them, and re-layouts  36.2 us
  transfers between devices with their start and end apart: 66, of which 23 were waited for; matrix products, arithmetic and copies ran while one was open for 12% of the time, Pallas kernels for 41%

profile of v4, /device:TPU:0, one launch (start us, length us, event | category | flops | bytes accessed | tf_op | source)
XLA Modules:
  0.0 639.8 jit_solution(2792572701649762723)
XLA Ops:
  47.2 13.0 %collective-permute-done.7.refs_4_.refs_1_ = bf16[1,64,2560]{2,1,0:T(8,128)(2,1)S(1)} collective-permute-done((bf16[1,64,2560]{2,1,0:T(8,128)(2,1)}, bf16[1,64,2560]{2,1,0:T(8,128)(2,1)S(1)}, u32[]{:S(2)}, u32[]{:S(2)}) %collective-permute-start.7) | collective-permute-done | bytes 327712 | tf_op jit(solution)/shard_map/ppermute | solution.py:565
  74.5 14.6 %shard_map.314.refs_2_.q_ref.k_ref.v_ref = bf16[1344,3072]{1,0:T(8,128)(2,1)} custom-call(bf16[1344,1024]{1,0:T(8,128)(2,1)} %shard_map.306.refs_2_.a_ref.rest_0_.refs_0_, bf16[1024,1536]{1,0:T(8,128)(2,1)} %bitcast.179, bf16[1024,1536]{1,0:T(8,128)(2,1)} %copy-done.11, f32[8,3072]{1,0:T(8,128)} %maximum_maximum_fusion.1.rest_0_, bf16[2,64,2560]{2,1,0:T(8,128)(2,1)} %bitcast.203), custom_call_target="tpu_custom_call" | custom-call | flops 8455716864 | bytes 17301504 | tf_op jit(solution)/shard_map/pallas_call | solution.py:416
  97.2 9.5 %shard_map.317 = (bf16[704,1024]{1,0:T(8,128)(2,1)}, bf16[704,1024]{1,0:T(8,128)(2,1)}) custom-call(bf16[1344,3072]{1,0:T(8,128)(2,1)} %shard_map.314.refs_2_.q_ref.k_ref.v_ref, bf16[1344,3072]{1,0:T(8,128)(2,1)} %shard_map.314.refs_2_.q_ref.k_ref.v_ref, bf16[1344,3072]{1,0:T(8,128)(2,1)} %shard_map.314.refs_2_.q_ref.k_ref.v_ref, ...), custom_call_target="tpu_custom_call" | custom-call | flops 3875536896 | bytes 2457600 | tf_op jit(solution)/shard_map/pallas_call | solution.py:135
  121.0 9.5 %shard_map.321 = (bf16[704,1024]{1,0:T(8,128)(2,1)}, bf16[704,1024]{1,0:T(8,128)(2,1)}) custom-call(bf16[1344,3072]{1,0:T(8,128)(2,1)} %shard_map.314.refs_2_.q_ref.k_ref.v_ref, bf16[1344,3072]{1,0:T(8,128)(2,1)} %shard_map.314.refs_2_.q_ref.k_ref.v_ref, ...), custom_call_target="tpu_custom_call", output_to_operand_aliasing={{0}: (5, {}), {1}: (6, {})} | custom-call | flops 3875536896 | bytes 2457600 | tf_op jit(solution)/shard_map/pallas_call | solution.py:135
  130.5 9.7 %shard_map.322 = (bf16[704,1024]{1,0:T(8,128)(2,1)}, bf16[704,1024]{1,0:T(8,128)(2,1)}) custom-call(bf16[1344,3072]{1,0:T(8,128)(2,1)} %shard_map.314.refs_2_.q_ref.k_ref.v_ref, bf16[1344,3072]{1,0:T(8,128)(2,1)} %shard_map.314.refs_2_.q_ref.k_ref.v_ref, ...), custom_call_target="tpu_custom_call", output_to_operand_aliasing={{0}: (5, {}), {1}: (6, {})} | custom-call | flops 3875536896 | bytes 2457600 | tf_op jit(solution)/shard_map/pallas_call | solution.py:135
  143.4 9.5 %shard_map.324 = (bf16[704,1024]{1,0:T(8,128)(2,1)}, bf16[704,1024]{1,0:T(8,128)(2,1)}) custom-call(bf16[1344,3072]{1,0:T(8,128)(2,1)} %shard_map.314.refs_2_.q_ref.k_ref.v_ref, bf16[1344,3072]{1,0:T(8,128)(2,1)} %shard_map.314.refs_2_.q_ref.k_ref.v_ref, ...), custom_call_target="tpu_custom_call", output_to_operand_aliasing={{0}: (5, {}), {1}: (6, {})} | custom-call | flops 3875536896 | bytes 2457600 | tf_op jit(solution)/shard_map/pallas_call | solution.py:135
  168.3 9.8 %collective-permute-done.20 = f32[2048]{0:T(1024)S(1)} collective-permute-done((f32[2048]{0:T(1024)S(1)}, f32[2048]{0:T(1024)S(1)}, u32[]{:S(2)}, u32[]{:S(2)}) %collective-permute-start.20) | collective-permute-done | bytes 8224 | tf_op jit(solution)/shard_map/ppermute | solution.py:568
  186.4 6.0 shard_map.329
  198.1 20.2 %shard_map.330 = (bf16[704,4096]{1,0:T(8,128)(2,1)}, bf16[704,4096]{1,0:T(8,128)(2,1)}) custom-call(bf16[704,1024]{1,0:T(8,128)(2,1)} %get-tuple-element.134.a_ref.la_ref, bf16[1024,2560]{1,0:T(8,128)(2,1)} %bitcast.165, bf16[1024,2560]{1,0:T(8,128)(2,1)} %collective-permute-done.17.r0_ref.r1_ref.r_ref, f32[8,4096]{1,0:T(8,128)} %concatenate.104.rest_0_), custom_call_target="tpu_custom_call" | custom-call | flops 5905580032 | bytes 21364736 | tf_op jit(solution)/shard_map/pallas_call | solution.py:416
  227.3 5.0 collective-permute-done.23.r0_ref.r1_ref.r_ref
  232.2 12.8 %shard_map.332 = f32[704,1024]{1,0:T(8,128)} custom-call(bf16[704,4096]{1,0:T(8,128)(2,1)} %get-tuple-element.75.refs_4_.a0_ref.a1_ref.ra_ref, bf16[704,4096]{1,0:T(8,128)(2,1)} %get-tuple-element.75.refs_4_.a0_ref.a1_ref.ra_ref, bf16[1024,2560]{1,0:T(8,128)(2,1)} %bitcast.170, bf16[1024,2560]{1,0:T(8,128)(2,1)} %bitcast.171, ...), custom_call_target="tpu_custom_call" | custom-call | flops 5905580032 | bytes 17039360 | tf_op jit(solution)/shard_map/pallas_call | solution.py:467
  266.8 6.9 %collective-permute-done.25 = bf16[64,1024]{1,0:T(8,128)(2,1)S(1)} collective-permute-done((bf16[64,1024]{1,0:T(8,128)(2,1)S(1)}, bf16[64,1024]{1,0:T(8,128)(2,1)S(1)}, u32[]{:S(2)}, u32[]{:S(2)}) %collective-permute-start.25) | collective-permute-done | bytes 131104 | tf_op jit(solution)/shard_map/ppermute | solution.py:565
  278.5 7.1 %collective-permute-done.28 = bf16[192,1024]{1,0:T(8,128)(2,1)S(1)} collective-permute-done((bf16[192,1024]{1,0:T(8,128)(2,1)}, bf16[192,1024]{1,0:T(8,128)(2,1)S(1)}, u32[]{:S(2)}, u32[]{:S(2)}) %collective-permute-start.28) | collective-permute-done | bytes 393248 | tf_op jit(solution)/shard_map/ppermute | solution.py:568
  298.7 8.3 %collective-permute-done.30 = bf16[256,1024]{1,0:T(8,128)(2,1)S(1)} collective-permute-done((bf16[256,1024]{1,0:T(8,128)(2,1)S(1)}, bf16[256,1024]{1,0:T(8,128)(2,1)S(1)}, u32[]{:S(2)}, u32[]{:S(2)}) %collective-permute-start.30) | collective-permute-done | bytes 524320 | tf_op jit(solution)/shard_map/ppermute | solution.py:568
  322.0 6.2 shard_map.335
  336.4 5.1 convolution_convert_fusion.1
  344.0 11.7 %shard_map.336 = (bf16[704,4096]{1,0:T(8,128)(2,1)}, f32[8,4096]{1,0:T(8,128)}) custom-call(bf16[704,1024]{1,0:T(8,128)(2,1)} %copy-done.23, bf16[1024,2560]{1,0:T(8,128)(2,1)} %bitcast.175, bf16[1024,2560]{1,0:T(8,128)(2,1)} %collective-permute-done.23.r0_ref.r1_ref.r_ref, bf16[704,4096]{1,0:T(8,128)(2,1)} %get-tuple-element.76.rest_0_), custom_call_target="tpu_custom_call" | custom-call | flops 5905580032 | bytes 15663104 | tf_op jit(solution)/shard_map/pallas_call | solution.py:416
  355.7 7.7 %convolution_convert_fusion = bf16[512,4096]{1,0:T(8,128)(2,1)} fusion(bf16[704,4096]{1,0:T(8,128)(2,1)} %get-tuple-element.77.rest_0_.a0_ref.a1_ref.ra_ref, bf16[704,1024]{1,0:T(8,128)(2,1)S(1)} %copy-done.22), kind=kOutput, calls=%fused_computation.3 | convolution fusion | flops 2954887168 | bytes 10682368 | tf_op jit(solution)/shard_map/dot_general | solution.py:32
  364.5 13.2 %shard_map.337 = (bf16[128,5120]{1,0:T(8,128)(2,1)}, bf16[128,5120]{1,0:T(8,128)(2,1)}, bf16[256,2560]{1,0:T(8,128)(2,1)}, bf16[256,2560]{1,0:T(8,128)(2,1)}) custom-call(bf16[704,1024]{1,0:T(8,128)(2,1)} %copy-done.23, bf16[704,1024]{1,0:T(8,128)(2,1)} %add_convert_fusion.a_ref.lb_ref, bf16[704,4096]{1,0:T(8,128)(2,1)} %get-tuple-element.75.refs_4_.a0_ref.a1_ref.ra_ref, ...), custom_call_target="tpu_custom_call" | custom-call | flops 3690987520 | bytes 17694720 | tf_op jit(solution)/shard_map/pallas_call | solution.py:366
  379.7 12.7 %shard_map.338.refs_4_ = f32[704,1024]{1,0:T(8,128)} custom-call(bf16[704,4096]{1,0:T(8,128)(2,1)} %get-tuple-element.77.rest_0_.a0_ref.a1_ref.ra_ref, bf16[704,4096]{1,0:T(8,128)(2,1)} %get-tuple-element.77.rest_0_.a0_ref.a1_ref.ra_ref, bf16[1024,2560]{1,0:T(8,128)(2,1)} %bitcast.166, bf16[1024,2560]{1,0:T(8,128)(2,1)} %bitcast.167, ...), custom_call_target="tpu_custom_call" | custom-call | flops 5905580032 | bytes 17039360 | tf_op jit(solution)/shard_map/pallas_call | solution.py:467
  401.4 7.7 %collective-permute-done.36.refs_1_ = bf16[128,5120]{1,0:T(8,128)(2,1)S(1)} collective-permute-done((bf16[128,5120]{1,0:T(8,128)(2,1)}, bf16[128,5120]{1,0:T(8,128)(2,1)S(1)}, u32[]{:S(2)}, u32[]{:S(2)}) %collective-permute-start.36) | collective-permute-done | bytes 1310752 | tf_op jit(solution)/shard_map/ppermute | solution.py:559
  422.1 13.2 %shard_map.341 = (bf16[128,5120]{1,0:T(8,128)(2,1)}, bf16[128,5120]{1,0:T(8,128)(2,1)}, bf16[256,2560]{1,0:T(8,128)(2,1)}, bf16[256,2560]{1,0:T(8,128)(2,1)}) custom-call(bf16[704,1024]{1,0:T(8,128)(2,1)} %get-tuple-element.134.a_ref.la_ref, bf16[704,1024]{1,0:T(8,128)(2,1)} %copy-done.17, bf16[704,4096]{1,0:T(8,128)(2,1)} %get-tuple-element.77.rest_0_.a0_ref.a1_ref.ra_ref, ...), custom_call_target="tpu_custom_call" | custom-call | flops 3690987520 | bytes 17694720 | tf_op jit(solution)/shard_map/pallas_call | solution.py:366
  441.1 12.5 %shard_map.343 = (bf16[1344,3072]{1,0:T(8,128)(2,1)}, f32[8,1024]{1,0:T(8,128)}) custom-call(bf16[1344,3072]{1,0:T(8,128)(2,1)} %shard_map.314.refs_2_.q_ref.k_ref.v_ref, bf16[1344,3072]{1,0:T(8,128)(2,1)} %shard_map.314.refs_2_.q_ref.k_ref.v_ref, bf16[1344,3072]{1,0:T(8,128)(2,1)} %shard_map.314.refs_2_.q_ref.k_ref.v_ref, ...), custom_call_target="tpu_custom_call" | custom-call | flops 9688842240 | bytes 4915200 | tf_op jit(solution)/shard_map/pallas_call | solution.py:228
  453.6 11.6 %collective-permute-done.43.refs_1_ = bf16[128,5120]{1,0:T(8,128)(2,1)S(1)} collective-permute-done((bf16[128,5120]{1,0:T(8,128)(2,1)}, bf16[128,5120]{1,0:T(8,128)(2,1)S(1)}, u32[]{:S(2)}, u32[]{:S(2)}) %collective-permute-start.43) | collective-permute-done | bytes 1310752 | tf_op jit(solution)/shard_map/ppermute | solution.py:559
  476.9 12.7 %shard_map.346 = (bf16[1344,3072]{1,0:T(8,128)(2,1)}, f32[8,1024]{1,0:T(8,128)}) custom-call(bf16[1344,3072]{1,0:T(8,128)(2,1)} %shard_map.314.refs_2_.q_ref.k_ref.v_ref, bf16[1344,3072]{1,0:T(8,128)(2,1)} %shard_map.314.refs_2_.q_ref.k_ref.v_ref, ...), custom_call_target="tpu_custom_call", output_to_operand_aliasing={{0}: (7, {}), {1}: (8, {})} | custom-call | flops 9688842240 | bytes 4915200 | tf_op jit(solution)/shard_map/pallas_call | solution.py:228
  498.2 6.5 %fusion.7 = bf16[512,1536]{1,0:T(8,128)(2,1)} fusion(bf16[1344,3072]{1,0:T(8,128)(2,1)} %get-tuple-element.98.rest_0_, bf16[1344,1024]{1,0:T(8,128)(2,1)} %shard_map.349.refs_0_), kind=kOutput, calls=%fused_computation.10 | convolution fusion | flops 2114715648 | bytes 7077888 | tf_op jit(solution)/shard_map/dot_general | solution.py:32
  508.5 5.3 fusion.10
  516.1 13.0 %shard_map.350 = (bf16[1344,3072]{1,0:T(8,128)(2,1)}, f32[8,1024]{1,0:T(8,128)}) custom-call(bf16[1344,3072]{1,0:T(8,128)(2,1)} %shard_map.314.refs_2_.q_ref.k_ref.v_ref, bf16[1344,3072]{1,0:T(8,128)(2,1)} %shard_map.314.refs_2_.q_ref.k_ref.v_ref, ...), custom_call_target="tpu_custom_call", output_to_operand_aliasing={{0}: (7, {}), {1}: (8, {})} | custom-call | flops 9688842240 | bytes 4915200 | tf_op jit(solution)/shard_map/pallas_call | solution.py:228
  549.7 12.6 %shard_map.355 = (bf16[1344,3072]{1,0:T(8,128)(2,1)}, f32[8,1024]{1,0:T(8,128)}) custom-call(bf16[1344,3072]{1,0:T(8,128)(2,1)} %shard_map.314.refs_2_.q_ref.k_ref.v_ref, bf16[1344,3072]{1,0:T(8,128)(2,1)} %shard_map.314.refs_2_.q_ref.k_ref.v_ref, ...), custom_call_target="tpu_custom_call", output_to_operand_aliasing={{0}: (7, {}), {1}: (8, {})} | custom-call | flops 9688842240 | bytes 4915200 | tf_op jit(solution)/shard_map/pallas_call | solution.py:228
  574.2 9.3 %shard_map.360.refs_1_ = bf16[640,1024]{1,0:T(8,128)(2,1)} custom-call(bf16[1344,3072]{1,0:T(8,128)(2,1)} %get-tuple-element.108.a0_ref.a1_ref.refs_0_, bf16[1344,3072]{1,0:T(8,128)(2,1)} %get-tuple-element.108.a0_ref.a1_ref.refs_0_, bf16[1024,1536]{1,0:T(8,128)(2,1)} %bitcast.180, bf16[1024,1536]{1,0:T(8,128)(2,1)} %bitcast.181, ...), custom_call_target="tpu_custom_call" | custom-call | flops 4026531840 | bytes 12845056 | tf_op jit(solution)/shard_map/pallas_call | solution.py:467
  593.1 10.7 %shard_map.363.refs_1_.x_ref = f32[704,1024]{1,0:T(8,128)} custom-call(bf16[1344,3072]{1,0:T(8,128)(2,1)} %shard_map.361.a0_ref.a1_ref, bf16[1344,3072]{1,0:T(8,128)(2,1)} %shard_map.361.a0_ref.a1_ref, bf16[1024,1536]{1,0:T(8,128)(2,1)} %bitcast.182, bf16[1024,1536]{1,0:T(8,128)(2,1)} %bitcast.183, bf16[1024,1536]{1,0:T(8,128)(2,1)} %copy-done.11, ...), custom_call_target="tpu_custom_call" | custom-call | flops 4429185024 | bytes 13500416 | tf_op jit(solution)/shard_map/pallas_call | solution.py:467
  609.9 8.2 %collective-permute-done.59 = bf16[2,64,1536]{2,1,0:T(8,128)(2,1)S(1)} collective-permute-done((bf16[2,64,1536]{2,1,0:T(8,128)(2,1)S(1)}, bf16[2,64,1536]{2,1,0:T(8,128)(2,1)S(1)}, u32[]{:S(2)}, u32[]{:S(2)}) %collective-permute-start.59) | collective-permute-done | bytes 393248 | tf_op jit(solution)/shard_map/ppermute | solution.py:565
  (597 shorter events, 315.5 us)
Async XLA Ops:
  15.9 19.1 %collective-permute-start.1 = (bf16[2,64,1536]{2,1,0:T(8,128)(2,1)}, bf16[2,64,1536]{2,1,0:T(8,128)(2,1)S(1)}, u32[]{:S(2)}, u32[]{:S(2)}) collective-permute-start(bf16[2,64,1536]{2,1,0:T(8,128)(2,1)} %shard_map.307.refs_0_.refs_1_), channel_id=1, source_target_pairs={{0,16},{8,24},{16,0},{24,8},{1,17},{9,25},{17,1},{25,9},{2,18},{10... | collective-permute-start | bytes 1179656 | tf_op jit(solution)/shard_map/ppermute | solution.py:559
  37.9 22.3 %collective-permute-start.2 = (bf16[2,2,64,1536]{3,2,1,0:T(8,128)(2,1)}, bf16[2,2,64,1536]{3,2,1,0:T(8,128)(2,1)S(1)}, u32[]{:S(2)}, u32[]{:S(2)}) collective-permute-start(bf16[2,2,64,1536]{3,2,1,0:T(8,128)(2,1)} %shard_map.308.refs_0_), channel_id=1, source_target_pairs={{0,1},{1,0},{2,3},{3,2},{4,5},{5,4},{6,7},{7,6},{8,9},{9,8},{10,11... | collective-permute-start | bytes 2359304 | tf_op jit(solution)/shard_map/ppermute | solution.py:568
  41.2 19.0 %collective-permute-start.6 = (bf16[2,2,64,1536]{3,2,1,0:T(8,128)(2,1)}, bf16[2,2,64,1536]{3,2,1,0:T(8,128)(2,1)S(1)}, u32[]{:S(2)}, u32[]{:S(2)}) collective-permute-start(bf16[2,2,64,1536]{3,2,1,0:T(8,128)(2,1)} %shard_map.310.refs_2_), channel_id=1, source_target_pairs={{0,16},{8,24},{16,0},{24,8},{1,17},{9,25},{17,1},{25,9},{2,18},{10... | collective-permute-start | bytes 2359304 | tf_op jit(solution)/shard_map/ppermute | solution.py:559
  93.9 19.2 %collective-permute-start.12 = (bf16[2,64,2560]{2,1,0:T(8,128)(2,1)}, bf16[2,64,2560]{2,1,0:T(8,128)(2,1)S(1)}, u32[]{:S(2)}, u32[]{:S(2)}) collective-permute-start(bf16[2,64,2560]{2,1,0:T(8,128)(2,1)} %bitcast.210), channel_id=1, source_target_pairs={{0,1},{1,0},{2,3},{3,2},{4,5},{5,4},{6,7},{7,6},{8,9},{9,8},{10,11... | collective-permute-start | bytes 1966088 | tf_op jit(solution)/shard_map/ppermute | solution.py:568
  96.1 21.6 %collective-permute-start.13 = (bf16[1,64,2560]{2,1,0:T(8,128)(2,1)}, bf16[1,64,2560]{2,1,0:T(8,128)(2,1)S(1)}, u32[]{:S(2)}, u32[]{:S(2)}) collective-permute-start(bf16[1,64,2560]{2,1,0:T(8,128)(2,1)} %shard_map.316.rest_1_.refs_0_), channel_id=1, source_target_pairs={{0,4},{2,6},{4,0},{6,2},{1,5},{3,7},{5,1},{7,3},{8,12},{10,14},{12... | collective-permute-start | bytes 983048 | tf_op jit(solution)/shard_map/ppermute | solution.py:565
  111.4 41.5 %collective-permute-start.15 = (bf16[2,2,64,2560]{3,2,1,0:T(8,128)(2,1)}, bf16[2,2,64,2560]{3,2,1,0:T(8,128)(2,1)S(1)}, u32[]{:S(2)}, u32[]{:S(2)}) collective-permute-start(bf16[2,2,64,2560]{3,2,1,0:T(8,128)(2,1)} %shard_map.318.rest_2_.refs_0_), channel_id=1, source_target_pairs={{0,1},{1,0},{2,3},{3,2},{4,5},{5,4},{6,7},{7,6},{8,9},{9,8},{10,11... | collective-permute-start | bytes 3932168 | tf_op jit(solution)/shard_map/ppermute | solution.py:568
  116.2 36.7 %collective-permute-start.16 = (bf16[2,2,64,2560]{3,2,1,0:T(8,128)(2,1)}, bf16[2,2,64,2560]{3,2,1,0:T(8,128)(2,1)S(1)}, u32[]{:S(2)}, u32[]{:S(2)}) collective-permute-start(bf16[2,2,64,2560]{3,2,1,0:T(8,128)(2,1)} %shard_map.319.rest_3_.refs_2_), channel_id=1, source_target_pairs={{0,16},{8,24},{16,0},{24,8},{1,17},{9,25},{17,1},{25,9},{2,18},{10... | collective-permute-start | bytes 3932168 | tf_op jit(solution)/shard_map/ppermute | solution.py:559
  120.4 19.7 %collective-permute-start.14 = (bf16[2,64,2560]{2,1,0:T(8,128)(2,1)}, bf16[2,64,2560]{2,1,0:T(8,128)(2,1)S(1)}, u32[]{:S(2)}, u32[]{:S(2)}) collective-permute-start(bf16[2,64,2560]{2,1,0:T(8,128)(2,1)} %bitcast.197), channel_id=1, source_target_pairs={{0,2},{2,0},{4,6},{6,4},{1,3},{3,1},{5,7},{7,5},{8,10},{10,8},{12,... | collective-permute-start | bytes 1966088 | tf_op jit(solution)/shard_map/ppermute | solution.py:565
  159.4 26.9 %collective-permute-start.17 = (bf16[1024,2560]{1,0:T(8,128)(2,1)}, bf16[1024,2560]{1,0:T(8,128)(2,1)}, u32[]{:S(2)}, u32[]{:S(2)}) collective-permute-start(bf16[1024,2560]{1,0:T(8,128)(2,1)} %bitcast.160), channel_id=1, source_target_pairs={{0,8},{8,0},{16,24},{24,16},{1,9},{9,1},{17,25},{25,17},{2,10},{10... | collective-permute-start | bytes 15728648 | tf_op jit(solution)/shard_map/ppermute | solution.py:562
  159.5 19.2 %collective-permute-start.18 = (bf16[2,64,2560]{2,1,0:T(8,128)(2,1)S(1)}, bf16[2,64,2560]{2,1,0:T(8,128)(2,1)S(1)}, u32[]{:S(2)}, u32[]{:S(2)}) collective-permute-start(bf16[2,64,2560]{2,1,0:T(8,128)(2,1)S(1)} %bitcast.207), channel_id=1, source_target_pairs={{0,16},{8,24},{16,0},{24,8},{1,17},{9,25},{17,1},{25,9},{2,18},{10... | collective-permute-start | bytes 1966088 | tf_op jit(solution)/shard_map/ppermute | solution.py:559
  161.1 21.5 %collective-permute-start.19 = (bf16[2,64,2560]{2,1,0:T(8,128)(2,1)S(1)}, bf16[2,64,2560]{2,1,0:T(8,128)(2,1)S(1)}, u32[]{:S(2)}, u32[]{:S(2)}) collective-permute-start(bf16[2,64,2560]{2,1,0:T(8,128)(2,1)S(1)} %bitcast.213), channel_id=1, source_target_pairs={{0,1},{1,0},{2,3},{3,2},{4,5},{5,4},{6,7},{7,6},{8,9},{9,8},{10,11... | collective-permute-start | bytes 1966088 | tf_op jit(solution)/shard_map/ppermute | solution.py:568
  182.0 36.3 %collective-permute-start.21 = (bf16[2,2,64,2560]{3,2,1,0:T(8,128)(2,1)}, bf16[2,2,64,2560]{3,2,1,0:T(8,128)(2,1)}, u32[]{:S(2)}, u32[]{:S(2)}) collective-permute-start(bf16[2,2,64,2560]{3,2,1,0:T(8,128)(2,1)} %shard_map.327.rest_2_.refs_0_), channel_id=1, source_target_pairs={{0,1},{1,0},{2,3},{3,2},{4,5},{5,4},{6,7},{7,6},{8,9},{9,8},{10,11... | collective-permute-start | bytes 3932168 | tf_op jit(solution)/shard_map/ppermute | solution.py:568
  185.8 32.5 %collective-permute-start.22 = (bf16[2,2,64,2560]{3,2,1,0:T(8,128)(2,1)}, bf16[2,2,64,2560]{3,2,1,0:T(8,128)(2,1)}, u32[]{:S(2)}, u32[]{:S(2)}) collective-permute-start(bf16[2,2,64,2560]{3,2,1,0:T(8,128)(2,1)} %shard_map.328.rest_3_.refs_2_), channel_id=1, source_target_pairs={{0,16},{8,24},{16,0},{24,8},{1,17},{9,25},{17,1},{25,9},{2,18},{10... | collective-permute-start | bytes 3932168 | tf_op jit(solution)/shard_map/ppermute | solution.py:559
  341.5 22.0 %collective-permute-start.34 = (bf16[512,4096]{1,0:T(8,128)(2,1)}, bf16[512,4096]{1,0:T(8,128)(2,1)}, u32[]{:S(2)}, u32[]{:S(2)}) collective-permute-start(bf16[512,4096]{1,0:T(8,128)(2,1)} %convolution_convert_fusion.1), channel_id=1, source_target_pairs={{0,8},{8,0},{16,24},{24,16},{1,9},{9,1},{17,25},{25,17},{2,10},{10... | collective-permute-start | bytes 12582920 | tf_op jit(solution)/shard_map/ppermute | solution.py:562
  343.5 19.9 %collective-permute-start.35 = (bf16[512,1024]{1,0:T(8,128)(2,1)}, bf16[512,1024]{1,0:T(8,128)(2,1)S(1)}, u32[]{:S(2)}, u32[]{:S(2)}) collective-permute-start(bf16[512,1024]{1,0:T(8,128)(2,1)} %convolution_convert_fusion.3), channel_id=1, source_target_pairs={{0,8},{8,0},{16,24},{24,16},{1,9},{9,1},{17,25},{25,17},{2,10},{10... | collective-permute-start | bytes 3145736 | tf_op jit(solution)/shard_map/ppermute | solution.py:562
  363.4 57.7 %collective-permute-start.38 = (bf16[512,4096]{1,0:T(8,128)(2,1)}, bf16[512,4096]{1,0:T(8,128)(2,1)}, u32[]{:S(2)}, u32[]{:S(2)}) collective-permute-start(bf16[512,4096]{1,0:T(8,128)(2,1)} %convolution_convert_fusion), channel_id=1, source_target_pairs={{0,8},{8,0},{16,24},{24,16},{1,9},{9,1},{17,25},{25,17},{2,10},{10... | collective-permute-start | bytes 12582920 | tf_op jit(solution)/shard_map/ppermute | solution.py:562
  377.7 31.4 %collective-permute-start.36 = (bf16[128,5120]{1,0:T(8,128)(2,1)}, bf16[128,5120]{1,0:T(8,128)(2,1)S(1)}, u32[]{:S(2)}, u32[]{:S(2)}) collective-permute-start(bf16[128,5120]{1,0:T(8,128)(2,1)} %get-tuple-element.78.rest_1_), channel_id=1, source_target_pairs={{0,16},{8,24},{16,0},{24,8},{1,17},{9,25},{17,1},{25,9},{2,18},{10... | collective-permute-start | bytes 3932168 | tf_op jit(solution)/shard_map/ppermute | solution.py:559
  378.2 31.2 %collective-permute-start.37 = (bf16[256,2560]{1,0:T(8,128)(2,1)}, bf16[256,2560]{1,0:T(8,128)(2,1)}, u32[]{:S(2)}, u32[]{:S(2)}) collective-permute-start(bf16[256,2560]{1,0:T(8,128)(2,1)} %get-tuple-element.79.rest_2_), channel_id=1, source_target_pairs={{0,1},{1,0},{2,3},{3,2},{4,5},{5,4},{6,7},{7,6},{8,9},{9,8},{10,11... | collective-permute-start | bytes 3932168 | tf_op jit(solution)/shard_map/ppermute | solution.py:568
  401.4 19.7 %collective-permute-start.39 = (bf16[512,1024]{1,0:T(8,128)(2,1)S(1)}, bf16[512,1024]{1,0:T(8,128)(2,1)S(1)}, u32[]{:S(2)}, u32[]{:S(2)}) collective-permute-start(bf16[512,1024]{1,0:T(8,128)(2,1)S(1)} %convolution_convert_fusion.2), channel_id=1, source_target_pairs={{0,8},{8,0},{16,24},{24,16},{1,9},{9,1},{17,25},{25,17},{2,10},{10... | collective-permute-start | bytes 3145736 | tf_op jit(solution)/shard_map/ppermute | solution.py:562
  414.3 22.7 %collective-permute-start.40 = (bf16[128,2560]{1,0:T(8,128)(2,1)}, bf16[128,2560]{1,0:T(8,128)(2,1)S(1)}, u32[]{:S(2)}, u32[]{:S(2)}) collective-permute-start(bf16[128,2560]{1,0:T(8,128)(2,1)} %get-tuple-element.82.rest_0_), channel_id=1, source_target_pairs={{0,1},{1,0},{2,3},{3,2},{4,5},{5,4},{6,7},{7,6},{8,9},{9,8},{10,11... | collective-permute-start | bytes 1966088 | tf_op jit(solution)/shard_map/ppermute | solution.py:568
  415.9 21.2 %collective-permute-start.41 = (bf16[128,2560]{1,0:T(8,128)(2,1)}, bf16[128,2560]{1,0:T(8,128)(2,1)S(1)}, u32[]{:S(2)}, u32[]{:S(2)}) collective-permute-start(bf16[128,2560]{1,0:T(8,128)(2,1)} %get-tuple-element.83.rest_1_), channel_id=1, source_target_pairs={{0,16},{8,24},{16,0},{24,8},{1,17},{9,25},{17,1},{25,9},{2,18},{10... | collective-permute-start | bytes 1966088 | tf_op jit(solution)/shard_map/ppermute | solution.py:559
  435.3 29.9 %collective-permute-start.43 = (bf16[128,5120]{1,0:T(8,128)(2,1)}, bf16[128,5120]{1,0:T(8,128)(2,1)S(1)}, u32[]{:S(2)}, u32[]{:S(2)}) collective-permute-start(bf16[128,5120]{1,0:T(8,128)(2,1)} %get-tuple-element.85.rest_0_), channel_id=1, source_target_pairs={{0,16},{8,24},{16,0},{24,8},{1,17},{9,25},{17,1},{25,9},{2,18},{10... | collective-permute-start | bytes 3932168 | tf_op jit(solution)/shard_map/ppermute | solution.py:559
  436.6 29.9 %collective-permute-start.44 = (bf16[256,2560]{1,0:T(8,128)(2,1)}, bf16[256,2560]{1,0:T(8,128)(2,1)S(1)}, u32[]{:S(2)}, u32[]{:S(2)}) collective-permute-start(bf16[256,2560]{1,0:T(8,128)(2,1)} %get-tuple-element.86.refs_4_.rest_1_), channel_id=1, source_target_pairs={{0,1},{1,0},{2,3},{3,2},{4,5},{5,4},{6,7},{7,6},{8,9},{9,8},{10,11... | collective-permute-start | bytes 3932168 | tf_op jit(solution)/shard_map/ppermute | solution.py:568
  441.1 31.7 %collective-permute-start.42 = (bf16[2,64,2560]{2,1,0:T(8,128)(2,1)}, bf16[2,64,2560]{2,1,0:T(8,128)(2,1)S(1)}, u32[]{:S(2)}, u32[]{:S(2)}) collective-permute-start(bf16[2,64,2560]{2,1,0:T(8,128)(2,1)} %get-tuple-element.89.rest_2_), channel_id=1, source_target_pairs={{0,2},{2,0},{4,6},{6,4},{1,3},{3,1},{5,7},{7,5},{8,10},{10,8},{12,... | collective-permute-start | bytes 1966088 | tf_op jit(solution)/shard_map/ppermute | solution.py:565
  471.6 22.5 %collective-permute-start.45 = (bf16[128,2560]{1,0:T(8,128)(2,1)}, bf16[128,2560]{1,0:T(8,128)(2,1)S(1)}, u32[]{:S(2)}, u32[]{:S(2)}) collective-permute-start(bf16[128,2560]{1,0:T(8,128)(2,1)} %get-tuple-element.96.rest_3_), channel_id=1, source_target_pairs={{0,1},{1,0},{2,3},{3,2},{4,5},{5,4},{6,7},{7,6},{8,9},{9,8},{10,11... | collective-permute-start | bytes 1966088 | tf_op jit(solution)/shard_map/ppermute | solution.py:568
  472.1 22.0 %collective-permute-start.46 = (bf16[128,2560]{1,0:T(8,128)(2,1)}, bf16[128,2560]{1,0:T(8,128)(2,1)S(1)}, u32[]{:S(2)}, u32[]{:S(2)}) collective-permute-start(bf16[128,2560]{1,0:T(8,128)(2,1)} %get-tuple-element.97.rest_4_), channel_id=1, source_target_pairs={{0,16},{8,24},{16,0},{24,8},{1,17},{9,25},{17,1},{25,9},{2,18},{10... | collective-permute-start | bytes 1966088 | tf_op jit(solution)/shard_map/ppermute | solution.py:559
  507.1 22.0 %collective-permute-start.50 = (bf16[2,64,2560]{2,1,0:T(8,128)(2,1)S(1)}, bf16[2,64,2560]{2,1,0:T(8,128)(2,1)S(1)}, u32[]{:S(2)}, u32[]{:S(2)}) collective-permute-start(bf16[2,64,2560]{2,1,0:T(8,128)(2,1)S(1)} %copy-done.28), channel_id=1, source_target_pairs={{0,2},{2,0},{4,6},{6,4},{1,3},{3,1},{5,7},{7,5},{8,10},{10,8},{12,... | collective-permute-start | bytes 1966088 | tf_op jit(solution)/shard_map/ppermute | solution.py:565
  515.0 25.8 %collective-permute-start.49 = (bf16[256,1536]{1,0:T(8,128)(2,1)S(1)}, bf16[256,1536]{1,0:T(8,128)(2,1)S(1)}, u32[]{:S(2)}, u32[]{:S(2)}) collective-permute-start(bf16[256,1536]{1,0:T(8,128)(2,1)S(1)} %slice.402.rest_2_), channel_id=1, source_target_pairs={{0,16},{8,24},{16,0},{24,8},{1,17},{9,25},{17,1},{25,9},{2,18},{10... | collective-permute-start | bytes 2359304 | tf_op jit(solution)/shard_map/ppermute | solution.py:559
  538.1 26.2 %collective-permute-start.54 = (f32[32,512]{1,0:T(8,128)}, f32[32,512]{1,0:T(8,128)S(1)}, u32[]{:S(2)}, u32[]{:S(2)}) collective-permute-start(f32[32,512]{1,0:T(8,128)} %get-tuple-element.141), channel_id=1, source_target_pairs={{0,1},{1,0},{2,3},{3,2},{4,5},{5,4},{6,7},{7,6},{8,9},{9,8},{10,11... | collective-permute-start | bytes 196616 | tf_op jit(solution)/shard_map/ppermute | solution.py:568
  539.7 22.7 %collective-permute-start.53 = (bf16[1,64,2560]{2,1,0:T(8,128)(2,1)}, bf16[1,64,2560]{2,1,0:T(8,128)(2,1)}, u32[]{:S(2)}, u32[]{:S(2)}) collective-permute-start(bf16[1,64,2560]{2,1,0:T(8,128)(2,1)} %get-tuple-element.107.refs_1_.rest_4_), channel_id=1, source_target_pairs={{0,4},{2,6},{4,0},{6,2},{1,5},{3,7},{5,1},{7,3},{8,12},{10,14},{12... | collective-permute-start | bytes 983048 | tf_op jit(solution)/shard_map/ppermute | solution.py:565
  544.3 20.7 %collective-permute-start.52 = (bf16[256,1536]{1,0:T(8,128)(2,1)}, bf16[256,1536]{1,0:T(8,128)(2,1)}, u32[]{:S(2)}, u32[]{:S(2)}) collective-permute-start(bf16[256,1536]{1,0:T(8,128)(2,1)} %add_convert_fusion.3.refs_1_.rest_2_), channel_id=1, source_target_pairs={{0,1},{1,0},{2,3},{3,2},{4,5},{5,4},{6,7},{7,6},{8,9},{9,8},{10,11... | collective-permute-start | bytes 2359304 | tf_op jit(solution)/shard_map/ppermute | solution.py:568
  583.6 37.2 %collective-permute-start.57 = (bf16[640,1024]{1,0:T(8,128)(2,1)}, bf16[640,1024]{1,0:T(8,128)(2,1)}, u32[]{:S(2)}, u32[]{:S(2)}) collective-permute-start(bf16[640,1024]{1,0:T(8,128)(2,1)} %shard_map.360.refs_1_), channel_id=1, source_target_pairs={{0,1},{1,0},{2,3},{3,2},{4,5},{5,4},{6,7},{7,6},{8,9},{9,8},{10,11... | collective-permute-start | bytes 3932168 | tf_op jit(solution)/shard_map/ppermute | solution.py:568
  (165 other events, 1230.4 us)

commit v5 on v4

--- a/solution.py
+++ b/solution.py
@@ -1076,8 +1076,7 @@
             vec = vec + px(vec, 1 << bit)
         vec = tie(vec, to_other)
         vec = vec + py(vec)
-        for bit in range(z_bits):
-            vec = vec + pz(vec, 1 << bit)
+        vec = vec + sum(pz(vec, k) for k in range(1, n_pa))
         place = (p0 * n_pa + z0) * n_ta + t0
         w32 = width // (blocks * n_ta)
         ff_rows = n_ta * ff_half // width

time: 650 us -> 669 us (1.029)
  waiting for transfers between devices: 107 us -> 118 us
    ppermute x20, waiting for transfers between devices: 31.7 us -> 49.3 us  [py(): return lax.ppermute(v, 'ta', [(i, i ^ 1) for i in range(n_ta)])]
    ppermute x21 -> x22, waiting for transfers between devices: 48.1 us -> 41.8 us  [pz(): return lax.ppermute(v, 'pa', [(i, i ^ k) for i in range(n_pa)])]
    ppermute x21 -> x22, starting transfers between devices: 29.2 us -> 32.5 us  [pz(): return lax.ppermute(v, 'pa', [(i, i ^ k) for i in range(n_pa)])]
    unnamed x267 -> x277, local copies, waits for them, and re-layouts: 36.2 us -> 39.4 us
  transfers between devices with their start and end apart: 66 -> 67, of which waited for: 23 -> 23; matrix products, arithmetic and copies ran while one was open for 12% -> 12% of each run, Pallas kernels for 41% -> 40%
where the time goes in v5:
time: 669 us; the launch traced here: 658 us
  Pallas kernels  304 us (45%)
  waiting for transfers between devices  118 us (18%)
  starting transfers between devices  74.6 us (11%)
  local copies, waits for them, and re-layouts  60.2 us (9%)
  other arithmetic  49.7 us (7%)
  matrix products  48.8 us (7%)
    pallas_call x6, Pallas kernels, mm_out(): pl.pallas_call(functools.partial(mm_out_kernel, chunk_of(m), half, len(ex...  57.8 us
    pallas_call x5, Pallas kernels, mm_in(): pl.pallas_call(functools.partial(mm_in_kernel, chunk_of(m), epilogue, sta...  55.8 us
    pallas_call x4, Pallas kernels, attend_back(): pl.pallas_call(functools.partial(attend_back_kernel, slots, tile_k, scale...  50.8 us
    ppermute x20, waiting for transfers between devices, py(): return lax.ppermute(v, 'ta', [(i, i ^ 1) for i in range(n_ta)])  49.3 us
    dot_general x11, matrix products, tn(): lax.dot_general(a, b, (((0,), (0,)), ((), ())), preferred_element_type=F32)  43.1 us
    ppermute x22, waiting for transfers between devices, pz(): return lax.ppermute(v, 'pa', [(i, i ^ k) for i in range(n_pa)])  41.8 us
    pallas_call x16, Pallas kernels, assemble(): pl.pallas_call(functools.partial(assemble_kernel, len(arrays), len(deps),...  40.8 us
    unnamed x277, local copies, waits for them, and re-layouts  39.4 us
  transfers between devices with their start and end apart: 67, of which 23 were waited for; matrix products, arithmetic and copies ran while one was open for 12% of the time, Pallas kernels for 40%

profile of v5, /device:TPU:0, one launch (start us, length us, event | category | flops | bytes accessed | tf_op | source)
XLA Modules:
  0.0 658.4 jit_solution(12667259915888806175)
XLA Ops:
  47.2 13.0 %collective-permute-done.7.refs_4_.refs_1_ = bf16[1,64,2560]{2,1,0:T(8,128)(2,1)S(1)} collective-permute-done((bf16[1,64,2560]{2,1,0:T(8,128)(2,1)}, bf16[1,64,2560]{2,1,0:T(8,128)(2,1)S(1)}, u32[]{:S(2)}, u32[]{:S(2)}) %collective-permute-start.7) | collective-permute-done | bytes 327712 | tf_op jit(solution)/shard_map/ppermute | solution.py:565
  74.5 14.6 %shard_map.314.refs_2_.q_ref.k_ref.v_ref = bf16[1344,3072]{1,0:T(8,128)(2,1)} custom-call(bf16[1344,1024]{1,0:T(8,128)(2,1)} %shard_map.306.refs_2_.a_ref.rest_0_.refs_0_, bf16[1024,1536]{1,0:T(8,128)(2,1)} %bitcast.179, bf16[1024,1536]{1,0:T(8,128)(2,1)} %copy-done.11, f32[8,3072]{1,0:T(8,128)} %maximum_maximum_fusion.1.rest_0_, bf16[2,64,2560]{2,1,0:T(8,128)(2,1)} %bitcast.203), custom_call_target="tpu_custom_call" | custom-call | flops 8455716864 | bytes 17301504 | tf_op jit(solution)/shard_map/pallas_call | solution.py:416
  97.2 9.5 %shard_map.317 = (bf16[704,1024]{1,0:T(8,128)(2,1)}, bf16[704,1024]{1,0:T(8,128)(2,1)}) custom-call(bf16[1344,3072]{1,0:T(8,128)(2,1)} %shard_map.314.refs_2_.q_ref.k_ref.v_ref, bf16[1344,3072]{1,0:T(8,128)(2,1)} %shard_map.314.refs_2_.q_ref.k_ref.v_ref, bf16[1344,3072]{1,0:T(8,128)(2,1)} %shard_map.314.refs_2_.q_ref.k_ref.v_ref, ...), custom_call_target="tpu_custom_call" | custom-call | flops 3875536896 | bytes 2457600 | tf_op jit(solution)/shard_map/pallas_call | solution.py:135
  121.0 9.5 %shard_map.321 = (bf16[704,1024]{1,0:T(8,128)(2,1)}, bf16[704,1024]{1,0:T(8,128)(2,1)}) custom-call(bf16[1344,3072]{1,0:T(8,128)(2,1)} %shard_map.314.refs_2_.q_ref.k_ref.v_ref, bf16[1344,3072]{1,0:T(8,128)(2,1)} %shard_map.314.refs_2_.q_ref.k_ref.v_ref, ...), custom_call_target="tpu_custom_call", output_to_operand_aliasing={{0}: (5, {}), {1}: (6, {})} | custom-call | flops 3875536896 | bytes 2457600 | tf_op jit(solution)/shard_map/pallas_call | solution.py:135
  130.5 9.7 %shard_map.322 = (bf16[704,1024]{1,0:T(8,128)(2,1)}, bf16[704,1024]{1,0:T(8,128)(2,1)}) custom-call(bf16[1344,3072]{1,0:T(8,128)(2,1)} %shard_map.314.refs_2_.q_ref.k_ref.v_ref, bf16[1344,3072]{1,0:T(8,128)(2,1)} %shard_map.314.refs_2_.q_ref.k_ref.v_ref, ...), custom_call_target="tpu_custom_call", output_to_operand_aliasing={{0}: (5, {}), {1}: (6, {})} | custom-call | flops 3875536896 | bytes 2457600 | tf_op jit(solution)/shard_map/pallas_call | solution.py:135
  143.4 9.5 %shard_map.324 = (bf16[704,1024]{1,0:T(8,128)(2,1)}, bf16[704,1024]{1,0:T(8,128)(2,1)}) custom-call(bf16[1344,3072]{1,0:T(8,128)(2,1)} %shard_map.314.refs_2_.q_ref.k_ref.v_ref, bf16[1344,3072]{1,0:T(8,128)(2,1)} %shard_map.314.refs_2_.q_ref.k_ref.v_ref, ...), custom_call_target="tpu_custom_call", output_to_operand_aliasing={{0}: (5, {}), {1}: (6, {})} | custom-call | flops 3875536896 | bytes 2457600 | tf_op jit(solution)/shard_map/pallas_call | solution.py:135
  168.3 9.8 %collective-permute-done.20 = f32[2048]{0:T(1024)S(1)} collective-permute-done((f32[2048]{0:T(1024)S(1)}, f32[2048]{0:T(1024)S(1)}, u32[]{:S(2)}, u32[]{:S(2)}) %collective-permute-start.20) | collective-permute-done | bytes 8224 | tf_op jit(solution)/shard_map/ppermute | solution.py:568
  186.4 6.0 shard_map.329
  198.1 20.2 %shard_map.330 = (bf16[704,4096]{1,0:T(8,128)(2,1)}, bf16[704,4096]{1,0:T(8,128)(2,1)}) custom-call(bf16[704,1024]{1,0:T(8,128)(2,1)} %get-tuple-element.134.a_ref.la_ref, bf16[1024,2560]{1,0:T(8,128)(2,1)} %bitcast.165, bf16[1024,2560]{1,0:T(8,128)(2,1)} %collective-permute-done.17.r0_ref.r1_ref.r_ref, f32[8,4096]{1,0:T(8,128)} %concatenate.104.rest_0_), custom_call_target="tpu_custom_call" | custom-call | flops 5905580032 | bytes 21364736 | tf_op jit(solution)/shard_map/pallas_call | solution.py:416
  232.3 12.8 %shard_map.332 = f32[704,1024]{1,0:T(8,128)} custom-call(bf16[704,4096]{1,0:T(8,128)(2,1)} %get-tuple-element.75.refs_4_.a0_ref.a1_ref.ra_ref, bf16[704,4096]{1,0:T(8,128)(2,1)} %get-tuple-element.75.refs_4_.a0_ref.a1_ref.ra_ref, bf16[1024,2560]{1,0:T(8,128)(2,1)} %bitcast.170, bf16[1024,2560]{1,0:T(8,128)(2,1)} %bitcast.171, ...), custom_call_target="tpu_custom_call" | custom-call | flops 5905580032 | bytes 17039360 | tf_op jit(solution)/shard_map/pallas_call | solution.py:467
  266.8 6.9 %collective-permute-done.25 = bf16[64,1024]{1,0:T(8,128)(2,1)S(1)} collective-permute-done((bf16[64,1024]{1,0:T(8,128)(2,1)S(1)}, bf16[64,1024]{1,0:T(8,128)(2,1)S(1)}, u32[]{:S(2)}, u32[]{:S(2)}) %collective-permute-start.25) | collective-permute-done | bytes 131104 | tf_op jit(solution)/shard_map/ppermute | solution.py:565
  278.5 7.1 %collective-permute-done.28 = bf16[192,1024]{1,0:T(8,128)(2,1)S(1)} collective-permute-done((bf16[192,1024]{1,0:T(8,128)(2,1)}, bf16[192,1024]{1,0:T(8,128)(2,1)S(1)}, u32[]{:S(2)}, u32[]{:S(2)}) %collective-permute-start.28) | collective-permute-done | bytes 393248 | tf_op jit(solution)/shard_map/ppermute | solution.py:568
  298.7 8.3 %collective-permute-done.30 = bf16[256,1024]{1,0:T(8,128)(2,1)S(1)} collective-permute-done((bf16[256,1024]{1,0:T(8,128)(2,1)S(1)}, bf16[256,1024]{1,0:T(8,128)(2,1)S(1)}, u32[]{:S(2)}, u32[]{:S(2)}) %collective-permute-start.30) | collective-permute-done | bytes 524320 | tf_op jit(solution)/shard_map/ppermute | solution.py:568
  322.0 6.2 shard_map.335
  336.4 5.1 convolution_convert_fusion.1
  344.1 11.8 %shard_map.336 = (bf16[704,4096]{1,0:T(8,128)(2,1)}, f32[8,4096]{1,0:T(8,128)}) custom-call(bf16[704,1024]{1,0:T(8,128)(2,1)} %copy-done.25, bf16[1024,2560]{1,0:T(8,128)(2,1)} %bitcast.175, bf16[1024,2560]{1,0:T(8,128)(2,1)} %collective-permute-done.23.r0_ref.r1_ref.r_ref, bf16[704,4096]{1,0:T(8,128)(2,1)} %get-tuple-element.76.rest_0_), custom_call_target="tpu_custom_call" | custom-call | flops 5905580032 | bytes 15663104 | tf_op jit(solution)/shard_map/pallas_call | solution.py:416
  355.8 7.7 %convolution_convert_fusion = bf16[512,4096]{1,0:T(8,128)(2,1)} fusion(bf16[704,4096]{1,0:T(8,128)(2,1)} %get-tuple-element.77.rest_0_.a0_ref.a1_ref.ra_ref, bf16[704,1024]{1,0:T(8,128)(2,1)S(1)} %copy-done.24), kind=kOutput, calls=%fused_computation.3 | convolution fusion | flops 2954887168 | bytes 10682368 | tf_op jit(solution)/shard_map/dot_general | solution.py:32
  364.6 13.2 %shard_map.337 = (bf16[128,5120]{1,0:T(8,128)(2,1)}, bf16[128,5120]{1,0:T(8,128)(2,1)}, bf16[256,2560]{1,0:T(8,128)(2,1)}, bf16[256,2560]{1,0:T(8,128)(2,1)}) custom-call(bf16[704,1024]{1,0:T(8,128)(2,1)} %copy-done.25, bf16[704,1024]{1,0:T(8,128)(2,1)} %add_convert_fusion.a_ref.lb_ref, bf16[704,4096]{1,0:T(8,128)(2,1)} %get-tuple-element.75.refs_4_.a0_ref.a1_ref.ra_ref, ...), custom_call_target="tpu_custom_call" | custom-call | flops 3690987520 | bytes 17694720 | tf_op jit(solution)/shard_map/pallas_call | solution.py:366
  379.8 12.7 %shard_map.338.refs_4_ = f32[704,1024]{1,0:T(8,128)} custom-call(bf16[704,4096]{1,0:T(8,128)(2,1)} %get-tuple-element.77.rest_0_.a0_ref.a1_ref.ra_ref, bf16[704,4096]{1,0:T(8,128)(2,1)} %get-tuple-element.77.rest_0_.a0_ref.a1_ref.ra_ref, bf16[1024,2560]{1,0:T(8,128)(2,1)} %bitcast.166, bf16[1024,2560]{1,0:T(8,128)(2,1)} %bitcast.167, ...), custom_call_target="tpu_custom_call" | custom-call | flops 5905580032 | bytes 17039360 | tf_op jit(solution)/shard_map/pallas_call | solution.py:467
  401.5 7.7 %collective-permute-done.36.refs_1_ = bf16[128,5120]{1,0:T(8,128)(2,1)S(1)} collective-permute-done((bf16[128,5120]{1,0:T(8,128)(2,1)}, bf16[128,5120]{1,0:T(8,128)(2,1)S(1)}, u32[]{:S(2)}, u32[]{:S(2)}) %collective-permute-start.36) | collective-permute-done | bytes 1310752 | tf_op jit(solution)/shard_map/ppermute | solution.py:559
  422.2 13.2 %shard_map.341 = (bf16[128,5120]{1,0:T(8,128)(2,1)}, bf16[128,5120]{1,0:T(8,128)(2,1)}, bf16[256,2560]{1,0:T(8,128)(2,1)}, bf16[256,2560]{1,0:T(8,128)(2,1)}) custom-call(bf16[704,1024]{1,0:T(8,128)(2,1)} %get-tuple-element.134.a_ref.la_ref, bf16[704,1024]{1,0:T(8,128)(2,1)} %copy-done.18, bf16[704,4096]{1,0:T(8,128)(2,1)} %get-tuple-element.77.rest_0_.a0_ref.a1_ref.ra_ref, ...), custom_call_target="tpu_custom_call" | custom-call | flops 3690987520 | bytes 17694720 | tf_op jit(solution)/shard_map/pallas_call | solution.py:366
  441.2 12.5 %shard_map.343 = (bf16[1344,3072]{1,0:T(8,128)(2,1)}, f32[8,1024]{1,0:T(8,128)}) custom-call(bf16[1344,3072]{1,0:T(8,128)(2,1)} %shard_map.314.refs_2_.q_ref.k_ref.v_ref, bf16[1344,3072]{1,0:T(8,128)(2,1)} %shard_map.314.refs_2_.q_ref.k_ref.v_ref, bf16[1344,3072]{1,0:T(8,128)(2,1)} %shard_map.314.refs_2_.q_ref.k_ref.v_ref, ...), custom_call_target="tpu_custom_call" | custom-call | flops 9688842240 | bytes 4915200 | tf_op jit(solution)/shard_map/pallas_call | solution.py:228
  453.7 11.6 %collective-permute-done.43.refs_1_ = bf16[128,5120]{1,0:T(8,128)(2,1)S(1)} collective-permute-done((bf16[128,5120]{1,0:T(8,128)(2,1)}, bf16[128,5120]{1,0:T(8,128)(2,1)S(1)}, u32[]{:S(2)}, u32[]{:S(2)}) %collective-permute-start.43) | collective-permute-done | bytes 1310752 | tf_op jit(solution)/shard_map/ppermute | solution.py:559
  476.9 12.7 %shard_map.346 = (bf16[1344,3072]{1,0:T(8,128)(2,1)}, f32[8,1024]{1,0:T(8,128)}) custom-call(bf16[1344,3072]{1,0:T(8,128)(2,1)} %shard_map.314.refs_2_.q_ref.k_ref.v_ref, bf16[1344,3072]{1,0:T(8,128)(2,1)} %shard_map.314.refs_2_.q_ref.k_ref.v_ref, ...), custom_call_target="tpu_custom_call", output_to_operand_aliasing={{0}: (7, {}), {1}: (8, {})} | custom-call | flops 9688842240 | bytes 4915200 | tf_op jit(solution)/shard_map/pallas_call | solution.py:228
  498.2 6.5 fusion.7
  508.5 5.3 fusion.10
  516.2 13.0 %shard_map.350 = (bf16[1344,3072]{1,0:T(8,128)(2,1)}, f32[8,1024]{1,0:T(8,128)}) custom-call(bf16[1344,3072]{1,0:T(8,128)(2,1)} %shard_map.314.refs_2_.q_ref.k_ref.v_ref, bf16[1344,3072]{1,0:T(8,128)(2,1)} %shard_map.314.refs_2_.q_ref.k_ref.v_ref, ...), custom_call_target="tpu_custom_call", output_to_operand_aliasing={{0}: (7, {}), {1}: (8, {})} | custom-call | flops 9688842240 | bytes 4915200 | tf_op jit(solution)/shard_map/pallas_call | solution.py:228
  549.6 12.6 %shard_map.355 = (bf16[1344,3072]{1,0:T(8,128)(2,1)}, f32[8,1024]{1,0:T(8,128)}) custom-call(bf16[1344,3072]{1,0:T(8,128)(2,1)} %shard_map.314.refs_2_.q_ref.k_ref.v_ref, bf16[1344,3072]{1,0:T(8,128)(2,1)} %shard_map.314.refs_2_.q_ref.k_ref.v_ref, ...), custom_call_target="tpu_custom_call", output_to_operand_aliasing={{0}: (7, {}), {1}: (8, {})} | custom-call | flops 9688842240 | bytes 4915200 | tf_op jit(solution)/shard_map/pallas_call | solution.py:228
  573.5 9.3 %shard_map.360.refs_1_ = bf16[640,1024]{1,0:T(8,128)(2,1)} custom-call(bf16[1344,3072]{1,0:T(8,128)(2,1)} %get-tuple-element.108.a0_ref.a1_ref.refs_0_, bf16[1344,3072]{1,0:T(8,128)(2,1)} %get-tuple-element.108.a0_ref.a1_ref.refs_0_, bf16[1024,1536]{1,0:T(8,128)(2,1)} %bitcast.180, bf16[1024,1536]{1,0:T(8,128)(2,1)} %bitcast.181, ...), custom_call_target="tpu_custom_call" | custom-call | flops 4026531840 | bytes 12845056 | tf_op jit(solution)/shard_map/pallas_call | solution.py:467
  592.9 10.7 %shard_map.363.refs_1_.x_ref = f32[704,1024]{1,0:T(8,128)} custom-call(bf16[1344,3072]{1,0:T(8,128)(2,1)} %shard_map.361.a0_ref.a1_ref, bf16[1344,3072]{1,0:T(8,128)(2,1)} %shard_map.361.a0_ref.a1_ref, bf16[1024,1536]{1,0:T(8,128)(2,1)} %bitcast.182, bf16[1024,1536]{1,0:T(8,128)(2,1)} %bitcast.183, bf16[1024,1536]{1,0:T(8,128)(2,1)} %copy-done.11, ...), custom_call_target="tpu_custom_call" | custom-call | flops 4429185024 | bytes 13500416 | tf_op jit(solution)/shard_map/pallas_call | solution.py:467
  612.1 5.5 collective-permute-done.59
  622.5 16.8 %collective-permute-done.57.refs_0_ = bf16[640,1024]{1,0:T(8,128)(2,1)S(1)} collective-permute-done((bf16[640,1024]{1,0:T(8,128)(2,1)S(1)}, bf16[640,1024]{1,0:T(8,128)(2,1)S(1)}, u32[]{:S(2)}, u32[]{:S(2)}) %collective-permute-start.57) | collective-permute-done | bytes 1310752 | tf_op jit(solution)/shard_map/ppermute | solution.py:568
  (608 shorter events, 324.9 us)
Async XLA Ops:
  15.9 19.1 %collective-permute-start.1 = (bf16[2,64,1536]{2,1,0:T(8,128)(2,1)}, bf16[2,64,1536]{2,1,0:T(8,128)(2,1)S(1)}, u32[]{:S(2)}, u32[]{:S(2)}) collective-permute-start(bf16[2,64,1536]{2,1,0:T(8,128)(2,1)} %shard_map.307.refs_0_.refs_1_), channel_id=1, source_target_pairs={{0,16},{8,24},{16,0},{24,8},{1,17},{9,25},{17,1},{25,9},{2,18},{10... | collective-permute-start | bytes 1179656 | tf_op jit(solution)/shard_map/ppermute | solution.py:559
  37.8 22.3 %collective-permute-start.2 = (bf16[2,2,64,1536]{3,2,1,0:T(8,128)(2,1)}, bf16[2,2,64,1536]{3,2,1,0:T(8,128)(2,1)S(1)}, u32[]{:S(2)}, u32[]{:S(2)}) collective-permute-start(bf16[2,2,64,1536]{3,2,1,0:T(8,128)(2,1)} %shard_map.308.refs_0_), channel_id=1, source_target_pairs={{0,1},{1,0},{2,3},{3,2},{4,5},{5,4},{6,7},{7,6},{8,9},{9,8},{10,11... | collective-permute-start | bytes 2359304 | tf_op jit(solution)/shard_map/ppermute | solution.py:568
  93.9 19.2 %collective-permute-start.12 = (bf16[2,64,2560]{2,1,0:T(8,128)(2,1)}, bf16[2,64,2560]{2,1,0:T(8,128)(2,1)S(1)}, u32[]{:S(2)}, u32[]{:S(2)}) collective-permute-start(bf16[2,64,2560]{2,1,0:T(8,128)(2,1)} %bitcast.210), channel_id=1, source_target_pairs={{0,1},{1,0},{2,3},{3,2},{4,5},{5,4},{6,7},{7,6},{8,9},{9,8},{10,11... | collective-permute-start | bytes 1966088 | tf_op jit(solution)/shard_map/ppermute | solution.py:568
  96.1 21.7 %collective-permute-start.13 = (bf16[1,64,2560]{2,1,0:T(8,128)(2,1)}, bf16[1,64,2560]{2,1,0:T(8,128)(2,1)S(1)}, u32[]{:S(2)}, u32[]{:S(2)}) collective-permute-start(bf16[1,64,2560]{2,1,0:T(8,128)(2,1)} %shard_map.316.rest_1_.refs_0_), channel_id=1, source_target_pairs={{0,4},{2,6},{4,0},{6,2},{1,5},{3,7},{5,1},{7,3},{8,12},{10,14},{12... | collective-permute-start | bytes 983048 | tf_op jit(solution)/shard_map/ppermute | solution.py:565
  111.4 41.5 %collective-permute-start.15 = (bf16[2,2,64,2560]{3,2,1,0:T(8,128)(2,1)}, bf16[2,2,64,2560]{3,2,1,0:T(8,128)(2,1)S(1)}, u32[]{:S(2)}, u32[]{:S(2)}) collective-permute-start(bf16[2,2,64,2560]{3,2,1,0:T(8,128)(2,1)} %shard_map.318.rest_2_.refs_0_), channel_id=1, source_target_pairs={{0,1},{1,0},{2,3},{3,2},{4,5},{5,4},{6,7},{7,6},{8,9},{9,8},{10,11... | collective-permute-start | bytes 3932168 | tf_op jit(solution)/shard_map/ppermute | solution.py:568
  116.2 36.7 %collective-permute-start.16 = (bf16[2,2,64,2560]{3,2,1,0:T(8,128)(2,1)}, bf16[2,2,64,2560]{3,2,1,0:T(8,128)(2,1)S(1)}, u32[]{:S(2)}, u32[]{:S(2)}) collective-permute-start(bf16[2,2,64,2560]{3,2,1,0:T(8,128)(2,1)} %shard_map.319.rest_3_.refs_2_), channel_id=1, source_target_pairs={{0,16},{8,24},{16,0},{24,8},{1,17},{9,25},{17,1},{25,9},{2,18},{10... | collective-permute-start | bytes 3932168 | tf_op jit(solution)/shard_map/ppermute | solution.py:559
  120.5 19.7 %collective-permute-start.14 = (bf16[2,64,2560]{2,1,0:T(8,128)(2,1)}, bf16[2,64,2560]{2,1,0:T(8,128)(2,1)S(1)}, u32[]{:S(2)}, u32[]{:S(2)}) collective-permute-start(bf16[2,64,2560]{2,1,0:T(8,128)(2,1)} %bitcast.197), channel_id=1, source_target_pairs={{0,2},{2,0},{4,6},{6,4},{1,3},{3,1},{5,7},{7,5},{8,10},{10,8},{12,... | collective-permute-start | bytes 1966088 | tf_op jit(solution)/shard_map/ppermute | solution.py:565
  159.4 26.9 %collective-permute-start.17 = (bf16[1024,2560]{1,0:T(8,128)(2,1)}, bf16[1024,2560]{1,0:T(8,128)(2,1)}, u32[]{:S(2)}, u32[]{:S(2)}) collective-permute-start(bf16[1024,2560]{1,0:T(8,128)(2,1)} %bitcast.160), channel_id=1, source_target_pairs={{0,8},{8,0},{16,24},{24,16},{1,9},{9,1},{17,25},{25,17},{2,10},{10... | collective-permute-start | bytes 15728648 | tf_op jit(solution)/shard_map/ppermute | solution.py:562
  159.5 19.2 %collective-permute-start.18 = (bf16[2,64,2560]{2,1,0:T(8,128)(2,1)S(1)}, bf16[2,64,2560]{2,1,0:T(8,128)(2,1)S(1)}, u32[]{:S(2)}, u32[]{:S(2)}) collective-permute-start(bf16[2,64,2560]{2,1,0:T(8,128)(2,1)S(1)} %bitcast.207), channel_id=1, source_target_pairs={{0,16},{8,24},{16,0},{24,8},{1,17},{9,25},{17,1},{25,9},{2,18},{10... | collective-permute-start | bytes 1966088 | tf_op jit(solution)/shard_map/ppermute | solution.py:559
  161.1 21.5 %collective-permute-start.19 = (bf16[2,64,2560]{2,1,0:T(8,128)(2,1)S(1)}, bf16[2,64,2560]{2,1,0:T(8,128)(2,1)S(1)}, u32[]{:S(2)}, u32[]{:S(2)}) collective-permute-start(bf16[2,64,2560]{2,1,0:T(8,128)(2,1)S(1)} %bitcast.213), channel_id=1, source_target_pairs={{0,1},{1,0},{2,3},{3,2},{4,5},{5,4},{6,7},{7,6},{8,9},{9,8},{10,11... | collective-permute-start | bytes 1966088 | tf_op jit(solution)/shard_map/ppermute | solution.py:568
  182.0 36.3 %collective-permute-start.21 = (bf16[2,2,64,2560]{3,2,1,0:T(8,128)(2,1)}, bf16[2,2,64,2560]{3,2,1,0:T(8,128)(2,1)}, u32[]{:S(2)}, u32[]{:S(2)}) collective-permute-start(bf16[2,2,64,2560]{3,2,1,0:T(8,128)(2,1)} %shard_map.327.rest_2_.refs_0_), channel_id=1, source_target_pairs={{0,1},{1,0},{2,3},{3,2},{4,5},{5,4},{6,7},{7,6},{8,9},{9,8},{10,11... | collective-permute-start | bytes 3932168 | tf_op jit(solution)/shard_map/ppermute | solution.py:568
  185.8 32.5 %collective-permute-start.22 = (bf16[2,2,64,2560]{3,2,1,0:T(8,128)(2,1)}, bf16[2,2,64,2560]{3,2,1,0:T(8,128)(2,1)}, u32[]{:S(2)}, u32[]{:S(2)}) collective-permute-start(bf16[2,2,64,2560]{3,2,1,0:T(8,128)(2,1)} %shard_map.328.rest_3_.refs_2_), channel_id=1, source_target_pairs={{0,16},{8,24},{16,0},{24,8},{1,17},{9,25},{17,1},{25,9},{2,18},{10... | collective-permute-start | bytes 3932168 | tf_op jit(solution)/shard_map/ppermute | solution.py:559
  341.5 22.1 %collective-permute-start.34 = (bf16[512,4096]{1,0:T(8,128)(2,1)}, bf16[512,4096]{1,0:T(8,128)(2,1)}, u32[]{:S(2)}, u32[]{:S(2)}) collective-permute-start(bf16[512,4096]{1,0:T(8,128)(2,1)} %convolution_convert_fusion.1), channel_id=1, source_target_pairs={{0,8},{8,0},{16,24},{24,16},{1,9},{9,1},{17,25},{25,17},{2,10},{10... | collective-permute-start | bytes 12582920 | tf_op jit(solution)/shard_map/ppermute | solution.py:562
  343.6 20.0 %collective-permute-start.35 = (bf16[512,1024]{1,0:T(8,128)(2,1)}, bf16[512,1024]{1,0:T(8,128)(2,1)S(1)}, u32[]{:S(2)}, u32[]{:S(2)}) collective-permute-start(bf16[512,1024]{1,0:T(8,128)(2,1)} %convolution_convert_fusion.3), channel_id=1, source_target_pairs={{0,8},{8,0},{16,24},{24,16},{1,9},{9,1},{17,25},{25,17},{2,10},{10... | collective-permute-start | bytes 3145736 | tf_op jit(solution)/shard_map/ppermute | solution.py:562
  363.5 57.6 %collective-permute-start.38 = (bf16[512,4096]{1,0:T(8,128)(2,1)}, bf16[512,4096]{1,0:T(8,128)(2,1)}, u32[]{:S(2)}, u32[]{:S(2)}) collective-permute-start(bf16[512,4096]{1,0:T(8,128)(2,1)} %convolution_convert_fusion), channel_id=1, source_target_pairs={{0,8},{8,0},{16,24},{24,16},{1,9},{9,1},{17,25},{25,17},{2,10},{10... | collective-permute-start | bytes 12582920 | tf_op jit(solution)/shard_map/ppermute | solution.py:562
  377.8 31.4 %collective-permute-start.36 = (bf16[128,5120]{1,0:T(8,128)(2,1)}, bf16[128,5120]{1,0:T(8,128)(2,1)S(1)}, u32[]{:S(2)}, u32[]{:S(2)}) collective-permute-start(bf16[128,5120]{1,0:T(8,128)(2,1)} %get-tuple-element.78.rest_1_), channel_id=1, source_target_pairs={{0,16},{8,24},{16,0},{24,8},{1,17},{9,25},{17,1},{25,9},{2,18},{10... | collective-permute-start | bytes 3932168 | tf_op jit(solution)/shard_map/ppermute | solution.py:559
  378.3 31.2 %collective-permute-start.37 = (bf16[256,2560]{1,0:T(8,128)(2,1)}, bf16[256,2560]{1,0:T(8,128)(2,1)}, u32[]{:S(2)}, u32[]{:S(2)}) collective-permute-start(bf16[256,2560]{1,0:T(8,128)(2,1)} %get-tuple-element.79.rest_2_), channel_id=1, source_target_pairs={{0,1},{1,0},{2,3},{3,2},{4,5},{5,4},{6,7},{7,6},{8,9},{9,8},{10,11... | collective-permute-start | bytes 3932168 | tf_op jit(solution)/shard_map/ppermute | solution.py:568
  401.5 19.7 %collective-permute-start.39 = (bf16[512,1024]{1,0:T(8,128)(2,1)S(1)}, bf16[512,1024]{1,0:T(8,128)(2,1)S(1)}, u32[]{:S(2)}, u32[]{:S(2)}) collective-permute-start(bf16[512,1024]{1,0:T(8,128)(2,1)S(1)} %convolution_convert_fusion.2), channel_id=1, source_target_pairs={{0,8},{8,0},{16,24},{24,16},{1,9},{9,1},{17,25},{25,17},{2,10},{10... | collective-permute-start | bytes 3145736 | tf_op jit(solution)/shard_map/ppermute | solution.py:562
  414.5 22.7 %collective-permute-start.40 = (bf16[128,2560]{1,0:T(8,128)(2,1)}, bf16[128,2560]{1,0:T(8,128)(2,1)S(1)}, u32[]{:S(2)}, u32[]{:S(2)}) collective-permute-start(bf16[128,2560]{1,0:T(8,128)(2,1)} %get-tuple-element.82.rest_0_), channel_id=1, source_target_pairs={{0,1},{1,0},{2,3},{3,2},{4,5},{5,4},{6,7},{7,6},{8,9},{9,8},{10,11... | collective-permute-start | bytes 1966088 | tf_op jit(solution)/shard_map/ppermute | solution.py:568
  416.0 21.2 %collective-permute-start.41 = (bf16[128,2560]{1,0:T(8,128)(2,1)}, bf16[128,2560]{1,0:T(8,128)(2,1)S(1)}, u32[]{:S(2)}, u32[]{:S(2)}) collective-permute-start(bf16[128,2560]{1,0:T(8,128)(2,1)} %get-tuple-element.83.rest_1_), channel_id=1, source_target_pairs={{0,16},{8,24},{16,0},{24,8},{1,17},{9,25},{17,1},{25,9},{2,18},{10... | collective-permute-start | bytes 1966088 | tf_op jit(solution)/shard_map/ppermute | solution.py:559
  435.4 29.9 %collective-permute-start.43 = (bf16[128,5120]{1,0:T(8,128)(2,1)}, bf16[128,5120]{1,0:T(8,128)(2,1)S(1)}, u32[]{:S(2)}, u32[]{:S(2)}) collective-permute-start(bf16[128,5120]{1,0:T(8,128)(2,1)} %get-tuple-element.85.rest_0_), channel_id=1, source_target_pairs={{0,16},{8,24},{16,0},{24,8},{1,17},{9,25},{17,1},{25,9},{2,18},{10... | collective-permute-start | bytes 3932168 | tf_op jit(solution)/shard_map/ppermute | solution.py:559
  436.7 29.9 %collective-permute-start.44 = (bf16[256,2560]{1,0:T(8,128)(2,1)}, bf16[256,2560]{1,0:T(8,128)(2,1)S(1)}, u32[]{:S(2)}, u32[]{:S(2)}) collective-permute-start(bf16[256,2560]{1,0:T(8,128)(2,1)} %get-tuple-element.86.refs_4_.rest_1_), channel_id=1, source_target_pairs={{0,1},{1,0},{2,3},{3,2},{4,5},{5,4},{6,7},{7,6},{8,9},{9,8},{10,11... | collective-permute-start | bytes 3932168 | tf_op jit(solution)/shard_map/ppermute | solution.py:568
  441.2 31.7 %collective-permute-start.42 = (bf16[2,64,2560]{2,1,0:T(8,128)(2,1)}, bf16[2,64,2560]{2,1,0:T(8,128)(2,1)S(1)}, u32[]{:S(2)}, u32[]{:S(2)}) collective-permute-start(bf16[2,64,2560]{2,1,0:T(8,128)(2,1)} %get-tuple-element.89.rest_2_), channel_id=1, source_target_pairs={{0,2},{2,0},{4,6},{6,4},{1,3},{3,1},{5,7},{7,5},{8,10},{10,8},{12,... | collective-permute-start | bytes 1966088 | tf_op jit(solution)/shard_map/ppermute | solution.py:565
  471.7 22.5 %collective-permute-start.45 = (bf16[128,2560]{1,0:T(8,128)(2,1)}, bf16[128,2560]{1,0:T(8,128)(2,1)S(1)}, u32[]{:S(2)}, u32[]{:S(2)}) collective-permute-start(bf16[128,2560]{1,0:T(8,128)(2,1)} %get-tuple-element.96.rest_3_), channel_id=1, source_target_pairs={{0,1},{1,0},{2,3},{3,2},{4,5},{5,4},{6,7},{7,6},{8,9},{9,8},{10,11... | collective-permute-start | bytes 1966088 | tf_op jit(solution)/shard_map/ppermute | solution.py:568
  472.2 22.0 %collective-permute-start.46 = (bf16[128,2560]{1,0:T(8,128)(2,1)}, bf16[128,2560]{1,0:T(8,128)(2,1)S(1)}, u32[]{:S(2)}, u32[]{:S(2)}) collective-permute-start(bf16[128,2560]{1,0:T(8,128)(2,1)} %get-tuple-element.97.rest_4_), channel_id=1, source_target_pairs={{0,16},{8,24},{16,0},{24,8},{1,17},{9,25},{17,1},{25,9},{2,18},{10... | collective-permute-start | bytes 1966088 | tf_op jit(solution)/shard_map/ppermute | solution.py:559
  507.1 22.1 %collective-permute-start.50 = (bf16[2,64,2560]{2,1,0:T(8,128)(2,1)S(1)}, bf16[2,64,2560]{2,1,0:T(8,128)(2,1)S(1)}, u32[]{:S(2)}, u32[]{:S(2)}) collective-permute-start(bf16[2,64,2560]{2,1,0:T(8,128)(2,1)S(1)} %copy-done.30), channel_id=1, source_target_pairs={{0,2},{2,0},{4,6},{6,4},{1,3},{3,1},{5,7},{7,5},{8,10},{10,8},{12,... | collective-permute-start | bytes 1966088 | tf_op jit(solution)/shard_map/ppermute | solution.py:565
  515.0 25.7 %collective-permute-start.49 = (bf16[256,1536]{1,0:T(8,128)(2,1)S(1)}, bf16[256,1536]{1,0:T(8,128)(2,1)S(1)}, u32[]{:S(2)}, u32[]{:S(2)}) collective-permute-start(bf16[256,1536]{1,0:T(8,128)(2,1)S(1)} %slice.402.rest_2_), channel_id=1, source_target_pairs={{0,16},{8,24},{16,0},{24,8},{1,17},{9,25},{17,1},{25,9},{2,18},{10... | collective-permute-start | bytes 2359304 | tf_op jit(solution)/shard_map/ppermute | solution.py:559
  538.2 26.0 %collective-permute-start.54 = (f32[32,512]{1,0:T(8,128)}, f32[32,512]{1,0:T(8,128)S(1)}, u32[]{:S(2)}, u32[]{:S(2)}) collective-permute-start(f32[32,512]{1,0:T(8,128)} %get-tuple-element.141), channel_id=1, source_target_pairs={{0,1},{1,0},{2,3},{3,2},{4,5},{5,4},{6,7},{7,6},{8,9},{9,8},{10,11... | collective-permute-start | bytes 196616 | tf_op jit(solution)/shard_map/ppermute | solution.py:568
  539.7 22.5 %collective-permute-start.53 = (bf16[1,64,2560]{2,1,0:T(8,128)(2,1)}, bf16[1,64,2560]{2,1,0:T(8,128)(2,1)}, u32[]{:S(2)}, u32[]{:S(2)}) collective-permute-start(bf16[1,64,2560]{2,1,0:T(8,128)(2,1)} %get-tuple-element.107.refs_1_.rest_4_), channel_id=1, source_target_pairs={{0,4},{2,6},{4,0},{6,2},{1,5},{3,7},{5,1},{7,3},{8,12},{10,14},{12... | collective-permute-start | bytes 983048 | tf_op jit(solution)/shard_map/ppermute | solution.py:565
  544.2 20.6 %collective-permute-start.52 = (bf16[256,1536]{1,0:T(8,128)(2,1)}, bf16[256,1536]{1,0:T(8,128)(2,1)}, u32[]{:S(2)}, u32[]{:S(2)}) collective-permute-start(bf16[256,1536]{1,0:T(8,128)(2,1)} %add_convert_fusion.3.refs_1_.rest_2_), channel_id=1, source_target_pairs={{0,1},{1,0},{2,3},{3,2},{4,5},{5,4},{6,7},{7,6},{8,9},{9,8},{10,11... | collective-permute-start | bytes 2359304 | tf_op jit(solution)/shard_map/ppermute | solution.py:568
  608.6 30.7 %collective-permute-start.57 = (bf16[640,1024]{1,0:T(8,128)(2,1)S(1)}, bf16[640,1024]{1,0:T(8,128)(2,1)S(1)}, u32[]{:S(2)}, u32[]{:S(2)}) collective-permute-start(bf16[640,1024]{1,0:T(8,128)(2,1)S(1)} %copy-done.19), channel_id=1, source_target_pairs={{0,1},{1,0},{2,3},{3,2},{4,5},{5,4},{6,7},{7,6},{8,9},{9,8},{10,11... | collective-permute-start | bytes 3932168 | tf_op jit(solution)/shard_map/ppermute | solution.py:568
  618.4 31.8 %collective-permute-start.60 = (bf16[1,64,1536]{2,1,0:T(8,128)(2,1)S(1)}, bf16[1,64,1536]{2,1,0:T(8,128)(2,1)S(1)}, u32[]{:S(2)}, u32[]{:S(2)}) collective-permute-start(bf16[1,64,1536]{2,1,0:T(8,128)(2,1)S(1)} %get-tuple-element.146.refs_1_), channel_id=1, source_target_pairs={{0,4},{2,6},{4,0},{6,2},{1,5},{3,7},{5,1},{7,3},{8,12},{10,14},{12... | collective-permute-start | bytes 589832 | tf_op jit(solution)/shard_map/ppermute | solution.py:565
  (171 other events, 1330.5 us)
